TPU v7x, 32 devices: a whole 2x2x4 slice. The times are simulated.
32 devices in a mesh: blk: 8 (over y, x, core), head: 4 (over z).
Axes of the slice: x: 2, y: 2, z: 4, core: 2. Of those that a mesh axis runs over, the one named last changes fastest.
Arguments:
- inputs: bfloat16 [2, 4096, 768], P(None, ('blk', 'head')), may hold values from -6 to 6
- cotangent: bfloat16 [2, 4096, 768], P(None, ('blk', 'head')), may hold values from -6 to 6
- random_blocks: int32 [2, 64, 12, 3], replicated, may hold values from 0 to 63, as said below
- global_blocks: int32 [2, 2], replicated, may hold values from 0 to 63, as said below
- query_weight: bfloat16 [768, 768], P(('blk', 'head')), may hold values from -0.21875 to 0.21875
- query_bias: bfloat16 [768], P(('blk', 'head')), may hold values from -3 to 3
- key_weight: bfloat16 [768, 768], P(('blk', 'head')), may hold values from -0.21875 to 0.21875
- value_weight: bfloat16 [768, 768], P(('blk', 'head')), may hold values from -0.21875 to 0.21875
- value_bias: bfloat16 [768], P(('blk', 'head')), may hold values from -3 to 3
- out_weight: bfloat16 [768, 768], P(('blk', 'head')), may hold values from -0.875 to 0.875
- out_bias: bfloat16 [768], P(('blk', 'head')), may hold values from -3 to 3
- attn_gain: bfloat16 [768], P(('blk', 'head')), may hold values from 0.5 to 1.5
- attn_shift: bfloat16 [768], P(('blk', 'head')), may hold values from -3 to 3
- up_weight: bfloat16 [768, 3072], P(('blk', 'head')), may hold values from -0.21875 to 0.21875
- up_bias: bfloat16 [3072], P(('blk', 'head')), may hold values from -3 to 3
- down_weight: bfloat16 [3072, 768], P(('blk', 'head')), may hold values from -0.109375 to 0.109375
- down_bias: bfloat16 [768], P(('blk', 'head')), may hold values from -3 to 3
- ffn_gain: bfloat16 [768], P(('blk', 'head')), may hold values from 0.5 to 1.5
- ffn_shift: bfloat16 [768], P(('blk', 'head')), may hold values from -3 to 3
Outputs:
- layer_out: bfloat16 [2, 4096, 768], P(None, ('blk', 'head'))
- input_grad: bfloat16 [2, 4096, 768], P(None, ('blk', 'head'))
- grad_query_weight: float32 [768, 768], P(('blk', 'head'))
- grad_query_bias: float32 [768], P(('blk', 'head'))
- grad_key_weight: float32 [768, 768], P(('blk', 'head'))
- grad_value_weight: float32 [768, 768], P(('blk', 'head'))
- grad_value_bias: float32 [768], P(('blk', 'head'))
- grad_out_weight: float32 [768, 768], P(('blk', 'head'))
- grad_out_bias: float32 [768], P(('blk', 'head'))
- grad_attn_gain: float32 [768], P(('blk', 'head'))
- grad_attn_shift: float32 [768], P(('blk', 'head'))
- grad_up_weight: float32 [768, 3072], P(('blk', 'head'))
- grad_up_bias: float32 [3072], P(('blk', 'head'))
- grad_down_weight: float32 [3072, 768], P(('blk', 'head'))
- grad_down_bias: float32 [768], P(('blk', 'head'))
- grad_ffn_gain: float32 [768], P(('blk', 'head'))
- grad_ffn_shift: float32 [768], P(('blk', 'head'))
Inputs may be any that keep to these rules, and one draw needn't show every extreme that they name: `random_blocks`: for each micro-batch, each run of 8 query blocks starting at a multiple of 8 and each run of 3 heads starting at a multiple of 3: at most 10 of their 72 entries lie in any one run of 8 key blocks starting at a multiple of 8, and exactly 10 lie in one such run. Entries may name a window or a global block. `global_blocks`: the 2 global blocks of a micro-batch are different; their positions are drawn anew for each micro-batch.
All inputs are finite; a program needn't handle non-finite values.
Results may differ from a plain program's by a relative error of at most 0.014.
Values may be sent and summed in bfloat16 or wider, within the bound.
A program may use at most 256 MiB of HBM per device.

v0:
```python
from functools import partial

import jax
import jax.numpy as jnp
from jax import lax
from jax.experimental import pallas as pl
from jax.experimental.pallas import tpu as pltpu
from jax.sharding import PartitionSpec as P

HEADS = 12
HD = 64
BLOCK = 64
RAND = 3
GLOB = 2


MESH = pl.DeviceIdType.MESH


def places():
    b = lax.axis_index("blk")
    h = lax.axis_index("head")
    core = b % 2
    x = (b // 2) % 2
    y = b // 4
    across_x = b + 2 - 4 * x
    across_y = b + 4 - 8 * y
    partner = b + 1 - 2 * core
    pair = h // 2
    line = (h, h + 1 - 2 * (h % 2), 2 - pair, 3 - 3 * pair)
    return b, h, core, x, y, across_x, across_y, partner, line


def meet(b, h, others, line):
    barrier = pltpu.get_barrier_semaphore()
    for other in others:
        pl.semaphore_signal(barrier, inc=1, device_id=(other, h), device_id_type=MESH)
    for d in range(1, 4):
        pl.semaphore_signal(barrier, inc=1, device_id=(b, line[d]), device_id_type=MESH)
    pl.semaphore_wait(barrier, len(others) + 3)


def remote(src, dst, send_sem, recv_sem, device):
    return pltpu.make_async_remote_copy(
        src_ref=src,
        dst_ref=dst,
        send_sem=send_sem,
        recv_sem=recv_sem,
        device_id=device,
        device_id_type=MESH,
    )


def gather_kernel(kinds, *refs):
    n = len(kinds)
    ins = refs[:n]
    outs = refs[n : 2 * n]
    own_sem, line_send, line_recv, send, recv = refs[2 * n :]
    b, h, core, x, y, across_x, across_y, partner, line = places()
    corner = across_x + 4 - 8 * y
    inner = jnp.logical_or(h == 1, h == 2)
    seen = jnp.where(inner, 2, 3)
    meet(b, h, (across_x, across_y, partner), line)

    def piece(i, place):
        return ins[i].at[place] if kinds[i][0] else ins[i]

    def slot(i, shard, place):
        return outs[i].at[shard * 4 + place] if kinds[i][1] else outs[i].at[place]

    def part(ref, cut):
        axis, start, size = cut
        return ref.at[(slice(None),) * axis + (pl.ds(start, size),)]

    started = []
    started_inner = []

    def go(copy, only_inner=False):
        if only_inner:

            @pl.when(inner)
            def _():
                copy.start()

            started_inner.append(copy)
        else:
            copy.start()
            started.append(copy)

    def along(i, src, landing, sender_at, receiver_at, place, only_inner=False):
        go(
            remote(
                src, landing, line_send.at[i, sender_at], line_recv.at[i, receiver_at], (b, place)
            ),
            only_inner,
        )

    def line_arrived(i, d):
        here = slot(i, b, line[d])
        remote(
            here, here, line_send.at[i, d], line_recv.at[i, d], (b, line[d])
        ).wait_recv()
        if not kinds[i][0]:
            if d == 1:
                along(i, here, here, 3, 3, 3 - h, True)
            else:
                along(i, here, here, d + 2, d, line[1], True)

    def out_of(i, d):
        return piece(i, h) if d == 0 else slot(i, b, line[d])

    def send_plane(i, d):
        for k, other in enumerate((across_x, across_y, partner)):
            go(
                remote(
                    out_of(i, d),
                    slot(i, b, line[d]),
                    send.at[i, d, k],
                    recv.at[i, d, k],
                    (other, h),
                )
            )

    def arrived(i, d, k, shard, cut=None):
        here = slot(i, shard, line[d])
        if cut is not None:
            here = part(here, cut)
        remote(here, here, send.at[i, d, k], recv.at[i, d, k], (partner, h)).wait_recv()
        return here

    def pass_on(i, d):
        first, second = kinds[i][2]
        here = arrived(i, d, 0, across_x)
        if first is not None:
            go(
                remote(
                    part(here, first),
                    part(here, first),
                    send.at[i, d, 6],
                    recv.at[i, d, 6],
                    (across_y, h),
                )
            )
        go(remote(here, here, send.at[i, d, 3], recv.at[i, d, 3], (partner, h)))
        here = arrived(i, d, 1, across_y)
        if second is not None:
            go(
                remote(
                    part(here, second),
                    part(here, second),
                    send.at[i, d, 7],
                    recv.at[i, d, 7],
                    (across_x, h),
                )
            )
        go(remote(here, here, send.at[i, d, 4], recv.at[i, d, 4], (partner, h)))

    def finish_corner(i, d):
        first, second = kinds[i][2]
        if first is not None:
            arrived(i, d, 6, corner, first)
        if second is not None:
            arrived(i, d, 7, corner, second)
        here = slot(i, corner, line[d])
        go(remote(here, here, send.at[i, d, 5], recv.at[i, d, 5], (partner, h)))

    spread = [i for i in range(n) if kinds[i][1]]
    straight = [i for i in range(n) if not kinds[i][1]]
    locals_ = []

    def send_straight(i):
        for d in (2, 3, 1):
            along(i, piece(i, line[d]), slot(i, b, h), d, 1 if d == 1 else seen, line[d])

    for i in spread:
        if kinds[i][0]:
            send_straight(i)
        else:
            along(i, piece(i, h), slot(i, b, h), 2, 2, 3 - h, True)
            along(i, piece(i, h), slot(i, b, h), 1, 1, line[1])
    if not spread:
        for i in straight:
            send_straight(i)
    for i in spread:
        send_plane(i, 0)
    for i in range(n):
        own = pltpu.make_async_copy(piece(i, h), slot(i, b, h), own_sem.at[i])
        own.start()
        locals_.append(own)
    for d in range(1, 4):
        for i in spread:
            line_arrived(i, d)
            send_plane(i, d)
        if d == 2 and spread:
            for i in straight:
                send_straight(i)
        for i in spread:
            pass_on(i, d - 1)
        if d > 1:
            for i in spread:
                finish_corner(i, d - 2)
    for i in spread:
        pass_on(i, 3)
    for d in (2, 3):
        for i in spread:
            finish_corner(i, d)
    for i in straight:
        for d in range(1, 4):
            line_arrived(i, d)
    partner_x = partner + 2 - 4 * x
    partner_y = partner + 4 - 8 * y
    partner_corner = partner_x + 4 - 8 * y
    for i in spread:
        for d in range(4):
            for k, shard in ((2, partner), (3, partner_x), (4, partner_y), (5, partner_corner)):
                arrived(i, d, k, shard)
    for own in locals_:
        own.wait()
    for copy in started:
        copy.wait_send()
    if started_inner:

        @pl.when(inner)
        def _():
            for copy in started_inner:
                copy.wait_send()


def gather_call(arrays, kinds, collective):
    n = len(arrays)
    shapes = []
    for a, (per_place, spread, _) in zip(arrays, kinds):
        chunk = a.shape[1:] if per_place else a.shape
        shapes.append(jax.ShapeDtypeStruct(((32 if spread else 4),) + chunk, a.dtype))
    return pl.pallas_call(
        partial(gather_kernel, kinds),
        out_shape=tuple(shapes),
        in_specs=[pl.BlockSpec(memory_space=pl.ANY)] * n,
        out_specs=tuple([pl.BlockSpec(memory_space=pl.ANY)] * n),
        scratch_shapes=[
            pltpu.SemaphoreType.DMA((n,)),
            pltpu.SemaphoreType.DMA((n, 6)),
            pltpu.SemaphoreType.DMA((n, 4)),
            pltpu.SemaphoreType.DMA((n, 4, 8)),
            pltpu.SemaphoreType.DMA((n, 4, 8)),
        ],
        compiler_params=pltpu.CompilerParams(collective_id=collective, has_side_effects=True),
        name=f"gather{collective}",
    )(*arrays)


def scatter_kernel(kinds, *refs):
    n = len(kinds)
    ins = refs[:n]
    outs = refs[n : 2 * n]
    rest = list(refs[2 * n :])
    bufs = {}
    for i in range(n):
        if kinds[i][1]:
            bufs[i] = rest[:6]
            rest = rest[6:]
            if kinds[i][0]:
                bufs[i] = bufs[i] + [rest[0]]
                rest = rest[1:]
    local_sem, own_sem, line_send, line_recv, core_send, core_recv, send, recv = rest
    b, h, core, x, y, across_x, across_y, partner, line = places()
    seen = jnp.where(jnp.logical_or(h == 1, h == 2), 2, 3)
    meet(b, h, (across_x, across_y, partner), line)
    chip = b // 2
    targets = (3 - chip, chip + 1 - 2 * x, chip + 2 - 4 * y, chip)
    started = []
    spread = [i for i in range(n) if kinds[i][1]]

    def go(copy):
        copy.start()
        started.append(copy)

    def part(ref, cut):
        axis, start, size = cut
        return ref.at[(slice(None),) * axis + (pl.ds(start, size),)]

    def along(i, src, landing, d):
        go(
            remote(
                src, landing, line_send.at[i, d], line_recv.at[i, 1 if d == 1 else seen], (b, line[d])
            )
        )

    locals_ = []
    loads = {}
    for t in range(4):
        for i in spread:
            from_partner, total = bufs[i][0], bufs[i][1]
            go(
                remote(
                    ins[i].at[pl.ds((targets[t] * 2 + 1 - core) * 4, 4)],
                    from_partner.at[t],
                    core_send.at[i, t],
                    core_recv.at[i, t],
                    (partner, h),
                )
            )
            load = pltpu.make_async_copy(
                ins[i].at[pl.ds((targets[t] * 2 + core) * 4, 4)], total.at[t], local_sem.at[i, t]
            )
            load.start()
            loads[i, t] = load
    for i in range(n):
        if i in spread:
            continue
        for d in (3, 2, 1):
            along(i, ins[i].at[line[d]], outs[i].at[h], d)
        own = pltpu.make_async_copy(ins[i].at[h], outs[i].at[h], own_sem.at[i])
        own.start()
        locals_.append(own)

    def wait_for(ref, i, d, k):
        remote(ref, ref, send.at[i, d, k], recv.at[i, d, k], (partner, h)).wait_recv()

    def ready(i, t):
        loads[i, t].wait()
        here = bufs[i][0].at[t]
        remote(here, here, core_send.at[i, t], core_recv.at[i, t], (partner, h)).wait_recv()

    def both_cores(i, t, d, extra=()):
        from_partner, total = bufs[i][0], bufs[i][1]
        place = line[d]
        value = total[t, place].astype(jnp.float32) + from_partner[t, place].astype(jnp.float32)
        for ref in extra:
            value = value + ref[d].astype(jnp.float32)
        total[t, place] = value.astype(total.dtype)

    def add_corner(i, t, d, ref, cut):
        total = bufs[i][1]
        axis, start, size = cut
        at = (t, line[d]) + (slice(None),) * axis + (pl.ds(start, size),)
        value = total[at].astype(jnp.float32) + ref[d].astype(jnp.float32)
        total[at] = value.astype(total.dtype)

    order = (3, 2, 1, 0)

    def corner_step(i):
        total = bufs[i][1]
        first, second = kinds[i][2]
        ready(i, 0)
        for d in order:
            both_cores(i, 0, d)
            mine = total.at[0, line[d]]
            if first is not None:
                go(remote(part(mine, first), bufs[i][2].at[d], send.at[i, d, 0], recv.at[i, d, 0], (across_x, h)))
            if second is not None:
                go(remote(part(mine, second), bufs[i][3].at[d], send.at[i, d, 1], recv.at[i, d, 1], (across_y, h)))

    def side_step(i):
        total = bufs[i][1]
        first, second = kinds[i][2]
        ready(i, 1)
        ready(i, 2)
        for d in order:
            both_cores(i, 1, d)
            if second is not None:
                wait_for(bufs[i][3].at[d], i, d, 1)
                add_corner(i, 1, d, bufs[i][3], second)
            go(remote(total.at[1, line[d]], bufs[i][4].at[d], send.at[i, d, 2], recv.at[i, d, 2], (across_x, h)))
            both_cores(i, 2, d)
            if first is not None:
                wait_for(bufs[i][2].at[d], i, d, 0)
                add_corner(i, 2, d, bufs[i][2], first)
            go(remote(total.at[2, line[d]], bufs[i][5].at[d], send.at[i, d, 3], recv.at[i, d, 3], (across_y, h)))

    def own_step(i):
        summed = kinds[i][0]
        total = bufs[i][1]
        ready(i, 3)
        for d in order:
            wait_for(bufs[i][4].at[d], i, d, 2)
            wait_for(bufs[i][5].at[d], i, d, 3)
            both_cores(i, 3, d, (bufs[i][4], bufs[i][5]))
            if d > 0:
                landing = bufs[i][6].at[1 if d == 1 else seen] if summed else outs[i].at[h]
                along(i, total.at[3, line[d]], landing, d)
            elif not summed:
                own = pltpu.make_async_copy(total.at[3, h], outs[i].at[h], own_sem.at[i])
                own.start()
                locals_.append(own)

    for i in spread:
        corner_step(i)
    for at, i in enumerate(spread):
        side_step(i)
        if at > 0:
            own_step(spread[at - 1])
    if spread:
        own_step(spread[-1])
    for i in range(n):
        summed = kinds[i][0]
        for d in range(1, 4):
            landing = bufs[i][6].at[d] if summed else outs[i].at[line[d]]
            remote(
                landing, landing, line_send.at[i, d], line_recv.at[i, d], (b, line[d])
            ).wait_recv()
        if summed:
            value = bufs[i][1][3, h].astype(jnp.float32)
            for d in range(1, 4):
                value = value + bufs[i][6][d].astype(jnp.float32)
            outs[i][...] = value
    for own in locals_:
        own.wait()
    for copy in started:
        copy.wait_send()


def scatter_call(arrays, kinds, collective):
    n = len(arrays)
    shapes = []
    out_specs = []
    scratch = []
    for a, (summed, spread, halves) in zip(arrays, kinds):
        chunk = a.shape[1:]
        if spread:
            scratch += [pltpu.VMEM((4, 4) + chunk, a.dtype), pltpu.VMEM((4, 4) + chunk, a.dtype)]
            for cut in halves:
                size = list(chunk)
                if cut is not None:
                    size[cut[0]] = cut[2]
                else:
                    size = [8, 128]
                scratch.append(pltpu.VMEM((4,) + tuple(size), a.dtype))
            scratch += [pltpu.VMEM((4,) + chunk, a.dtype)] * 2
            if summed:
                scratch.append(pltpu.VMEM((4,) + chunk, a.dtype))
        if summed:
            shapes.append(jax.ShapeDtypeStruct(chunk, jnp.float32))
            out_specs.append(pl.BlockSpec(memory_space=pltpu.VMEM))
        else:
            shapes.append(jax.ShapeDtypeStruct((4,) + chunk, a.dtype))
            out_specs.append(pl.BlockSpec(memory_space=pl.ANY))
    return pl.pallas_call(
        partial(scatter_kernel, kinds),
        out_shape=tuple(shapes),
        in_specs=[pl.BlockSpec(memory_space=pl.ANY)] * n,
        out_specs=tuple(out_specs),
        scratch_shapes=scratch
        + [
            pltpu.SemaphoreType.DMA((n, 4)),
            pltpu.SemaphoreType.DMA((n,)),
            pltpu.SemaphoreType.DMA((n, 4)),
            pltpu.SemaphoreType.DMA((n, 4)),
            pltpu.SemaphoreType.DMA((n, 4)),
            pltpu.SemaphoreType.DMA((n, 4)),
            pltpu.SemaphoreType.DMA((n, 4, 4)),
            pltpu.SemaphoreType.DMA((n, 4, 4)),
        ],
        compiler_params=pltpu.CompilerParams(
            collective_id=collective, has_side_effects=True, vmem_limit_bytes=60 * 2**20
        ),
        name=f"scatter{collective}",
    )(*arrays)


def lanes_of(shape, low):
    lane = lax.broadcasted_iota(jnp.int32, shape, len(shape) - 1)
    if isinstance(low, bool):
        return lane < HD if low else lane >= HD
    return lane // HD == jnp.where(low, 0, 1)


def dot(left_side, right_side, contract=((1,), (0,))):
    return lax.dot_general(
        left_side, right_side, (contract, ((), ())), preferred_element_type=jnp.float32
    )


ROWS = ((1,), (1,))
COLS = ((0,), (0,))


def halves(array, col):
    return array[:, col : col + HD]


def project_kernel(x_ref, w_ref, bias_ref, q_out, kv_out):
    rows = x_ref.shape[1]
    width = x_ref.shape[2]
    tokens = x_ref[...].reshape(2 * rows, width)
    made = []
    for k in range(3):
        part = dot(tokens, w_ref[:, k * width : (k + 1) * width])
        if k != 1:
            part = part + bias_ref[k // 2 : k // 2 + 1, :]
        made.append(part.astype(jnp.bfloat16))
    q, k, v = made
    groups, per, _, _ = q_out.shape
    for g in range(groups):
        for j in range(per):
            col = (g * per + j) * HD
            q_out[g, j] = jnp.concatenate([halves(q[:rows], col), halves(q[rows:], col)], axis=1)
            kv_out[g, j] = jnp.concatenate([halves(k[:rows], col), halves(v[:rows], col)], axis=1)
            kv_out[g, per + j] = jnp.concatenate([halves(v[rows:], col), halves(k[rows:], col)], axis=1)


def project_call(tokens, weight, bias, groups):
    micro, rows, width = tokens.shape
    per = HEADS // groups
    whole = pl.BlockSpec(memory_space=pltpu.VMEM)
    return pl.pallas_call(
        project_kernel,
        out_shape=(
            jax.ShapeDtypeStruct((groups, per, rows, 2 * HD), jnp.bfloat16),
            jax.ShapeDtypeStruct((groups, 2 * per, rows, 2 * HD), jnp.bfloat16),
        ),
        grid=(1,),
        in_specs=[
            pl.BlockSpec((micro, rows, width), lambda i: (0, 0, 0)),
            pl.BlockSpec((width, 3 * width), lambda i: (0, 0)),
            pl.BlockSpec(bias.shape, lambda i: (0, 0)),
        ],
        out_specs=(
            pl.BlockSpec((groups, per, rows, 2 * HD), lambda i: (0, 0, 0, 0)),
            pl.BlockSpec((groups, 2 * per, rows, 2 * HD), lambda i: (0, 0, 0, 0)),
        ),
        compiler_params=pltpu.CompilerParams(vmem_limit_bytes=56 * 2**20),
        name="project",
    )(tokens, weight, bias)


def listed_rows(table_ref, blocks, per, m, n, j):
    shard = table_ref[2 * blocks * per * RAND + 2 * GLOB]
    total = table_ref[2 * blocks * per * RAND + 2 * GLOB + 1]
    here = shard * blocks + n
    rows = [jnp.maximum(here - 1, 0), here, jnp.minimum(here + 1, total - 1)]
    for r in range(RAND):
        rows.append(table_ref[((m * blocks + n) * per + j) * RAND + r])
    for g in range(GLOB):
        rows.append(table_ref[2 * blocks * per * RAND + m * GLOB + g])
    return rows, here, total


def global_of(table_ref, blocks, per, at):
    base = 2 * blocks * per * RAND
    return table_ref[base + at], table_ref[base + 2 * GLOB]


def outside(here, total, listed):
    lane = lax.broadcasted_iota(jnp.int32, (1, listed * BLOCK), 1)
    before = jnp.logical_and(lane < BLOCK, here == 0)
    after = jnp.logical_and(
        jnp.logical_and(lane >= 2 * BLOCK, lane < 3 * BLOCK), here == total - 1
    )
    return jnp.where(jnp.logical_or(before, after), -jnp.inf, 0.0)


def only(value, low):
    return jnp.where(lanes_of(value.shape, low), value, jnp.zeros_like(value))


def attend_kernel(table_ref, q_ref, kv_ref, out_ref, lse_ref):
    places_, per, in_place, block, _ = q_ref.shape
    blocks = places_ * in_place
    scale = jnp.bfloat16(HD ** (-0.5))
    units = [(j, m) for j in range(per) for m in range(2)]

    def query_block(n, carry):
        kvs, scores = [], []
        for j, m in units:
            rows, here, total = listed_rows(table_ref, blocks, per, m, n, j)
            kvs.append(
                jnp.concatenate(
                    [kv_ref[r // in_place, m * per + j, r % in_place] for r in rows], axis=0
                )
            )
            q = only(q_ref[n // in_place, j, n % in_place], m == 0) * scale
            scores.append(dot(q, kvs[-1], ROWS) + outside(here, total, len(rows)))
        raised = []
        for (j, m), score in zip(units, scores):
            top = jnp.max(score, axis=1, keepdims=True)
            raised.append(jnp.exp(score - top))
            total_sum = jnp.sum(raised[-1], axis=1, keepdims=True)
            raised[-1] = raised[-1] * (1.0 / total_sum)
            lse_ref[n // in_place, j, m, n % in_place] = jnp.broadcast_to(
                top + jnp.log(total_sum), (block, 2 * HD)
            )
        outs = [dot(r.astype(jnp.bfloat16), kv) for r, kv in zip(raised, kvs)]
        for j in range(per):
            out_ref[n // in_place, j, n % in_place] = jnp.where(
                lanes_of(outs[0].shape, True), outs[2 * j + 1], outs[2 * j]
            ).astype(jnp.bfloat16)
        return carry

    lax.fori_loop(0, blocks, query_block, 0)
    step = 8
    heads = range(per)

    def global_rows(at, carry):
        m = at // GLOB
        row, shard = global_of(table_ref, blocks, per, at)
        local = row % blocks
        at_place, at_row = local // in_place, local % in_place

        @pl.when(row // blocks == shard)
        def _():
            def keys(j, spot):
                return kv_ref[pl.ds(spot, step), m * per + j].reshape(
                    step * in_place * block, 2 * HD
                )

            spots = range(0, kv_ref.shape[0], step)
            qs = [only(q_ref[at_place, j, at_row], m == 0) * scale for j in heads]
            scores = [[dot(qs[j], keys(j, spot), ROWS) for spot in spots] for j in heads]
            raised, sums = [], []
            for j in heads:
                top = scores[j][0].max(axis=1, keepdims=True)
                for s in scores[j][1:]:
                    top = jnp.maximum(top, s.max(axis=1, keepdims=True))
                raised.append([jnp.exp(s - top) for s in scores[j]])
                sums.append(sum(jnp.sum(r, axis=1, keepdims=True) for r in raised[j]))
                lse_ref[at_place, j, m, at_row] = jnp.broadcast_to(
                    top + jnp.log(sums[j]), (block, 2 * HD)
                )
            for j in heads:
                out = sum(
                    dot(r.astype(jnp.bfloat16), keys(j, spot)) for r, spot in zip(raised[j], spots)
                )
                old = out_ref[at_place, j, at_row]
                out_ref[at_place, j, at_row] = jnp.where(
                    lanes_of(old.shape, m == 1), (out / sums[j]).astype(jnp.bfloat16), old
                )

        return carry

    lax.fori_loop(0, 2 * GLOB, global_rows, 0)


def attend_call(table, q, kv):
    spec = pl.BlockSpec(memory_space=pltpu.VMEM)
    places_, per, in_place, block, lanes = q.shape
    return pl.pallas_call(
        attend_kernel,
        out_shape=(
            jax.ShapeDtypeStruct(q.shape, jnp.bfloat16),
            jax.ShapeDtypeStruct((places_, per, 2, in_place, block, lanes), jnp.float32),
        ),
        in_specs=[pl.BlockSpec(memory_space=pltpu.SMEM), spec, spec],
        out_specs=(spec, spec),
        compiler_params=pltpu.CompilerParams(vmem_limit_bytes=56 * 2**20),
        name="attend",
    )(table, q, kv)


def attend_back_kernel(
    table_ref, q_ref, kv_in, d_ref, out_ref, lse_ref, dq_ref, dkv_out, total_ref, kv_ref, in_sem, out_sem
):
    places_, per, in_place, block, _ = q_ref.shape
    blocks = places_ * in_place
    scale = jnp.bfloat16(HD ** (-0.5))
    units = [(j, m) for j in range(per) for m in range(2)]

    step = 8
    fetch = pltpu.make_async_copy(kv_in, kv_ref, in_sem)
    fetch.start()

    def clear(i, carry):
        total_ref[i] = jnp.zeros(total_ref.shape[1:], jnp.float32)
        return carry

    lax.fori_loop(0, total_ref.shape[0], clear, 0)
    fetch.wait()

    def pair_of(n, j, m, keep):
        at = (n // in_place, j, n % in_place)
        q = only(q_ref[at], m == 0) * scale
        d = only(d_ref[at], m == 1)
        if keep is not None:
            d = d * keep
        delta = jnp.sum(
            d.astype(jnp.float32) * out_ref[at].astype(jnp.float32), axis=1, keepdims=True
        )
        return jnp.concatenate([q, d], axis=0), delta

    def wide(column, width):
        return jnp.concatenate([column] * (width // column.shape[1]), axis=1)

    def query_block(n, carry):
        listed, kvs, pairs, deltas, boths = [], [], [], [], []
        for j, m in units:
            rows, here, total = listed_rows(table_ref, blocks, per, m, n, j)
            is_global = jnp.logical_or(here == rows[-1], here == rows[-2])
            keep = jnp.where(is_global, 0.0, 1.0).astype(jnp.bfloat16)
            kv = jnp.concatenate(
                [kv_ref[r // in_place, m * per + j, r % in_place] for r in rows], axis=0
            )
            pair, delta = pair_of(n, j, m, keep)
            listed.append(rows)
            kvs.append(kv)
            pairs.append(pair)
            deltas.append(delta)
            boths.append(dot(pair, kv, ROWS))
        weights = []
        for (j, m), both, delta, kv, rows in zip(units, boths, deltas, kvs, listed):
            width = both.shape[1]
            lse = lse_ref[n // in_place, j, m, n % in_place]
            scores = both[:block] + outside(here, total, len(rows))
            probs = jnp.exp(scores - wide(lse, width))
            d_scores = probs * (both[block:] - delta)
            weights.append(
                jnp.concatenate(
                    [d_scores.astype(jnp.bfloat16), probs.astype(jnp.bfloat16)], axis=0
                )
            )
        outs = []
        for (j, m), weight, pair, kv, rows in zip(units, weights, pairs, kvs, listed):
            d_kv = dot(weight, pair, COLS)
            for at, r in enumerate(rows):
                total_ref[r // in_place, m * per + j, r % in_place] += d_kv[
                    at * block : (at + 1) * block
                ]
            outs.append(dot(weight[:block], kv) * HD ** (-0.5))
        for j in range(per):
            dq_ref[n // in_place, j, n % in_place] = jnp.where(
                lanes_of(outs[0].shape, True), outs[2 * j], outs[2 * j + 1]
            ).astype(jnp.bfloat16)
        return carry

    lax.fori_loop(0, blocks, query_block, 0)

    heads = range(per)

    def global_rows(at, carry):
        m = at // GLOB
        row, shard = global_of(table_ref, blocks, per, at)
        local = row % blocks
        at_place, at_row = local // in_place, local % in_place

        @pl.when(row // blocks == shard)
        def _():
            pairs = [pair_of(local, j, m, None) for j in heads]

            def some_keys(spot, d_qs):
                at_keys = pl.ds(spot * step, step)
                kvs = [
                    kv_ref[at_keys, m * per + j].reshape(step * in_place * block, 2 * HD)
                    for j in heads
                ]
                boths = [dot(pairs[j][0], kvs[j], ROWS) for j in heads]
                weights = []
                for j in heads:
                    lse = lse_ref[at_place, j, m, at_row]
                    probs = jnp.exp(boths[j][:block] - wide(lse, boths[j].shape[1]))
                    d_scores = probs * (boths[j][block:] - pairs[j][1])
                    weights.append(
                        jnp.concatenate(
                            [d_scores.astype(jnp.bfloat16), probs.astype(jnp.bfloat16)], axis=0
                        )
                    )
                for j in heads:
                    total_ref[at_keys, m * per + j] += dot(weights[j], pairs[j][0], COLS).reshape(
                        step, in_place, block, 2 * HD
                    )
                return tuple(d_qs[j] + dot(weights[j][:block], kvs[j]) for j in heads)

            d_qs = lax.fori_loop(
                0,
                kv_ref.shape[0] // step,
                some_keys,
                tuple(jnp.zeros((block, 2 * HD), jnp.float32) for _ in heads),
            )
            for j in heads:
                old = dq_ref[at_place, j, at_row]
                dq_ref[at_place, j, at_row] = jnp.where(
                    lanes_of(old.shape, m == 0), (d_qs[j] * HD ** (-0.5)).astype(jnp.bfloat16), old
                )

        return carry

    lax.fori_loop(0, 2 * GLOB, global_rows, 0)

    def give(i, carry):
        kv_ref[i] = total_ref[i].astype(jnp.bfloat16)
        return carry

    gives = []
    for at, s in enumerate(range(0, total_ref.shape[0], step)):
        lax.fori_loop(s, s + step, give, 0)
        gives.append(
            pltpu.make_async_copy(
                kv_ref.at[pl.ds(s, step)], dkv_out.at[pl.ds(s, step)], out_sem.at[at]
            )
        )
        gives[-1].start()
    for copy in gives:
        copy.wait()


def attend_back_call(table, q, kv, d, out, lse):
    spec = pl.BlockSpec(memory_space=pltpu.VMEM)
    far = pl.BlockSpec(memory_space=pl.ANY)
    return pl.pallas_call(
        attend_back_kernel,
        out_shape=(
            jax.ShapeDtypeStruct(q.shape, jnp.bfloat16),
            jax.ShapeDtypeStruct(kv.shape, jnp.bfloat16),
        ),
        in_specs=[pl.BlockSpec(memory_space=pltpu.SMEM), spec, far, spec, spec, spec],
        out_specs=(spec, far),
        scratch_shapes=[
            pltpu.VMEM(kv.shape, jnp.float32),
            pltpu.VMEM(kv.shape, jnp.bfloat16),
            pltpu.SemaphoreType.DMA,
            pltpu.SemaphoreType.DMA((kv.shape[0] // 8,)),
        ],
        compiler_params=pltpu.CompilerParams(vmem_limit_bytes=60 * 2**20),
        name="attend_back",
    )(table, q, kv, d, out, lse)


def centre(values):
    center = jnp.mean(values, axis=1, keepdims=True)
    centred = values - center
    spread = jnp.mean(centred * centred, axis=1, keepdims=True)
    inverse = lax.rsqrt(spread + 1e-12)
    return centred * inverse, inverse


def centre_back(hat, inverse, grad):
    return inverse * (
        grad
        - jnp.mean(grad, axis=1, keepdims=True)
        - hat * jnp.mean(grad * hat, axis=1, keepdims=True)
    )


def rows_sum(values):
    return jnp.sum(values, axis=0, keepdims=True)


def dense_kernel(
    c_ref, x_ref, cot_ref, wo_in, up_in, down_in, vec_ref, up_bias_ref,
    out_ref, d_mix_ref, d_c_ref, g_out_ref, g_up_out, g_down_out, g_vec_ref, g_up_bias_ref,
    ctx, first, hat, low, low_t, act, slope, ffn, wo_ref, up_ref, down_ref, g_up_ref, g_down_ref, in_sem, out_sem,
):
    groups, per, rows, _ = c_ref.shape
    width = x_ref.shape[2]
    ff = up_ref.shape[1]
    chunk = 384
    fetches = [
        pltpu.make_async_copy(wo_in.at[:, pl.ds(3 * width, width)], wo_ref, in_sem.at[0]),
        pltpu.make_async_copy(up_in, up_ref, in_sem.at[1]),
        pltpu.make_async_copy(down_in, down_ref, in_sem.at[2]),
    ]
    for copy in fetches:
        copy.start()
    out_bias, attn_gain, attn_shift, down_bias, ffn_gain, ffn_shift = (
        vec_ref[k : k + 1, :] for k in range(6)
    )
    for p in range(HEADS // 2):
        one = c_ref[(2 * p) // per, (2 * p) % per]
        two = c_ref[(2 * p + 1) // per, (2 * p + 1) % per]
        at = pl.ds(p * 2 * HD, 2 * HD)
        ctx[:rows, at] = jnp.concatenate([one[:, HD:], two[:, HD:]], axis=1)
        ctx[rows:, at] = jnp.concatenate([one[:, :HD], two[:, :HD]], axis=1)
    tokens = x_ref[...].reshape(2 * rows, width).astype(jnp.float32)
    fetches[0].wait()
    hat_first, inverse_first = centre(tokens + dot(ctx[...], wo_ref[...]) + out_bias)
    hat[...] = hat_first
    first[...] = hat_first * attn_gain + attn_shift
    low[...] = first[...].astype(jnp.bfloat16)
    low_t[...] = first[...].T.astype(jnp.bfloat16)
    ffn[...] = first[...] + down_bias
    fetches[1].wait()
    fetches[2].wait()

    def forward(i, carry):
        at = pl.ds(pl.multiple_of(i * chunk, chunk), chunk)
        hidden = dot(low[...], up_ref[:, at]) + up_bias_ref[:, at]
        share = 0.5 * (1.0 + lax.erf(hidden * 0.7071067811865476))
        bell = jnp.exp(-0.5 * hidden * hidden) * 0.3989422804014327
        slope[:, at] = share + hidden * bell
        act_low = (hidden * share).astype(jnp.bfloat16)
        act[:, at] = act_low
        ffn[...] += dot(act_low, down_ref[at, :])
        return carry

    lax.fori_loop(0, ff // chunk, forward, 0)
    hat_second, inverse_second = centre(ffn[...])
    out_ref[...] = (
        (hat_second * ffn_gain + ffn_shift).astype(jnp.bfloat16).reshape(2, rows, width)
    )
    cot = cot_ref[...].reshape(2 * rows, width).astype(jnp.float32)
    g_vec_ref[4:5, :] = rows_sum(cot * hat_second)
    g_vec_ref[5:6, :] = rows_sum(cot)
    d_second = centre_back(hat_second, inverse_second, cot * ffn_gain)
    d_ffn = d_second.astype(jnp.bfloat16)
    g_vec_ref[3:4, :] = rows_sum(d_ffn.astype(jnp.float32))
    ffn[...] = d_second

    def leave(i):
        at = pl.ds(pl.multiple_of(i * chunk, chunk), chunk)
        return (
            pltpu.make_async_copy(g_up_ref.at[:, at], g_up_out.at[:, at], out_sem.at[0, i]),
            pltpu.make_async_copy(g_down_ref.at[at, :], g_down_out.at[at, :], out_sem.at[1, i]),
        )

    def backward(i, carry):
        at = pl.ds(pl.multiple_of(i * chunk, chunk), chunk)
        d_act = dot(d_ffn, down_ref[at, :], ROWS)
        d_hidden = (d_act * slope[:, at]).astype(jnp.bfloat16)
        g_up_bias_ref[:, at] = rows_sum(d_hidden.astype(jnp.float32))
        g_down_ref[at, :] = dot(act[:, at], d_ffn, COLS).astype(jnp.bfloat16)
        g_up_ref[:, at] = dot(low_t[...], d_hidden).astype(jnp.bfloat16)
        for copy in leave(i):
            copy.start()
        ffn[...] += dot(d_hidden, up_ref[:, at], ROWS)
        return carry

    lax.fori_loop(0, ff // chunk, backward, 0)
    d_first = ffn[...]
    g_vec_ref[1:2, :] = rows_sum(d_first * hat[...])
    g_vec_ref[2:3, :] = rows_sum(d_first)
    d_mix = centre_back(hat[...], inverse_first, d_first * attn_gain)
    d_mix_ref[...] = d_mix
    d_branch = d_mix.astype(jnp.bfloat16)
    g_vec_ref[0:1, :] = rows_sum(d_branch.astype(jnp.float32))
    g_vec_ref[6:8, :] = jnp.zeros((2, width), jnp.float32)
    g_out_ref[...] = dot(ctx[...], d_branch, COLS).astype(jnp.bfloat16)
    d_ctx = dot(d_branch, wo_ref[...], ROWS).astype(jnp.bfloat16)
    for head in range(HEADS):
        d_c_ref[head // per, head % per] = jnp.concatenate(
            [halves(d_ctx[rows:], head * HD), halves(d_ctx[:rows], head * HD)], axis=1
        )
    for i in range(ff // chunk):
        for copy in leave(i):
            copy.wait()


def dense_call(c, tokens, cot, mixed, up, down, vec, up_bias):
    micro, rows, width = tokens.shape
    ff = up.shape[1]
    both = micro * rows
    far = pl.BlockSpec(memory_space=pl.ANY)
    f32, bf16 = jnp.float32, jnp.bfloat16

    def full(shape):
        return pl.BlockSpec(memory_space=pltpu.VMEM)

    outs = (
        jax.ShapeDtypeStruct(tokens.shape, bf16),
        jax.ShapeDtypeStruct((both, width), f32),
        jax.ShapeDtypeStruct(c.shape, bf16),
        jax.ShapeDtypeStruct((width, width), bf16),
        jax.ShapeDtypeStruct((width, ff), bf16),
        jax.ShapeDtypeStruct((ff, width), bf16),
        jax.ShapeDtypeStruct((8, width), f32),
        jax.ShapeDtypeStruct((1, ff), f32),
    )
    return pl.pallas_call(
        dense_kernel,
        out_shape=outs,
        in_specs=[
            full(c.shape),
            full(tokens.shape),
            full(cot.shape),
            far,
            far,
            far,
            full(vec.shape),
            full(up_bias.shape),
        ],
        out_specs=tuple(far if k in (4, 5) else full(o.shape) for k, o in enumerate(outs)),
        scratch_shapes=[
            pltpu.VMEM((both, width), bf16),
            pltpu.VMEM((both, width), f32),
            pltpu.VMEM((both, width), f32),
            pltpu.VMEM((both, width), bf16),
            pltpu.VMEM((width, both), bf16),
            pltpu.VMEM((both, ff), bf16),
            pltpu.VMEM((both, ff), f32),
            pltpu.VMEM((both, width), f32),
            pltpu.VMEM((width, width), bf16),
            pltpu.VMEM((width, ff), bf16),
            pltpu.VMEM((ff, width), bf16),
            pltpu.VMEM((width, ff), bf16),
            pltpu.VMEM((ff, width), bf16),
            pltpu.SemaphoreType.DMA((3,)),
            pltpu.SemaphoreType.DMA((2, ff // 384)),
        ],
        compiler_params=pltpu.CompilerParams(vmem_limit_bytes=60 * 2**20),
        name="dense",
    )(c, tokens, cot, mixed, up, down, vec, up_bias)


def project_back_kernel(
    q_ref, kv_ref, x_ref, w_ref, d_mix_ref, g_out_ref, d_x_ref, g_ref, g_vec_ref, d_q, d_k, d_v
):
    groups, per, rows, _ = q_ref.shape
    width = x_ref.shape[2]
    for p in range(HEADS // 2):
        at = pl.ds(p * 2 * HD, 2 * HD)

        def of(ref, shift, low):
            sides = []
            for head in (2 * p, 2 * p + 1):
                tile = ref[head // per, shift + head % per]
                sides.append(tile[:, :HD] if low else tile[:, HD:])
            return jnp.concatenate(sides, axis=1)

        d_q[:rows, at] = of(q_ref, 0, True)
        d_q[rows:, at] = of(q_ref, 0, False)
        d_k[:rows, at] = of(kv_ref, 0, True)
        d_v[:rows, at] = of(kv_ref, 0, False)
        d_k[rows:, at] = of(kv_ref, per, False)
        d_v[rows:, at] = of(kv_ref, per, True)
    tokens = x_ref[...].reshape(2 * rows, width)
    d_x = d_mix_ref[...]
    for k, part in enumerate((d_q, d_k, d_v)):
        at = slice(k * width, (k + 1) * width)
        d_x = d_x + dot(part[...], w_ref[:, at], ROWS)
        g_ref[:, at] = dot(tokens, part[...], COLS).astype(jnp.bfloat16)
        if k != 1:
            g_vec_ref[k // 2 : k // 2 + 1, :] = rows_sum(part[...].astype(jnp.float32))
    g_ref[:, 3 * width :] = g_out_ref[...]
    g_vec_ref[2:8, :] = jnp.zeros((6, width), jnp.float32)
    d_x_ref[...] = d_x.astype(jnp.bfloat16).reshape(2, rows, width)


def project_back_call(q, kv, tokens, mixed, d_mix, g_out):
    micro, rows, width = tokens.shape
    f32, bf16 = jnp.float32, jnp.bfloat16

    def full(shape):
        return pl.BlockSpec(shape, lambda i: (0,) * len(shape), pipeline_mode=pl.Buffered(1))

    outs = (
        jax.ShapeDtypeStruct(tokens.shape, bf16),
        jax.ShapeDtypeStruct((width, 4 * width), bf16),
        jax.ShapeDtypeStruct((8, width), f32),
    )
    return pl.pallas_call(
        project_back_kernel,
        out_shape=outs,
        grid=(1,),
        in_specs=[
            full(q.shape),
            full(kv.shape),
            full(tokens.shape),
            full((width, 3 * width)),
            full(d_mix.shape),
            full(g_out.shape),
        ],
        out_specs=tuple(full(o.shape) for o in outs),
        scratch_shapes=[pltpu.VMEM((micro * rows, width), bf16)] * 3,
        compiler_params=pltpu.CompilerParams(vmem_limit_bytes=56 * 2**20),
        name="project_back",
    )(q, kv, tokens, mixed, d_mix, g_out)


def cut(axis, start, size):
    return (axis, start, size)


def near_body(inputs, cotangent, random_blocks, global_blocks, *shards):
    (
        query_weight, query_bias, key_weight, value_weight, value_bias, out_weight, out_bias, attn_gain,
        attn_shift, up_weight, up_bias, down_weight, down_bias, ffn_gain, ffn_shift,
    ) = shards
    groups = lax.axis_size("head")
    shard_count = lax.axis_size("blk")
    devices = groups * shard_count
    shard = lax.axis_index("blk")
    group = lax.axis_index("head")
    micro, rows, width = inputs.shape
    depth = query_weight.shape[0]
    ff = up_weight.shape[1]
    per = HEADS // groups
    in_place = rows // BLOCK
    blocks = groups * in_place
    vectors = jnp.stack(
        [query_bias, value_bias, out_bias, attn_gain, attn_shift, down_bias, ffn_gain, ffn_shift], axis=1
    )
    vectors = jnp.concatenate([vectors, up_bias.reshape(depth, -1)], axis=1)
    vectors = jnp.pad(vectors, ((0, 0), (0, 128 - vectors.shape[1])))
    mixed_shard = jnp.concatenate(
        [query_weight, key_weight, value_weight, out_weight, vectors], axis=1
    )
    half = 2 * width
    (mixed,) = gather_call(
        [mixed_shard], [(False, True, (cut(1, 0, half), cut(1, half, half + 128)))], 1
    )
    mixed = mixed.reshape(width, -1)
    rows_f32 = mixed[:, 4 * width : 4 * width + 16].astype(jnp.float32).T
    bias = rows_f32[:8]
    vec = rows_f32[2:10]
    up_bias_row = mixed[:, 4 * width + 8 : 4 * width + 8 + ff // width].astype(jnp.float32).reshape(1, ff)
    q_parts, kv_parts = project_call(inputs, mixed, bias, groups)
    pairs = (cut(0, 0, per), cut(0, per, per))
    q, kv, up, down = gather_call(
        [q_parts, kv_parts, up_weight, down_weight],
        [
            (True, False, None),
            (True, True, pairs),
            (False, True, (cut(1, 0, ff), None)),
            (False, True, (None, cut(1, 0, width))),
        ],
        2,
    )
    up = up.reshape(width, ff)
    down = down.reshape(ff, width)
    mine = lax.dynamic_slice(
        random_blocks,
        (0, shard * blocks, group * per, 0),
        (micro, blocks, per, RAND),
    )
    table = jnp.concatenate(
        [
            mine.reshape(-1),
            global_blocks.reshape(-1),
            jnp.stack([shard, shard_count * blocks]).astype(jnp.int32),
        ]
    )
    split = (in_place, BLOCK, 2 * HD)
    q = q.reshape((groups, per) + split)
    kv = kv.reshape((devices, 2 * per) + split)
    packed = (groups, per, rows, 2 * HD)
    attended, lse = attend_call(table, q, kv)
    (context,) = gather_call([attended.reshape(packed)], [(True, False, None)], 3)
    layer_out, d_mix, d_context, g_out, g_up, g_down, g_vec, g_up_bias = dense_call(
        context, inputs, cotangent, mixed, up, down, vec, up_bias_row
    )
    (d_context,) = gather_call([d_context], [(True, False, None)], 4)
    d_q, d_kv = attend_back_call(table, q, kv, d_context.reshape(q.shape), attended, lse)
    d_q, d_kv, grad_up, grad_down = scatter_call(
        [
            d_q.reshape(packed),
            d_kv.reshape(devices, 2 * per, rows, 2 * HD),
            g_up.reshape(devices, depth, ff),
            g_down.reshape(devices, -1, width),
        ],
        [
            (False, False, None),
            (False, True, pairs),
            (True, True, (cut(1, 0, ff), None)),
            (True, True, (None, cut(1, 0, width))),
        ],
        5,
    )
    input_grad, g_mixed, g_vec_two = project_back_call(d_q, d_kv, inputs, mixed, d_mix, g_out)
    sums = jnp.concatenate([g_vec_two[:2], g_vec[:6]], axis=0).reshape(8, devices, depth)
    sums = jnp.concatenate(
        [sums.transpose(1, 0, 2), g_up_bias.reshape(devices, ff // width, depth)], axis=1
    )
    sums = jnp.pad(sums, ((0, 0), (0, 16 - sums.shape[1]), (0, 128 - depth)))
    grad_mixed, grad_vec = scatter_call(
        [g_mixed.reshape(devices, depth, 4 * width), sums],
        [
            (True, True, (cut(1, 0, half), cut(1, half, half))),
            (True, True, (cut(1, 0, 128), None)),
        ],
        6,
    )
    grad_query, grad_key, grad_value, grad_out = (
        grad_mixed[:, k * width : (k + 1) * width] for k in range(4)
    )
    vector = [grad_vec[k, :depth] for k in range(8)]
    grad_up_bias = grad_vec[8 : 8 + ff // width, :depth].reshape(-1)
    return (
        layer_out, input_grad, grad_query, vector[0], grad_key, grad_value, vector[1], grad_out,
        vector[2], vector[3], vector[4], grad_up, grad_up_bias, grad_down, vector[5], vector[6], vector[7],
    )


def with_halo(cells, sides, width):
    for axis, dim in sides:
        count = lax.axis_size(axis)
        ends = count - 1
        head = lax.slice_in_dim(cells, 0, width, axis=dim)
        tail = lax.slice_in_dim(cells, cells.shape[dim] - width, cells.shape[dim], axis=dim)
        cells = jnp.concatenate(
            [
                lax.ppermute(tail, axis, [(i, (i + 1) % count) for i in range(ends)]),
                cells,
                lax.ppermute(head, axis, [((i + 1) % count, i) for i in range(ends)]),
            ],
            axis=dim,
        )
    return cells


def combined_all(part, axis, combine):
    gathered = jax.tree.map(lambda a: lax.all_gather(a, axis), part)

    def take(source):
        return jax.tree.map(lambda a: lax.dynamic_index_in_dim(a, source, 0, False), gathered)

    return lax.fori_loop(
        1, lax.axis_size(axis), lambda source, state: combine(state, take(source)), take(0)
    )


def taken(table, rows):
    return lax.map(lambda row: lax.dynamic_index_in_dim(table, row, 0, False), rows)


def layer_norm(values, norm_gain, norm_shift):
    center = jnp.mean(values, axis=-1, keepdims=True)
    centred = values - center
    spread = jnp.mean(centred * centred, axis=-1, keepdims=True)
    return centred * lax.rsqrt(spread + 1e-12) * norm_gain + norm_shift


def gelu_exact(values):
    return jax.nn.gelu(values, approximate=False)


def matmul(left_side, right_side):
    return jnp.dot(left_side, right_side, preferred_element_type=jnp.float32)


def matmul_left(left_side, right_side):
    return lax.dot_general(
        left_side, right_side, (((0,), (0,)), ((), ())), preferred_element_type=jnp.float32
    )


def matmul_right(left_side, right_side):
    return lax.dot_general(
        left_side, right_side, (((1,), (1,)), ((), ())), preferred_element_type=jnp.float32
    )


def column_sum(values):
    return jnp.sum(values.astype(jnp.float32), axis=0)


def combine_parts(earlier, later_part):
    joint_top = jnp.maximum(earlier[0], later_part[0])
    first_factor = jnp.exp(earlier[0] - joint_top)
    second_factor = jnp.exp(later_part[0] - joint_top)
    return (
        joint_top,
        earlier[1] * first_factor + later_part[1] * second_factor,
        earlier[2] * first_factor[..., None] + later_part[2] * second_factor[..., None],
    )


def fetch_weights(
    query_weight,
    query_bias,
    key_weight,
    value_weight,
    value_bias,
    out_weight,
    out_bias,
    attn_gain,
    attn_shift,
    up_weight,
    up_bias,
    down_weight,
    down_bias,
    ffn_gain,
    ffn_shift,
):
    return (
        lax.all_gather(query_weight, ("blk", "head"), axis=0, tiled=True),
        lax.all_gather(query_bias, ("blk", "head"), axis=0, tiled=True),
        lax.all_gather(key_weight, ("blk", "head"), axis=0, tiled=True),
        lax.all_gather(value_weight, ("blk", "head"), axis=0, tiled=True),
        lax.all_gather(value_bias, ("blk", "head"), axis=0, tiled=True),
        lax.all_gather(out_weight, ("blk", "head"), axis=0, tiled=True),
        lax.all_gather(out_bias, ("blk", "head"), axis=0, tiled=True),
        lax.all_gather(attn_gain, ("blk", "head"), axis=0, tiled=True),
        lax.all_gather(attn_shift, ("blk", "head"), axis=0, tiled=True),
        lax.all_gather(up_weight, ("blk", "head"), axis=0, tiled=True),
        lax.all_gather(up_bias, ("blk", "head"), axis=0, tiled=True),
        lax.all_gather(down_weight, ("blk", "head"), axis=0, tiled=True),
        lax.all_gather(down_bias, ("blk", "head"), axis=0, tiled=True),
        lax.all_gather(ffn_gain, ("blk", "head"), axis=0, tiled=True),
        lax.all_gather(ffn_shift, ("blk", "head"), axis=0, tiled=True),
    )


def reduce_grads(totals):
    return (
        lax.psum_scatter(totals[0], ("blk", "head"), scatter_dimension=0, tiled=True),
        lax.psum_scatter(totals[1], ("blk", "head"), scatter_dimension=0, tiled=True),
        lax.psum_scatter(totals[2], ("blk", "head"), scatter_dimension=0, tiled=True),
        lax.psum_scatter(totals[3], ("blk", "head"), scatter_dimension=0, tiled=True),
        lax.psum_scatter(totals[4], ("blk", "head"), scatter_dimension=0, tiled=True),
        lax.psum_scatter(totals[5], ("blk", "head"), scatter_dimension=0, tiled=True),
        lax.psum_scatter(totals[6], ("blk", "head"), scatter_dimension=0, tiled=True),
        lax.psum_scatter(totals[7], ("blk", "head"), scatter_dimension=0, tiled=True),
        lax.psum_scatter(totals[8], ("blk", "head"), scatter_dimension=0, tiled=True),
        lax.psum_scatter(totals[9], ("blk", "head"), scatter_dimension=0, tiled=True),
        lax.psum_scatter(totals[10], ("blk", "head"), scatter_dimension=0, tiled=True),
        lax.psum_scatter(totals[11], ("blk", "head"), scatter_dimension=0, tiled=True),
        lax.psum_scatter(totals[12], ("blk", "head"), scatter_dimension=0, tiled=True),
        lax.psum_scatter(totals[13], ("blk", "head"), scatter_dimension=0, tiled=True),
        lax.psum_scatter(totals[14], ("blk", "head"), scatter_dimension=0, tiled=True),
    )


def sparse_forward(packed):
    group_queries, group_keys, group_values, group_allowed = packed
    attn_scale = HD ** (-0.5)
    scores = (
        jnp.einsum("gqhd,ghkd->ghqk", group_queries, group_keys, preferred_element_type=jnp.float32)
        * attn_scale
    )
    scores = jnp.where(group_allowed[:, None, None, :], scores, -jnp.inf)
    row_top = jnp.max(scores, axis=-1, keepdims=True)
    raised = jnp.exp(scores - row_top)
    row_total = jnp.sum(raised, axis=-1, keepdims=True)
    probs_low = (raised / row_total).astype(jnp.bfloat16)
    output = jnp.einsum(
        "ghqk,ghkd->gqhd", probs_low, group_values, preferred_element_type=jnp.float32
    )
    return (output, (row_top + jnp.log(row_total))[..., 0])


def sparse_backward(nearby, carried, packed):
    group_queries, group_keys, group_values, group_allowed, group_lse, group_grad = packed
    attn_scale = HD ** (-0.5)
    per_group = group_queries.shape[0]
    heads_dev = group_queries.shape[2]
    scores = (
        jnp.einsum("gqhd,ghkd->ghqk", group_queries, group_keys, preferred_element_type=jnp.float32)
        * attn_scale
    )
    scores = jnp.where(group_allowed[:, None, None, :], scores, -jnp.inf)
    probs = jnp.exp(scores - group_lse[..., None])
    d_probs = jnp.einsum(
        "gqhd,ghkd->ghqk", group_grad, group_values, preferred_element_type=jnp.float32
    )
    row_delta = jnp.sum(probs * d_probs, axis=-1, keepdims=True)
    d_scores = (probs * (d_probs - row_delta)).astype(jnp.bfloat16)
    d_queries = (
        jnp.einsum("ghqk,ghkd->gqhd", d_scores, group_keys, preferred_element_type=jnp.float32)
        * attn_scale
    )
    d_keys = (
        jnp.einsum("ghqk,gqhd->ghkd", d_scores, group_queries, preferred_element_type=jnp.float32)
        * attn_scale
    )
    d_values = jnp.einsum(
        "ghqk,gqhd->ghkd",
        probs.astype(jnp.bfloat16),
        group_grad,
        preferred_element_type=jnp.float32,
    )
    d_keys = d_keys.reshape(per_group, heads_dev, -1, BLOCK, HD)
    d_values = d_values.reshape(per_group, heads_dev, -1, BLOCK, HD)
    carried = (
        carried[0] + jnp.sum(d_keys[:, :, nearby:], axis=0),
        carried[1] + jnp.sum(d_values[:, :, nearby:], axis=0),
    )
    return (carried, (d_queries, d_keys[:, :, :nearby], d_values[:, :, :nearby]))


def micro_batch(tokens, cotangent_rows, random_rows, global_rows, weights):
    (
        full_query,
        full_query_bias,
        full_key,
        full_value,
        full_value_bias,
        full_out,
        full_out_bias,
        full_attn_gain,
        full_attn_shift,
        full_up,
        full_up_bias,
        full_down,
        full_down_bias,
        full_ffn_gain,
        full_ffn_shift,
    ) = weights
    attn_scale = HD ** (-0.5)
    shards = lax.axis_size("blk")
    head_groups = lax.axis_size("head")
    shard_index = lax.axis_index("blk")
    group_index = lax.axis_index("head")
    heads_dev = HEADS // head_groups
    group_width = heads_dev * HD
    listed = 3 + RAND + GLOB
    nearby = 3 + RAND
    projected = jnp.stack(
        [
            matmul(tokens, full_query) + full_query_bias,
            matmul(tokens, full_key),
            matmul(tokens, full_value) + full_value_bias,
        ]
    ).astype(jnp.bfloat16)
    by_head = lax.all_to_all(projected, "head", split_axis=2, concat_axis=1, tiled=True)
    row_count = by_head.shape[1]
    block_count = row_count // BLOCK
    blocks_all = block_count * shards
    key_rows = by_head[1]
    value_rows = by_head[2]
    padded = with_halo(by_head[1:3], (("blk", 1),), BLOCK)
    extended = padded.reshape(2, block_count + 2, BLOCK, heads_dev, HD).transpose(0, 1, 3, 2, 4)
    window = jnp.stack([extended[:, offset : offset + block_count] for offset in range(3)], axis=3)
    block_ids = shard_index * block_count + jnp.arange(block_count, dtype=jnp.int32)
    neighbour = block_ids[:, None] + jnp.arange(-1, 2, dtype=jnp.int32)[None, :]
    inside = (neighbour >= 0) & (neighbour < blocks_all)
    head_table = lax.dynamic_slice_in_dim(random_rows, group_index * heads_dev, heads_dev, 1)
    requests = block_count * heads_dev * RAND
    all_requests = head_table.reshape(shards, requests)
    capacity = (requests + shards - 1) // shards + 1
    wanted = lax.dynamic_slice_in_dim(all_requests, shard_index, 1, 0)[0]
    source = wanted // block_count
    place = jnp.arange(requests, dtype=jnp.int32)
    earlier = (place[:, None] > place[None, :]).astype(jnp.int32)
    same_source = (source[:, None] == source[None, :]).astype(jnp.int32)
    slot_index = jnp.sum(earlier * same_source, axis=1)
    mine_mask = (all_requests // block_count == shard_index).astype(jnp.int32)
    send_order = jnp.sum(earlier[None] * mine_mask[:, None, :], axis=2)
    match_mask = mine_mask[:, :, None] * (
        send_order[:, :, None] == jnp.arange(capacity, dtype=jnp.int32)[None, None, :]
    ).astype(jnp.int32)
    head_of = jnp.arange(requests, dtype=jnp.int32) // RAND % heads_dev
    row_of = all_requests % block_count * heads_dev + head_of[None, :]
    send_rows = jnp.sum(match_mask * row_of[:, :, None], axis=1)
    filled = jnp.sum(match_mask, axis=1).astype(jnp.float32)
    block_table = (
        by_head[1:3]
        .reshape(2, block_count, BLOCK, heads_dev, HD)
        .transpose(1, 3, 0, 2, 4)
        .reshape(block_count * heads_dev, 2, BLOCK, HD)
    )
    outgoing = taken(block_table, send_rows.reshape(-1))
    incoming = lax.all_to_all(outgoing, "blk", split_axis=0, concat_axis=0, tiled=True)
    fetched = taken(incoming, source * capacity + slot_index).reshape(
        block_count, heads_dev, RAND, 2, BLOCK, HD
    )
    owner_shard = global_rows // block_count
    present = owner_shard == shard_index
    local_block = global_rows % block_count
    own_rows = jnp.stack(
        [
            lax.dynamic_index_in_dim(
                by_head.reshape(3, block_count, BLOCK, group_width), local_block[g], 1, False
            )
            for g in range(GLOB)
        ],
        axis=1,
    )
    shared = lax.psum(
        jnp.where(present[None, :, None, None], own_rows.astype(jnp.float32), 0.0), "blk"
    ).astype(jnp.bfloat16)
    shared_pairs = shared[1:3].reshape(2, GLOB, BLOCK, heads_dev, HD).transpose(0, 3, 1, 2, 4)

    def listed_blocks(which):
        near_part = window[which]
        random_part = fetched[:, :, :, which]
        global_part = jnp.broadcast_to(
            shared_pairs[which][None], (block_count, heads_dev, GLOB, BLOCK, HD)
        )
        return jnp.concatenate([near_part, random_part, global_part], axis=2).reshape(
            block_count, heads_dev, listed * BLOCK, HD
        )

    per_group = min(8, block_count)
    group_count = block_count // per_group
    query_groups = by_head[0].reshape(group_count, per_group, BLOCK, heads_dev, HD)
    key_groups = listed_blocks(0).reshape(group_count, per_group, heads_dev, listed * BLOCK, HD)
    value_groups = listed_blocks(1).reshape(group_count, per_group, heads_dev, listed * BLOCK, HD)
    allowed = jnp.repeat(
        jnp.concatenate([inside, jnp.ones((block_count, RAND + GLOB), jnp.bool_)], axis=1),
        BLOCK,
        axis=1,
    )
    allow_groups = allowed.reshape(group_count, per_group, listed * BLOCK)
    sparse_out, sparse_lse = lax.map(
        sparse_forward, (query_groups, key_groups, value_groups, allow_groups)
    )
    global_queries = shared[0].reshape(GLOB, BLOCK, heads_dev, HD)
    key_heads = key_rows.reshape(row_count, heads_dev, HD)
    value_wide = value_rows.reshape(row_count, heads_dev, HD).astype(jnp.float32)
    global_scores = (
        jnp.einsum("gqhd,khd->ghqk", global_queries, key_heads, preferred_element_type=jnp.float32)
        * attn_scale
    )
    global_top = jnp.max(global_scores, axis=-1)
    global_raised = jnp.exp(global_scores - global_top[..., None])
    merged = combined_all(
        (
            global_top,
            jnp.sum(global_raised, axis=-1),
            jnp.einsum(
                "ghqk,khd->ghqd", global_raised, value_wide, precision=lax.Precision.HIGHEST
            ),
        ),
        "blk",
        combine_parts,
    )
    global_out = merged[2] / merged[1][..., None]
    global_lse = merged[0] + jnp.log(merged[1])
    global_hits = (block_ids[:, None] == global_rows[None, :]).astype(jnp.float32)
    is_global = jnp.sum(global_hits, axis=1) > 0
    replaced = jnp.einsum("ng,ghqd->nqhd", global_hits, global_out, precision=lax.Precision.HIGHEST)
    context = jnp.where(
        is_global[:, None, None, None],
        replaced,
        sparse_out.reshape(block_count, BLOCK, heads_dev, HD),
    )
    context_rows = context.reshape(row_count, group_width).astype(jnp.bfloat16)
    context_tokens = lax.all_to_all(context_rows, "head", split_axis=0, concat_axis=1, tiled=True)
    branch = matmul(context_tokens, full_out) + full_out_bias
    first_in = tokens.astype(jnp.float32) + branch
    first_norm, first_pull = jax.vjp(
        layer_norm,
        first_in,
        full_attn_gain.astype(jnp.float32),
        full_attn_shift.astype(jnp.float32),
    )
    first_low = first_norm.astype(jnp.bfloat16)
    hidden = matmul(first_low, full_up) + full_up_bias
    act_value, gelu_pull = jax.vjp(gelu_exact, hidden)
    act_low = act_value.astype(jnp.bfloat16)
    ffn_out = matmul(act_low, full_down) + full_down_bias
    result, second_pull = jax.vjp(
        layer_norm,
        first_norm + ffn_out,
        full_ffn_gain.astype(jnp.float32),
        full_ffn_shift.astype(jnp.float32),
    )
    d_second, grad_ffn_gain, grad_ffn_shift = second_pull(cotangent_rows.astype(jnp.float32))
    d_ffn = d_second.astype(jnp.bfloat16)
    grad_down = matmul_left(act_low, d_ffn)
    grad_down_bias = column_sum(d_ffn)
    (d_hidden,) = gelu_pull(matmul_right(d_ffn, full_down))
    d_hidden_low = d_hidden.astype(jnp.bfloat16)
    grad_up = matmul_left(first_low, d_hidden_low)
    grad_up_bias = column_sum(d_hidden_low)
    d_first = d_second + matmul_right(d_hidden_low, full_up)
    d_mix, grad_attn_gain, grad_attn_shift = first_pull(d_first)
    d_branch = d_mix.astype(jnp.bfloat16)
    grad_out = matmul_left(context_tokens, d_branch)
    grad_out_bias = column_sum(d_branch)
    d_context = matmul_right(d_branch, full_out).astype(jnp.bfloat16)
    d_heads = lax.all_to_all(d_context, "head", split_axis=1, concat_axis=0, tiled=True).reshape(
        block_count, BLOCK, heads_dev, HD
    )
    d_sparse = jnp.where(is_global[:, None, None, None], jnp.zeros_like(d_heads), d_heads)
    d_global = lax.psum(
        jnp.where(
            present[:, None, None, None], taken(d_heads, local_block).astype(jnp.float32), 0.0
        ),
        "blk",
    )
    start_carry = (
        jnp.zeros((heads_dev, GLOB, BLOCK, HD), jnp.float32),
        jnp.zeros((heads_dev, GLOB, BLOCK, HD), jnp.float32),
    )
    global_sums, (d_query_parts, near_keys, near_values) = lax.scan(
        partial(sparse_backward, nearby),
        start_carry,
        (
            query_groups,
            key_groups,
            value_groups,
            allow_groups,
            sparse_lse,
            d_sparse.reshape(group_count, per_group, BLOCK, heads_dev, HD),
        ),
    )
    d_query_sparse = d_query_parts.reshape(block_count, BLOCK, heads_dev, HD)
    near_keys = near_keys.reshape(block_count, heads_dev, nearby, BLOCK, HD)
    near_values = near_values.reshape(block_count, heads_dev, nearby, BLOCK, HD)
    near_grads = jnp.stack([near_keys[:, :, :3], near_values[:, :, :3]])
    ext_grads = jnp.zeros((2, block_count + 2, heads_dev, BLOCK, HD), jnp.float32)
    for offset in range(3):
        ext_grads = ext_grads + jnp.pad(
            near_grads[:, :, :, offset], ((0, 0), (offset, 2 - offset), (0, 0), (0, 0), (0, 0))
        )
    rim_pair = jnp.stack([ext_grads[:, 0], ext_grads[:, block_count + 1]], axis=1)
    arrived = with_halo(rim_pair.astype(jnp.bfloat16), (("blk", 1),), 1).astype(rim_pair.dtype)
    inner_grads = ext_grads[:, 1 : block_count + 1]
    inner_grads = inner_grads.at[:, 0].add(arrived[:, 0]).at[:, block_count - 1].add(arrived[:, 3])
    far_grads = jnp.stack([near_keys[:, :, 3:], near_values[:, :, 3:]], axis=3).reshape(
        requests, 2, BLOCK, HD
    )
    outbox = (
        jnp.zeros((shards, capacity, 2, BLOCK, HD), jnp.float32)
        .at[source, slot_index]
        .set(far_grads)
    )
    arrived_slots = (
        lax.all_to_all(
            outbox.astype(jnp.bfloat16), "blk", split_axis=0, concat_axis=0, tiled=True
        ).astype(outbox.dtype)
        * filled[:, :, None, None, None]
    )
    landed = (
        jnp.zeros((block_count * heads_dev, 2, BLOCK, HD), jnp.float32)
        .at[send_rows.reshape(-1)]
        .add(arrived_slots.reshape(shards * capacity, 2, BLOCK, HD))
    )
    landed = landed.reshape(block_count, heads_dev, 2, BLOCK, HD)
    global_probs = jnp.exp(global_scores - global_lse[..., None])
    d_probs_global = jnp.einsum(
        "gqhd,khd->ghqk", d_global, value_wide, precision=lax.Precision.HIGHEST
    )
    delta_global = jnp.einsum(
        "gqhd,ghqd->ghq", d_global, global_out, precision=lax.Precision.HIGHEST
    )
    d_scores_global = (global_probs * (d_probs_global - delta_global[..., None])).astype(
        jnp.bfloat16
    )
    d_global_queries = (
        jnp.einsum("ghqk,khd->gqhd", d_scores_global, key_heads, preferred_element_type=jnp.float32)
        * attn_scale
    )
    d_keys_global = (
        jnp.einsum(
            "ghqk,gqhd->khd", d_scores_global, global_queries, preferred_element_type=jnp.float32
        )
        * attn_scale
    )
    d_values_global = jnp.einsum(
        "ghqk,gqhd->khd", global_probs, d_global, precision=lax.Precision.HIGHEST
    )
    returned = lax.psum(
        jnp.stack(
            [
                d_global_queries,
                global_sums[0].transpose(1, 2, 0, 3),
                global_sums[1].transpose(1, 2, 0, 3),
            ]
        ),
        "blk",
    )
    owned_grads = jnp.einsum(
        "ng,cgqhd->cnqhd", global_hits, returned, precision=lax.Precision.HIGHEST
    )
    d_query_total = d_query_sparse + owned_grads[0]
    d_key_total = (
        (inner_grads[0] + landed[:, :, 0]).transpose(0, 2, 1, 3)
        + d_keys_global.reshape(block_count, BLOCK, heads_dev, HD)
        + owned_grads[1]
    )
    d_value_total = (
        (inner_grads[1] + landed[:, :, 1]).transpose(0, 2, 1, 3)
        + d_values_global.reshape(block_count, BLOCK, heads_dev, HD)
        + owned_grads[2]
    )
    stacked = (
        jnp.stack([d_query_total, d_key_total, d_value_total])
        .reshape(3, row_count, group_width)
        .astype(jnp.bfloat16)
    )
    token_grads = lax.all_to_all(stacked, "head", split_axis=1, concat_axis=2, tiled=True)
    d_tokens = (
        d_mix
        + matmul_right(token_grads[0], full_query)
        + matmul_right(token_grads[1], full_key)
        + matmul_right(token_grads[2], full_value)
    )
    grads = (
        matmul_left(tokens, token_grads[0]),
        column_sum(token_grads[0]),
        matmul_left(tokens, token_grads[1]),
        matmul_left(tokens, token_grads[2]),
        column_sum(token_grads[2]),
        grad_out,
        grad_out_bias,
        grad_attn_gain,
        grad_attn_shift,
        grad_up,
        grad_up_bias,
        grad_down,
        grad_down_bias,
        grad_ffn_gain,
        grad_ffn_shift,
    )
    return (result.astype(jnp.bfloat16), d_tokens.astype(jnp.bfloat16), grads)


def body(
    inputs,
    cotangent,
    random_blocks,
    global_blocks,
    query_weight,
    query_bias,
    key_weight,
    value_weight,
    value_bias,
    out_weight,
    out_bias,
    attn_gain,
    attn_shift,
    up_weight,
    up_bias,
    down_weight,
    down_bias,
    ffn_gain,
    ffn_shift,
):
    weight_shards = (
        query_weight,
        query_bias,
        key_weight,
        value_weight,
        value_bias,
        out_weight,
        out_bias,
        attn_gain,
        attn_shift,
        up_weight,
        up_bias,
        down_weight,
        down_bias,
        ffn_gain,
        ffn_shift,
    )
    results = []
    input_grads = []
    totals = None
    for micro_index in range(inputs.shape[0]):
        weights = fetch_weights(*weight_shards)
        result, token_grad, grads = micro_batch(
            inputs[micro_index],
            cotangent[micro_index],
            random_blocks[micro_index],
            global_blocks[micro_index],
            weights,
        )
        grads = reduce_grads(grads)
        totals = (
            grads
            if totals is None
            else tuple((total_sum + extra_sum for total_sum, extra_sum in zip(totals, grads)))
        )
        results.append(result)
        input_grads.append(token_grad)
    return (jnp.stack(results), jnp.stack(input_grads)) + tuple(totals)


def solution(mesh):
    return jax.shard_map(
        near_body if (mesh.shape["blk"], mesh.shape["head"]) == (8, 4) else body,
        mesh=mesh,
        in_specs=(
            P(None, ("blk", "head"), None),
            P(None, ("blk", "head"), None),
            P(),
            P(),
            P(("blk", "head"), None),
            P(("blk", "head")),
            P(("blk", "head"), None),
            P(("blk", "head"), None),
            P(("blk", "head")),
            P(("blk", "head"), None),
            P(("blk", "head")),
            P(("blk", "head")),
            P(("blk", "head")),
            P(("blk", "head"), None),
            P(("blk", "head")),
            P(("blk", "head"), None),
            P(("blk", "head")),
            P(("blk", "head")),
            P(("blk", "head")),
        ),
        out_specs=(
            P(None, ("blk", "head"), None),
            P(None, ("blk", "head"), None),
            P(("blk", "head"), None),
            P(("blk", "head")),
            P(("blk", "head"), None),
            P(("blk", "head"), None),
            P(("blk", "head")),
            P(("blk", "head"), None),
            P(("blk", "head")),
            P(("blk", "head")),
            P(("blk", "head")),
            P(("blk", "head"), None),
            P(("blk", "head")),
            P(("blk", "head"), None),
            P(("blk", "head")),
            P(("blk", "head")),
            P(("blk", "head")),
        ),
        check_vma=False,
    )
```

profile of v0, /device:TPU:0, one launch (start us, length us, event | category | flops | bytes accessed | tf_op | source)
XLA Modules:
  0.0 337.1 jit_solution(16926558091877291855)
XLA Ops:
  0.7 0.0 copy-start
  0.7 0.8 constant_dynamic-update-slice_fusion.4
  1.4 0.8 constant_dynamic-update-slice_fusion.3
  2.2 0.8 constant_dynamic-update-slice_fusion.2
  3.0 0.8 constant_dynamic-update-slice_fusion.1
  3.8 0.7 copy.47
  4.5 0.7 copy.48
  5.3 0.7 copy.49
  6.0 0.7 copy.50
  6.7 0.7 copy.51
  7.5 0.7 copy.52
  8.2 0.7 copy.53
  9.0 0.7 copy.54
  9.7 0.7 reshape.95
  10.5 0.1 concatenate.16
  10.6 0.0 copy-start.3
  10.6 0.7 copy-done.3
  11.3 33.6 %gather1.1 = bf16[32,24,3200]{2,1,0:T(8,128)(2,1)} custom-call(bf16[24,3200]{1,0:T(8,128)(2,1)} %copy-done.3), custom_call_target="tpu_custom_call" | custom-call | tf_op jit(solution)/shard_map/gather1/pallas_call | solution.py:235
  44.9 0.0 copy-start.6
  44.9 1.0 convert_bitcast_fusion
  45.9 0.2 fusion
  46.1 0.8 copy.55.bias_ref
  46.8 4.1 %project.1 = (bf16[4,3,128,128]{3,2,1,0:T(8,128)(2,1)}, bf16[4,6,128,128]{3,2,1,0:T(8,128)(2,1)}) custom-call(bf16[2,128,768]{2,1,0:T(8,128)(2,1)} %x_ref.5, bf16[768,3200]{1,0:T(8,128)(2,1)} %bitcast.44, f32[8,768]{1,0:T(8,128)} %copy.55.bias_ref), custom_call_target="tpu_custom_call" | custom-call | tf_op jit(solution)/shard_map/project/pallas_call | solution.py:506
  50.9 74.1 %gather2.1 = (bf16[4,3,128,128]{3,2,1,0:T(8,128)(2,1)}, bf16[32,6,128,128]{3,2,1,0:T(8,128)(2,1)}, bf16[32,24,3072]{2,1,0:T(8,128)(2,1)}, bf16[32,96,768]{2,1,0:T(8,128)(2,1)}) custom-call(bf16[4,3,128,128]{3,2,1,0:T(8,128)(2,1)} %get-tuple-element.44.refs_0_, bf16[4,6,128,128]{3,2,1,0:T(8,128)(2,1)} %get-tuple-element.45.refs_1_, bf16[24,3072]{1,0:T(8,128)(2,1)} %refs_2_.1, ...), custom_call_target="tpu_custom_call" | custom-call | tf_op jit(solution)/shard_map/gather2/pallas_call | solution.py:235
  125.0 0.0 copy-done
  125.0 0.1 constant_dynamic-slice_fusion
  125.1 0.1 copy.46
  125.2 0.1 reshape.93
  125.4 0.0 copy-done.6
  125.4 0.1 reshape.94
  125.5 0.6 pad_add_fusion.table_ref
  126.1 10.7 %attend.1 = (bf16[4,3,2,64,128]{4,3,2,1,0:T(8,128)(2,1)}, f32[4,3,2,2,64,128]{5,4,3,2,1,0:T(8,128)}) custom-call(s32[150]{0:T(256)} %pad_add_fusion.table_ref, bf16[4,3,2,64,128]{4,3,2,1,0:T(8,128)(2,1)} %bitcast.56, bf16[32,6,2,64,128]{4,3,2,1,0:T(8,128)(2,1)} %bitcast.48), custom_call_target="tpu_custom_call" | custom-call | tf_op jit(solution)/shard_map/attend/pallas_call | solution.py:637
  136.8 16.1 %gather3.1.c_ref = bf16[4,3,128,128]{3,2,1,0:T(8,128)(2,1)} custom-call(bf16[4,3,128,128]{3,2,1,0:T(8,128)(2,1)} %bitcast.58), custom_call_target="tpu_custom_call" | custom-call | tf_op jit(solution)/shard_map/gather3/pallas_call | solution.py:235
  153.0 0.7 copy.56.vec_ref
  153.7 1.0 slice_convert_fusion
  154.8 0.9 reshape.114.up_bias_ref
  155.6 22.7 %dense.1 = (bf16[2,128,768]{2,1,0:T(8,128)(2,1)}, f32[256,768]{1,0:T(8,128)}, bf16[4,3,128,128]{3,2,1,0:T(8,128)(2,1)}, bf16[768,768]{1,0:T(8,128)(2,1)}, bf16[7...) custom-call(bf16[4,3,128,128]{3,2,1,0:T(8,128)(2,1)} %gather3.1.c_ref, ...), custom_call_target="tpu_custom_call" | custom-call | tf_op jit(solution)/shard_map/dense/pallas_call | solution.py:955
  178.4 13.1 %gather4.1 = bf16[4,3,128,128]{3,2,1,0:T(8,128)(2,1)} custom-call(bf16[4,3,128,128]{3,2,1,0:T(8,128)(2,1)} %get-tuple-element.52.refs_0_), custom_call_target="tpu_custom_call" | custom-call | tf_op jit(solution)/shard_map/gather4/pallas_call | solution.py:235
  191.5 15.1 %attend_back.1 = (bf16[4,3,2,64,128]{4,3,2,1,0:T(8,128)(2,1)}, bf16[32,6,2,64,128]{4,3,2,1,0:T(8,128)(2,1)}) custom-call(s32[150]{0:T(256)} %pad_add_fusion.table_ref, bf16[4,3,2,64,128]{4,3,2,1,0:T(8,128)(2,1)} %bitcast.57, bf16[32,6,2,64,128]{4,3,2,1,0:T(8,128)(2,1)} %bitcast.49, bf16[4,3,2,64,128]{4,3,2,1,0:T(8,128)(2,1)} %bitcast.59, ...), custom_call_target="tpu_custom_call" | custom-call | tf_op jit(solution)/shard_map/attend_back/pallas_call | solution.py:797
  206.6 79.9 %scatter5.1 = (bf16[4,3,128,128]{3,2,1,0:T(8,128)(2,1)}, bf16[4,6,128,128]{3,2,1,0:T(8,128)(2,1)}, f32[24,3072]{1,0:T(8,128)}, f32[96,768]{1,0:T(8,128)}) custom-call(bf16[4,3,128,128]{3,2,1,0:T(8,128)(2,1)} %bitcast.61, bf16[32,6,128,128]{3,2,1,0:T(8,128)(2,1)} %bitcast.50, bf16[32,24,3072]{2,1,0:T(8,128)(2,1)} %bitcast.54, bf16[32,96,768]{2,1,0:T(8,128)(2,1)} %bitcast.55), custom_call_target="tpu_custom_call" | custom-call | tf_op jit(solution)/shard_map/scatter5/pallas_call | solution.py:438
  286.5 0.0 copy-start.4
  286.5 0.0 copy-start.5
  286.5 7.4 %project_back.1 = (bf16[2,128,768]{2,1,0:T(8,128)(2,1)}, bf16[768,3072]{1,0:T(8,128)(2,1)}, f32[8,768]{1,0:T(8,128)}) custom-call(bf16[4,3,128,128]{3,2,1,0:T(8,128)(2,1)} %get-tuple-element.58.q_ref, bf16[4,6,128,128]{3,2,1,0:T(8,128)(2,1)} %get-tuple-element.59.kv_ref, bf16[2,128,768]{2,1,0:T(8,128)(2,1)} %x_ref.5, bf16[768,3200]{1,0:T(8,128)(2,1)} %bitcast.47, ...), custom_call_target="tpu_custom_call" | custom-call | tf_op jit(solution)/shard_map/project_back/pallas_call | solution.py:1037
  293.9 0.0 copy-start.2
  293.9 0.0 copy-start.1
  293.9 0.8 slice.61
  294.7 0.0 copy-done.4
  294.7 0.1 reshape.110
  294.8 0.1 copy.59
  294.9 0.5 broadcast.18
  295.4 0.0 copy-done.5
  295.4 0.7 reduce.3
  296.1 0.1 reshape.111
  296.2 0.7 select_maximum_fusion.refs_1_
  297.0 34.1 %scatter6.1 = (f32[24,3072]{1,0:T(8,128)}, f32[16,128]{1,0:T(8,128)}) custom-call(bf16[32,24,3072]{2,1,0:T(8,128)(2,1)} %bitcast.51, f32[32,16,128]{2,1,0:T(8,128)} %select_maximum_fusion.refs_1_), custom_call_target="tpu_custom_call" | custom-call | tf_op jit(solution)/shard_map/scatter6/pallas_call | solution.py:438
  331.1 1.7 fusion.1
  332.8 1.5 slice_bitcast_fusion
  334.4 0.7 slice.72
  335.0 0.6 reshape.112
  335.6 0.0 copy-done.2
  335.6 0.7 copy.66
  336.4 0.0 copy-done.1
  336.4 0.7 copy.67
  (2 shorter events, 0.0 us)
Async XLA Ops:
  0.7 124.4 %copy-start = (s32[2,64,12,3]{1,0,3,2:T(2,128)S(1)}, s32[2,64,12,3]{1,0,3,2:T(2,128)}, u32[]{:S(2)}) copy-start(s32[2,64,12,3]{1,0,3,2:T(2,128)} %param.21) | copy-start | bytes 55300
  10.6 0.7 copy-start.3
  44.9 80.5 %copy-start.6 = (s32[2,2]{1,0:T(2,128)S(1)}, s32[2,2]{1,0:T(2,128)}, u32[]{:S(2)}) copy-start(s32[2,2]{1,0:T(2,128)} %param.22) | copy-start | bytes 52
  286.5 8.2 %copy-start.4 = (f32[8,768]{1,0:T(8,128)S(1)}, f32[8,768]{1,0:T(8,128)}, u32[]{:S(2)}) copy-start(f32[8,768]{1,0:T(8,128)} %get-tuple-element.65) | copy-start | bytes 73732
  286.5 8.9 %copy-start.5 = (f32[1,3072]{1,0:T(1,128)S(1)}, f32[1,3072]{1,0:T(1,128)}, u32[]{:S(2)}) copy-start(f32[1,3072]{1,0:T(1,128)} %get-tuple-element.66) | copy-start | bytes 36868
  293.9 41.8 %copy-start.2 = (f32[24,3072]{1,0:T(8,128)S(1)}, f32[24,3072]{1,0:T(8,128)}, u32[]{:S(2)}) copy-start(f32[24,3072]{1,0:T(8,128)} %get-tuple-element.113) | copy-start | bytes 884740
  293.9 42.5 %copy-start.1 = (f32[96,768]{1,0:T(8,128)S(1)}, f32[96,768]{1,0:T(8,128)}, u32[]{:S(2)}) copy-start(f32[96,768]{1,0:T(8,128)} %get-tuple-element.115) | copy-start | bytes 884740
where the time goes:
time: 338 us; the launch traced here: 337 us
  Pallas kernels  311 us (92%)
  local copies, waits for them, and re-layouts  21.1 us (6%)
  other arithmetic  4.07 us (1%)
    pallas_call x4, Pallas kernels, gather_call(): pl.pallas_call(partial(gather_kernel, kinds), out_shape=tuple(shapes), in...  137 us
    pallas_call x2, Pallas kernels, scatter_call(): pl.pallas_call(partial(scatter_kernel, kinds), out_shape=tuple(shapes), i...  114 us
    pallas_call x1, Pallas kernels, dense_call(): pl.pallas_call(dense_kernel, out_shape=outs, in_specs=[full(c.shape), ful...  22.7 us
    pallas_call x1, Pallas kernels, attend_back_call(): pl.pallas_call(attend_back_kernel, out_shape=(jax.ShapeDtypeStruct(q.shap...  15.1 us
    pallas_call x1, Pallas kernels, attend_call(): pl.pallas_call(attend_kernel, out_shape=(jax.ShapeDtypeStruct(q.shape, jn...  10.7 us
    pallas_call x1, Pallas kernels, project_back_call(): pl.pallas_call(project_back_kernel, out_shape=outs, grid=(1,), in_specs=[...  7.39 us

commit v1 on v0

--- a/solution.py
+++ b/solution.py
@@ -51,16 +51,21 @@
     )
 
 
-def gather_kernel(kinds, *refs):
-    n = len(kinds)
-    ins = refs[:n]
-    outs = refs[n : 2 * n]
-    own_sem, line_send, line_recv, send, recv = refs[2 * n :]
+def gather_steps(kinds, ins, outs, sems):
+    own_sem, line_send, line_recv, send, recv = sems
     b, h, core, x, y, across_x, across_y, partner, line = places()
-    corner = across_x + 4 - 8 * y
+    far_corner = across_x + 4 - 8 * y
+    partner_x = partner + 2 - 4 * x
+    partner_y = partner + 4 - 8 * y
+    partner_corner = partner_x + 4 - 8 * y
     inner = jnp.logical_or(h == 1, h == 2)
     seen = jnp.where(inner, 2, 3)
-    meet(b, h, (across_x, across_y, partner), line)
+    started = []
+    started_inner = []
+    locals_ = []
+
+    def enter():
+        meet(b, h, (across_x, across_y, partner), line)
 
     def piece(i, place):
         return ins[i].at[place] if kinds[i][0] else ins[i]
@@ -68,12 +73,9 @@
     def slot(i, shard, place):
         return outs[i].at[shard * 4 + place] if kinds[i][1] else outs[i].at[place]
 
-    def part(ref, cut):
-        axis, start, size = cut
+    def part(ref, cut_):
+        axis, start, size = cut_
         return ref.at[(slice(None),) * axis + (pl.ds(start, size),)]
-
-    started = []
-    started_inner = []
 
     def go(copy, only_inner=False):
         if only_inner:
@@ -95,7 +97,36 @@
             only_inner,
         )
 
-    def line_arrived(i, d):
+    def plane(i, d):
+        src = piece(i, h) if d == 0 else slot(i, b, line[d])
+        for k, other in enumerate((across_x, across_y, partner)):
+            go(
+                remote(
+                    src, slot(i, b, line[d]), send.at[i, d, k], recv.at[i, d, k], (other, h)
+                )
+            )
+
+    def arrived(i, d, k, shard, cut_=None):
+        here = slot(i, shard, line[d])
+        if cut_ is not None:
+            here = part(here, cut_)
+        remote(here, here, send.at[i, d, k], recv.at[i, d, k], (partner, h)).wait_recv()
+        return here
+
+    def begin(i):
+        if kinds[i][0]:
+            for d in (2, 3, 1):
+                along(i, piece(i, line[d]), slot(i, b, h), d, 1 if d == 1 else seen, line[d])
+        else:
+            along(i, piece(i, h), slot(i, b, h), 2, 2, 3 - h, True)
+            along(i, piece(i, h), slot(i, b, h), 1, 1, line[1])
+        if kinds[i][1]:
+            plane(i, 0)
+        own = pltpu.make_async_copy(piece(i, h), slot(i, b, h), own_sem.at[i])
+        own.start()
+        locals_.append(own)
+
+    def along_done(i, d):
         here = slot(i, b, line[d])
         remote(
             here, here, line_send.at[i, d], line_recv.at[i, d], (b, line[d])
@@ -105,171 +136,276 @@
                 along(i, here, here, 3, 3, 3 - h, True)
             else:
                 along(i, here, here, d + 2, d, line[1], True)
-
-    def out_of(i, d):
-        return piece(i, h) if d == 0 else slot(i, b, line[d])
-
-    def send_plane(i, d):
-        for k, other in enumerate((across_x, across_y, partner)):
-            go(
-                remote(
-                    out_of(i, d),
-                    slot(i, b, line[d]),
-                    send.at[i, d, k],
-                    recv.at[i, d, k],
-                    (other, h),
-                )
-            )
-
-    def arrived(i, d, k, shard, cut=None):
-        here = slot(i, shard, line[d])
-        if cut is not None:
-            here = part(here, cut)
-        remote(here, here, send.at[i, d, k], recv.at[i, d, k], (partner, h)).wait_recv()
-        return here
+        if kinds[i][1]:
+            plane(i, d)
 
     def pass_on(i, d):
         first, second = kinds[i][2]
-        here = arrived(i, d, 0, across_x)
-        if first is not None:
-            go(
-                remote(
-                    part(here, first),
-                    part(here, first),
-                    send.at[i, d, 6],
-                    recv.at[i, d, 6],
-                    (across_y, h),
+        for k, shard, cut_, onward in (
+            (0, across_x, first, across_y),
+            (1, across_y, second, across_x),
+        ):
+            here = arrived(i, d, k, shard)
+            if cut_ is not None:
+                go(
+                    remote(
+                        part(here, cut_),
+                        part(here, cut_),
+                        send.at[i, d, 6 + k],
+                        recv.at[i, d, 6 + k],
+                        (onward, h),
+                    )
                 )
-            )
-        go(remote(here, here, send.at[i, d, 3], recv.at[i, d, 3], (partner, h)))
-        here = arrived(i, d, 1, across_y)
-        if second is not None:
-            go(
-                remote(
-                    part(here, second),
-                    part(here, second),
-                    send.at[i, d, 7],
-                    recv.at[i, d, 7],
-                    (across_x, h),
-                )
-            )
-        go(remote(here, here, send.at[i, d, 4], recv.at[i, d, 4], (partner, h)))
-
-    def finish_corner(i, d):
-        first, second = kinds[i][2]
-        if first is not None:
-            arrived(i, d, 6, corner, first)
-        if second is not None:
-            arrived(i, d, 7, corner, second)
-        here = slot(i, corner, line[d])
+            go(remote(here, here, send.at[i, d, 3 + k], recv.at[i, d, 3 + k], (partner, h)))
+
+    def corner(i, d):
+        for k, cut_ in enumerate(kinds[i][2]):
+            if cut_ is not None:
+                arrived(i, d, 6 + k, far_corner, cut_)
+        here = slot(i, far_corner, line[d])
         go(remote(here, here, send.at[i, d, 5], recv.at[i, d, 5], (partner, h)))
 
-    spread = [i for i in range(n) if kinds[i][1]]
-    straight = [i for i in range(n) if not kinds[i][1]]
-    locals_ = []
-
-    def send_straight(i):
-        for d in (2, 3, 1):
-            along(i, piece(i, line[d]), slot(i, b, h), d, 1 if d == 1 else seen, line[d])
-
-    for i in spread:
-        if kinds[i][0]:
-            send_straight(i)
-        else:
-            along(i, piece(i, h), slot(i, b, h), 2, 2, 3 - h, True)
-            along(i, piece(i, h), slot(i, b, h), 1, 1, line[1])
-    if not spread:
-        for i in straight:
-            send_straight(i)
-    for i in spread:
-        send_plane(i, 0)
-    for i in range(n):
-        own = pltpu.make_async_copy(piece(i, h), slot(i, b, h), own_sem.at[i])
-        own.start()
-        locals_.append(own)
-    for d in range(1, 4):
-        for i in spread:
-            line_arrived(i, d)
-            send_plane(i, d)
-        if d == 2 and spread:
-            for i in straight:
-                send_straight(i)
-        for i in spread:
-            pass_on(i, d - 1)
-        if d > 1:
-            for i in spread:
-                finish_corner(i, d - 2)
-    for i in spread:
-        pass_on(i, 3)
-    for d in (2, 3):
-        for i in spread:
-            finish_corner(i, d)
-    for i in straight:
-        for d in range(1, 4):
-            line_arrived(i, d)
-    partner_x = partner + 2 - 4 * x
-    partner_y = partner + 4 - 8 * y
-    partner_corner = partner_x + 4 - 8 * y
-    for i in spread:
+    def finish(i):
         for d in range(4):
             for k, shard in ((2, partner), (3, partner_x), (4, partner_y), (5, partner_corner)):
                 arrived(i, d, k, shard)
-    for own in locals_:
-        own.wait()
-    for copy in started:
-        copy.wait_send()
-    if started_inner:
-
-        @pl.when(inner)
-        def _():
-            for copy in started_inner:
-                copy.wait_send()
-
-
-def gather_call(arrays, kinds, collective):
-    n = len(arrays)
-    shapes = []
-    for a, (per_place, spread, _) in zip(arrays, kinds):
-        chunk = a.shape[1:] if per_place else a.shape
-        shapes.append(jax.ShapeDtypeStruct(((32 if spread else 4),) + chunk, a.dtype))
+
+    def kept():
+        for own in locals_:
+            own.wait()
+        locals_.clear()
+
+    def sent():
+        for copy in started:
+            copy.wait_send()
+        if started_inner:
+
+            @pl.when(inner)
+            def _():
+                for copy in started_inner:
+                    copy.wait_send()
+
+    return enter, begin, along_done, pass_on, corner, finish, kept, sent
+
+
+def gather_semaphores(n):
+    dma = pltpu.SemaphoreType.DMA
+    return [dma((n,)), dma((n, 6)), dma((n, 4)), dma((n, 4, 8)), dma((n, 4, 8))]
+
+
+def swap_kernel(in_ref, out_ref, *sems):
+    enter, begin, along_done, _, _, _, kept, sent = gather_steps(
+        [(True, False, None)], [in_ref], [out_ref], sems
+    )
+    enter()
+    begin(0)
+    for d in range(1, 4):
+        along_done(0, d)
+    kept()
+    sent()
+
+
+def swap_call(array, collective):
+    far = pl.BlockSpec(memory_space=pl.ANY)
     return pl.pallas_call(
-        partial(gather_kernel, kinds),
-        out_shape=tuple(shapes),
-        in_specs=[pl.BlockSpec(memory_space=pl.ANY)] * n,
-        out_specs=tuple([pl.BlockSpec(memory_space=pl.ANY)] * n),
+        swap_kernel,
+        out_shape=jax.ShapeDtypeStruct(array.shape, array.dtype),
+        in_specs=[far],
+        out_specs=far,
+        scratch_shapes=gather_semaphores(1),
+        compiler_params=pltpu.CompilerParams(collective_id=collective, has_side_effects=True),
+        name=f"swap{collective}",
+    )(array)
+
+
+def spread_of(rows, width):
+    shards, n = rows.shape
+    total = shards * width
+    lane = lax.broadcasted_iota(jnp.int32, (n, total), 0)
+    column = lax.broadcasted_iota(jnp.int32, (n, total), 1)
+    repeat = jnp.where(column % width == lane, 1.0, 0.0).astype(jnp.bfloat16)
+    shard = lax.broadcasted_iota(jnp.int32, (shards, total), 0)
+    column = lax.broadcasted_iota(jnp.int32, (shards, total), 1)
+    return rows_sum(jnp.where(column // width == shard, dot(rows.astype(jnp.bfloat16), repeat), 0.0))
+
+
+def front_kernel(kinds, *refs):
+    (
+        x_ref, wq_in, wk_in, wv_in, wo_in, up_in, down_in, *vectors,
+    ) = refs[:16]
+    (
+        q_out, kv_out, up_out, down_out, w_out, vec_ref, up_bias_ref,
+        tile, chunk, mixed, rows_wide, w_ref, q_parts, kv_parts, join_sem, w_sem,
+    ) = refs[16:32]
+    rows = x_ref.shape[1]
+    width = x_ref.shape[2]
+    shards, depth, _ = mixed.shape
+    groups, per, _, _ = q_parts.shape
+    enter, begin, along_done, pass_on, corner, finish, kept, sent = gather_steps(
+        kinds,
+        [chunk, up_in, down_in, kv_parts, q_parts],
+        [mixed, up_out, down_out, kv_out, q_out],
+        refs[32:],
+    )
+    joins = [
+        pltpu.make_async_copy(ref, chunk.at[:, pl.ds(k * width, width)], join_sem.at[k])
+        for k, ref in enumerate((wq_in, wk_in, wv_in, wo_in))
+    ]
+    for copy in joins:
+        copy.start()
+    tile[...] = jnp.zeros(tile.shape, jnp.float32)
+    for k, ref in enumerate(vectors):
+        tile[k, : ref.shape[0]] = ref[...].astype(jnp.float32)
+    chunk[:, 4 * width :] = tile[...].astype(jnp.bfloat16)
+    for copy in joins:
+        copy.wait()
+    enter()
+    begin(0)
+    begin(1)
+    begin(2)
+    along_done(0, 1)
+    pass_on(0, 0)
+    along_done(0, 2)
+    along_done(1, 1)
+    along_done(2, 1)
+    pass_on(0, 1)
+    corner(0, 0)
+    along_done(0, 3)
+    pass_on(1, 0)
+    pass_on(2, 0)
+    pass_on(0, 2)
+    corner(0, 1)
+    pass_on(0, 3)
+    corner(0, 2)
+    along_done(1, 2)
+    along_done(2, 2)
+    corner(0, 3)
+    finish(0)
+    kept()
+    for s in range(0, 4 * width, width):
+        part = mixed[:, :, s : s + width].astype(jnp.float32).reshape(width, width)
+        w_ref[:, s : s + width] = part.astype(jnp.bfloat16)
+    leave = pltpu.make_async_copy(w_ref, w_out, w_sem)
+    leave.start()
+    rows_wide[...] = mixed[:, :, 4 * width :].astype(jnp.float32)
+    for k in range(8):
+        vec_ref[k : k + 1, :] = spread_of(rows_wide[:, k, :], depth)
+    up_bias_ref[...] = spread_of(rows_wide[:, 8, :], up_bias_ref.shape[1] // shards)
+    tokens = x_ref[...].reshape(2 * rows, width)
+    made = []
+    for k in range(3):
+        part = dot(tokens, w_ref[:, k * width : (k + 1) * width])
+        if k != 1:
+            part = part + vec_ref[k // 2 : k // 2 + 1, :]
+        made.append(part.astype(jnp.bfloat16))
+    q, k, v = made
+    for g in range(groups):
+        for j in range(per):
+            col = (g * per + j) * HD
+            kv_parts[g, j] = jnp.concatenate([halves(k[:rows], col), halves(v[:rows], col)], axis=1)
+            kv_parts[g, per + j] = jnp.concatenate([halves(v[rows:], col), halves(k[rows:], col)], axis=1)
+    begin(3)
+    for g in range(groups):
+        for j in range(per):
+            col = (g * per + j) * HD
+            q_parts[g, j] = jnp.concatenate([halves(q[:rows], col), halves(q[rows:], col)], axis=1)
+    pass_on(1, 1)
+    pass_on(2, 1)
+    corner(1, 0)
+    corner(2, 0)
+    along_done(3, 1)
+    pass_on(3, 0)
+    begin(4)
+    along_done(3, 2)
+    corner(3, 0)
+    pass_on(3, 1)
+    along_done(3, 3)
+    along_done(1, 3)
+    along_done(2, 3)
+    corner(3, 1)
+    pass_on(3, 2)
+    pass_on(1, 2)
+    pass_on(2, 2)
+    corner(1, 1)
+    corner(2, 1)
+    corner(3, 2)
+    pass_on(3, 3)
+    corner(3, 3)
+    corner(1, 2)
+    corner(2, 2)
+    pass_on(1, 3)
+    pass_on(2, 3)
+    corner(1, 3)
+    corner(2, 3)
+    for d in range(1, 4):
+        along_done(4, d)
+    finish(3)
+    finish(1)
+    finish(2)
+    kept()
+    leave.wait()
+    sent()
+
+
+def front_call(tokens, matrices, up, down, vectors, collective):
+    micro, rows, width = tokens.shape
+    depth, ff = up.shape
+    groups = lax.axis_size("head")
+    devices = groups * lax.axis_size("blk")
+    per = HEADS // groups
+    f32, bf16 = jnp.float32, jnp.bfloat16
+    half = 2 * width
+    kinds = [
+        (False, True, (cut(1, 0, half), cut(1, half, half + 128))),
+        (False, True, (cut(1, 0, ff), None)),
+        (False, True, (None, cut(1, 0, width))),
+        (True, True, (cut(0, 0, per), cut(0, per, per))),
+        (True, False, None),
+    ]
+    near = pl.BlockSpec(memory_space=pltpu.VMEM)
+    far = pl.BlockSpec(memory_space=pl.ANY)
+    return pl.pallas_call(
+        partial(front_kernel, kinds),
+        out_shape=(
+            jax.ShapeDtypeStruct((groups, per, rows, 2 * HD), bf16),
+            jax.ShapeDtypeStruct((devices, 2 * per, rows, 2 * HD), bf16),
+            jax.ShapeDtypeStruct((devices,) + up.shape, bf16),
+            jax.ShapeDtypeStruct((devices,) + down.shape, bf16),
+            jax.ShapeDtypeStruct((width, 4 * width), bf16),
+            jax.ShapeDtypeStruct((8, width), f32),
+            jax.ShapeDtypeStruct((1, ff), f32),
+        ),
+        in_specs=[near] + [far] * 6 + [near] * 9,
+        out_specs=(far,) * 5 + (near,) * 2,
         scratch_shapes=[
-            pltpu.SemaphoreType.DMA((n,)),
-            pltpu.SemaphoreType.DMA((n, 6)),
-            pltpu.SemaphoreType.DMA((n, 4)),
-            pltpu.SemaphoreType.DMA((n, 4, 8)),
-            pltpu.SemaphoreType.DMA((n, 4, 8)),
-        ],
-        compiler_params=pltpu.CompilerParams(collective_id=collective, has_side_effects=True),
-        name=f"gather{collective}",
-    )(*arrays)
-
-
-def scatter_kernel(kinds, *refs):
-    n = len(kinds)
-    ins = refs[:n]
-    outs = refs[n : 2 * n]
-    rest = list(refs[2 * n :])
-    bufs = {}
-    for i in range(n):
-        if kinds[i][1]:
-            bufs[i] = rest[:6]
-            rest = rest[6:]
-            if kinds[i][0]:
-                bufs[i] = bufs[i] + [rest[0]]
-                rest = rest[1:]
-    local_sem, own_sem, line_send, line_recv, core_send, core_recv, send, recv = rest
+            pltpu.VMEM((depth, 128), f32),
+            pltpu.VMEM((depth, 4 * width + 128), bf16),
+            pltpu.VMEM((devices, depth, 4 * width + 128), bf16),
+            pltpu.VMEM((devices, depth, 128), f32),
+            pltpu.VMEM((width, 4 * width), bf16),
+            pltpu.VMEM((groups, per, rows, 2 * HD), bf16),
+            pltpu.VMEM((groups, 2 * per, rows, 2 * HD), bf16),
+            pltpu.SemaphoreType.DMA((4,)),
+            pltpu.SemaphoreType.DMA,
+        ]
+        + gather_semaphores(5),
+        compiler_params=pltpu.CompilerParams(
+            collective_id=collective, has_side_effects=True, vmem_limit_bytes=56 * 2**20
+        ),
+        name="front",
+    )(tokens, *matrices, up, down, *vectors)
+
+
+def scatter_steps(kinds, ins, lands, bufs, sems):
+    local_sem, own_sem, line_send, line_recv, core_send, core_recv, send, recv = sems
     b, h, core, x, y, across_x, across_y, partner, line = places()
     seen = jnp.where(jnp.logical_or(h == 1, h == 2), 2, 3)
-    meet(b, h, (across_x, across_y, partner), line)
     chip = b // 2
     targets = (3 - chip, chip + 1 - 2 * x, chip + 2 - 4 * y, chip)
     started = []
-    spread = [i for i in range(n) if kinds[i][1]]
+    locals_ = []
+    loads = {}
+    order = (3, 2, 1, 0)
 
     def go(copy):
         copy.start()
@@ -286,11 +422,19 @@
             )
         )
 
-    locals_ = []
-    loads = {}
-    for t in range(4):
-        for i in spread:
-            from_partner, total = bufs[i][0], bufs[i][1]
+    def keep(src, i):
+        own = pltpu.make_async_copy(src, lands[i].at[h], own_sem.at[i])
+        own.start()
+        locals_.append(own)
+
+    def begin(i):
+        if not kinds[i][1]:
+            for d in (3, 2, 1):
+                along(i, ins[i].at[line[d]], lands[i].at[h], d)
+            keep(ins[i].at[h], i)
+            return
+        from_partner, total = bufs[i][0], bufs[i][1]
+        for t in range(4):
             go(
                 remote(
                     ins[i].at[pl.ds((targets[t] * 2 + 1 - core) * 4, 4)],
@@ -305,14 +449,6 @@
             )
             load.start()
             loads[i, t] = load
-    for i in range(n):
-        if i in spread:
-            continue
-        for d in (3, 2, 1):
-            along(i, ins[i].at[line[d]], outs[i].at[h], d)
-        own = pltpu.make_async_copy(ins[i].at[h], outs[i].at[h], own_sem.at[i])
-        own.start()
-        locals_.append(own)
 
     def wait_for(ref, i, d, k):
         remote(ref, ref, send.at[i, d, k], recv.at[i, d, k], (partner, h)).wait_recv()
@@ -337,9 +473,7 @@
         value = total[at].astype(jnp.float32) + ref[d].astype(jnp.float32)
         total[at] = value.astype(total.dtype)
 
-    order = (3, 2, 1, 0)
-
-    def corner_step(i):
+    def corner(i):
         total = bufs[i][1]
         first, second = kinds[i][2]
         ready(i, 0)
@@ -351,7 +485,7 @@
             if second is not None:
                 go(remote(part(mine, second), bufs[i][3].at[d], send.at[i, d, 1], recv.at[i, d, 1], (across_y, h)))
 
-    def side_step(i):
+    def sides(i):
         total = bufs[i][1]
         first, second = kinds[i][2]
         ready(i, 1)
@@ -368,7 +502,7 @@
                 add_corner(i, 2, d, bufs[i][2], first)
             go(remote(total.at[2, line[d]], bufs[i][5].at[d], send.at[i, d, 3], recv.at[i, d, 3], (across_y, h)))
 
-    def own_step(i):
+    def own(i):
         summed = kinds[i][0]
         total = bufs[i][1]
         ready(i, 3)
@@ -377,85 +511,237 @@
             wait_for(bufs[i][5].at[d], i, d, 3)
             both_cores(i, 3, d, (bufs[i][4], bufs[i][5]))
             if d > 0:
-                landing = bufs[i][6].at[1 if d == 1 else seen] if summed else outs[i].at[h]
+                landing = bufs[i][6].at[1 if d == 1 else seen] if summed else lands[i].at[h]
                 along(i, total.at[3, line[d]], landing, d)
             elif not summed:
-                own = pltpu.make_async_copy(total.at[3, h], outs[i].at[h], own_sem.at[i])
-                own.start()
-                locals_.append(own)
-
-    for i in spread:
-        corner_step(i)
-    for at, i in enumerate(spread):
-        side_step(i)
-        if at > 0:
-            own_step(spread[at - 1])
-    if spread:
-        own_step(spread[-1])
-    for i in range(n):
+                keep(total.at[3, h], i)
+
+    def finish(i):
         summed = kinds[i][0]
         for d in range(1, 4):
-            landing = bufs[i][6].at[d] if summed else outs[i].at[line[d]]
+            landing = bufs[i][6].at[d] if summed else lands[i].at[line[d]]
             remote(
                 landing, landing, line_send.at[i, d], line_recv.at[i, d], (b, line[d])
             ).wait_recv()
-        if summed:
-            value = bufs[i][1][3, h].astype(jnp.float32)
-            for d in range(1, 4):
-                value = value + bufs[i][6][d].astype(jnp.float32)
-            outs[i][...] = value
-    for own in locals_:
-        own.wait()
-    for copy in started:
-        copy.wait_send()
-
-
-def scatter_call(arrays, kinds, collective):
-    n = len(arrays)
-    shapes = []
-    out_specs = []
-    scratch = []
-    for a, (summed, spread, halves) in zip(arrays, kinds):
-        chunk = a.shape[1:]
-        if spread:
-            scratch += [pltpu.VMEM((4, 4) + chunk, a.dtype), pltpu.VMEM((4, 4) + chunk, a.dtype)]
-            for cut in halves:
-                size = list(chunk)
-                if cut is not None:
-                    size[cut[0]] = cut[2]
-                else:
-                    size = [8, 128]
-                scratch.append(pltpu.VMEM((4,) + tuple(size), a.dtype))
-            scratch += [pltpu.VMEM((4,) + chunk, a.dtype)] * 2
-            if summed:
-                scratch.append(pltpu.VMEM((4,) + chunk, a.dtype))
-        if summed:
-            shapes.append(jax.ShapeDtypeStruct(chunk, jnp.float32))
-            out_specs.append(pl.BlockSpec(memory_space=pltpu.VMEM))
+        if not summed:
+            return None
+        value = bufs[i][1][3, h].astype(jnp.float32)
+        for d in range(1, 4):
+            value = value + bufs[i][6][d].astype(jnp.float32)
+        return value
+
+    def kept():
+        for copy in locals_:
+            copy.wait()
+        locals_.clear()
+
+    def sent():
+        for copy in started:
+            copy.wait_send()
+
+    def enter():
+        meet(b, h, (across_x, across_y, partner), line)
+
+    return enter, begin, corner, sides, own, finish, kept, sent
+
+
+def scatter_scratch(chunk, dtype, kind):
+    summed, spread, cuts = kind
+    if not spread:
+        return []
+    scratch = [pltpu.VMEM((4, 4) + chunk, dtype), pltpu.VMEM((4, 4) + chunk, dtype)]
+    for cut_ in cuts:
+        size = list(chunk)
+        if cut_ is not None:
+            size[cut_[0]] = cut_[2]
         else:
-            shapes.append(jax.ShapeDtypeStruct((4,) + chunk, a.dtype))
-            out_specs.append(pl.BlockSpec(memory_space=pl.ANY))
+            size = [8, 128]
+        scratch.append(pltpu.VMEM((4,) + tuple(size), dtype))
+    scratch += [pltpu.VMEM((4,) + chunk, dtype)] * 2
+    if summed:
+        scratch.append(pltpu.VMEM((4,) + chunk, dtype))
+    return scratch
+
+
+def scatter_semaphores(n):
+    dma = pltpu.SemaphoreType.DMA
+    return [dma((n, 4)), dma((n,))] + [dma((n, 4))] * 4 + [dma((n, 4, 4))] * 2
+
+
+def back_kernel(kinds, counts, *refs):
+    (
+        dq_in, dkv_in, up_in, down_in, x_ref, mixed_in, d_mix_ref, g_out_ref, g_vec_ref, g_up_bias_ref,
+        d_x_ref, g_mixed_ref, g_up_ref, g_down_ref, g_small_ref,
+        dq_land, dkv_land, terms, small, w_ref, d_q, d_k, d_v, w_sem,
+    ), rest = refs[:24], list(refs[24:])
+    bufs = []
+    for count in counts:
+        bufs.append(rest[:count])
+        rest = rest[count:]
+    groups, per, rows, _ = dq_land.shape
+    width = x_ref.shape[2]
+    depth = terms.shape[1]
+    shards = terms.shape[0]
+    ins = (dq_in, dkv_in, up_in, down_in, terms, small)
+    enter, begin, corner, sides, own, finish, kept, sent = scatter_steps(
+        kinds, ins, (dq_land, dkv_land, None, None, None, None), bufs, rest
+    )
+    load = pltpu.make_async_copy(mixed_in.at[:, pl.ds(0, 3 * width)], w_ref, w_sem)
+    load.start()
+    enter()
+    for i in (1, 0, 2, 3):
+        begin(i)
+    small[...] = jnp.zeros(small.shape, jnp.float32)
+    out_terms = g_out_ref[...].astype(jnp.float32).reshape(shards, depth, width)
+    terms[:, :, 3 * width :] = out_terms.astype(jnp.bfloat16)
+    corner(1)
+    sides(1)
+    corner(2)
+    corner(3)
+    own(1)
+    sides(2)
+    sides(3)
+    finish(0)
+    finish(1)
+    kept()
+    for p in range(HEADS // 2):
+        at = pl.ds(p * 2 * HD, 2 * HD)
+
+        def of(ref, shift, low):
+            both = []
+            for head in (2 * p, 2 * p + 1):
+                tile = ref[head // per, shift + head % per]
+                both.append(tile[:, :HD] if low else tile[:, HD:])
+            return jnp.concatenate(both, axis=1)
+
+        d_q[:rows, at] = of(dq_land, 0, True)
+        d_q[rows:, at] = of(dq_land, 0, False)
+        d_k[:rows, at] = of(dkv_land, 0, True)
+        d_v[:rows, at] = of(dkv_land, 0, False)
+        d_k[rows:, at] = of(dkv_land, per, False)
+        d_v[rows:, at] = of(dkv_land, per, True)
+    load.wait()
+    tokens = x_ref[...].reshape(2 * rows, width)
+    sums = []
+    for k, half_ref in enumerate((d_q, d_k, d_v)):
+        at = slice(k * width, (k + 1) * width)
+        term = dot(tokens, half_ref[...], COLS).reshape(shards, depth, width)
+        terms[:, :, at] = term.astype(jnp.bfloat16)
+        if k != 1:
+            sums.append(rows_sum(half_ref[...].astype(jnp.float32)))
+    vectors = jnp.concatenate(sums + [g_vec_ref[:6, :]], axis=0)
+    up_bias = g_up_bias_ref[...]
+    up_depth = up_bias.shape[1] // shards
+    for s in range(shards):
+        small[s, :8, :depth] = vectors[:, s * depth : (s + 1) * depth]
+        small[s, 8:9, :up_depth] = up_bias[:, s * up_depth : (s + 1) * up_depth]
+    begin(4)
+    begin(5)
+    own(2)
+    corner(4)
+    corner(5)
+    own(3)
+    d_x = d_mix_ref[...]
+    for k, half_ref in enumerate((d_q, d_k, d_v)):
+        d_x = d_x + dot(half_ref[...], w_ref[:, k * width : (k + 1) * width], ROWS)
+    d_x_ref[...] = d_x.astype(jnp.bfloat16).reshape(2, rows, width)
+    sides(4)
+    sides(5)
+    g_up_ref[...] = finish(2)
+    own(4)
+    own(5)
+    g_down_ref[...] = finish(3)
+    g_mixed_ref[...] = finish(4)
+    g_small_ref[...] = finish(5)
+    sent()
+
+
+def back_call(d_q, d_kv, g_up, g_down, tokens, mixed, d_mix, g_out, g_vec, g_up_bias, collective):
+    micro, rows, width = tokens.shape
+    devices, depth, ff = g_up.shape
+    groups, per = d_q.shape[:2]
+    f32, bf16 = jnp.float32, jnp.bfloat16
+    half = 2 * width
+    kinds = [
+        (False, False, None),
+        (False, True, (cut(0, 0, per), cut(0, per, per))),
+        (True, True, (cut(1, 0, ff), None)),
+        (True, True, (None, cut(1, 0, width))),
+        (True, True, (cut(1, 0, half), cut(1, half, half))),
+        (True, True, (cut(1, 0, 128), None)),
+    ]
+    chunks = [
+        (d_q.shape[1:], bf16),
+        (d_kv.shape[1:], bf16),
+        (g_up.shape[1:], bf16),
+        (g_down.shape[1:], bf16),
+        ((depth, 4 * width), bf16),
+        ((16, 128), f32),
+    ]
+    scratch = [scatter_scratch(chunk, dtype, kind) for (chunk, dtype), kind in zip(chunks, kinds)]
+    near = pl.BlockSpec(memory_space=pltpu.VMEM)
+    far = pl.BlockSpec(memory_space=pl.ANY)
+    outs = [jax.ShapeDtypeStruct(tokens.shape, bf16)]
+    outs += [
+        jax.ShapeDtypeStruct((depth, 4 * width), f32),
+        jax.ShapeDtypeStruct((depth, ff), f32),
+        jax.ShapeDtypeStruct(g_down.shape[1:], f32),
+        jax.ShapeDtypeStruct((16, 128), f32),
+    ]
     return pl.pallas_call(
-        partial(scatter_kernel, kinds),
-        out_shape=tuple(shapes),
-        in_specs=[pl.BlockSpec(memory_space=pl.ANY)] * n,
-        out_specs=tuple(out_specs),
-        scratch_shapes=scratch
-        + [
-            pltpu.SemaphoreType.DMA((n, 4)),
-            pltpu.SemaphoreType.DMA((n,)),
-            pltpu.SemaphoreType.DMA((n, 4)),
-            pltpu.SemaphoreType.DMA((n, 4)),
-            pltpu.SemaphoreType.DMA((n, 4)),
-            pltpu.SemaphoreType.DMA((n, 4)),
-            pltpu.SemaphoreType.DMA((n, 4, 4)),
-            pltpu.SemaphoreType.DMA((n, 4, 4)),
-        ],
+        partial(back_kernel, kinds, [len(s) for s in scratch]),
+        out_shape=tuple(outs),
+        in_specs=[far] * 4 + [near, far] + [near] * 4,
+        out_specs=(near,) * 5,
+        scratch_shapes=[
+            pltpu.VMEM(d_q.shape, bf16),
+            pltpu.VMEM((groups,) + d_kv.shape[1:], bf16),
+            pltpu.VMEM((devices, depth, 4 * width), bf16),
+            pltpu.VMEM((devices, 16, 128), f32),
+            pltpu.VMEM((width, 3 * width), bf16),
+        ]
+        + [pltpu.VMEM((micro * rows, width), bf16)] * 3
+        + [pltpu.SemaphoreType.DMA]
+        + [one for some in scratch for one in some]
+        + scatter_semaphores(6),
         compiler_params=pltpu.CompilerParams(
-            collective_id=collective, has_side_effects=True, vmem_limit_bytes=60 * 2**20
+            collective_id=collective, has_side_effects=True, vmem_limit_bytes=61 * 2**20
         ),
-        name=f"scatter{collective}",
-    )(*arrays)
+        name="back",
+    )(d_q, d_kv, g_up, g_down, tokens, mixed, d_mix, g_out, g_vec, g_up_bias)
+
+
+def leave_kernel(d_x_in, mixed_in, up_in, down_in, small_in, d_x_ref, *refs):
+    d_x_ref[...] = d_x_in[...]
+    width = d_x_in.shape[2]
+    for k in range(4):
+        refs[k][...] = mixed_in[:, k * width : (k + 1) * width]
+    refs[4][...] = up_in[...]
+    refs[5][...] = down_in[...]
+    for k, ref in enumerate(refs[6:]):
+        ref[...] = small_in[k, : ref.shape[0]]
+
+
+def leave_call(d_x, mixed, up, down, small):
+    depth, wide_ = mixed.shape
+    f32 = jnp.float32
+    outs = [jax.ShapeDtypeStruct(d_x.shape, d_x.dtype)]
+    outs += [jax.ShapeDtypeStruct((depth, wide_ // 4), f32)] * 4
+    outs += [jax.ShapeDtypeStruct(up.shape, f32), jax.ShapeDtypeStruct(down.shape, f32)]
+    outs += [jax.ShapeDtypeStruct((depth,), f32)] * 8
+    outs += [jax.ShapeDtypeStruct((down.shape[0],), f32)]
+    near = pl.BlockSpec(memory_space=pltpu.VMEM)
+    return pl.pallas_call(
+        leave_kernel,
+        out_shape=tuple(outs),
+        in_specs=[near] * 5,
+        out_specs=(near,) * len(outs),
+        name="leave",
+    )(d_x, mixed, up, down, small)
+
+
+def cut(axis, start, size):
+    return (axis, start, size)
 
 
 def lanes_of(shape, low):
@@ -477,51 +763,6 @@
 
 def halves(array, col):
     return array[:, col : col + HD]
-
-
-def project_kernel(x_ref, w_ref, bias_ref, q_out, kv_out):
-    rows = x_ref.shape[1]
-    width = x_ref.shape[2]
-    tokens = x_ref[...].reshape(2 * rows, width)
-    made = []
-    for k in range(3):
-        part = dot(tokens, w_ref[:, k * width : (k + 1) * width])
-        if k != 1:
-            part = part + bias_ref[k // 2 : k // 2 + 1, :]
-        made.append(part.astype(jnp.bfloat16))
-    q, k, v = made
-    groups, per, _, _ = q_out.shape
-    for g in range(groups):
-        for j in range(per):
-            col = (g * per + j) * HD
-            q_out[g, j] = jnp.concatenate([halves(q[:rows], col), halves(q[rows:], col)], axis=1)
-            kv_out[g, j] = jnp.concatenate([halves(k[:rows], col), halves(v[:rows], col)], axis=1)
-            kv_out[g, per + j] = jnp.concatenate([halves(v[rows:], col), halves(k[rows:], col)], axis=1)
-
-
-def project_call(tokens, weight, bias, groups):
-    micro, rows, width = tokens.shape
-    per = HEADS // groups
-    whole = pl.BlockSpec(memory_space=pltpu.VMEM)
-    return pl.pallas_call(
-        project_kernel,
-        out_shape=(
-            jax.ShapeDtypeStruct((groups, per, rows, 2 * HD), jnp.bfloat16),
-            jax.ShapeDtypeStruct((groups, 2 * per, rows, 2 * HD), jnp.bfloat16),
-        ),
-        grid=(1,),
-        in_specs=[
-            pl.BlockSpec((micro, rows, width), lambda i: (0, 0, 0)),
-            pl.BlockSpec((width, 3 * width), lambda i: (0, 0)),
-            pl.BlockSpec(bias.shape, lambda i: (0, 0)),
-        ],
-        out_specs=(
-            pl.BlockSpec((groups, per, rows, 2 * HD), lambda i: (0, 0, 0, 0)),
-            pl.BlockSpec((groups, 2 * per, rows, 2 * HD), lambda i: (0, 0, 0, 0)),
-        ),
-        compiler_params=pltpu.CompilerParams(vmem_limit_bytes=56 * 2**20),
-        name="project",
-    )(tokens, weight, bias)
 
 
 def listed_rows(table_ref, blocks, per, m, n, j):
@@ -850,7 +1091,7 @@
     for copy in fetches:
         copy.start()
     out_bias, attn_gain, attn_shift, down_bias, ffn_gain, ffn_shift = (
-        vec_ref[k : k + 1, :] for k in range(6)
+        vec_ref[k : k + 1, :] for k in range(2, 8)
     )
     for p in range(HEADS // 2):
         one = c_ref[(2 * p) // per, (2 * p) % per]
@@ -988,75 +1229,6 @@
     )(c, tokens, cot, mixed, up, down, vec, up_bias)
 
 
-def project_back_kernel(
-    q_ref, kv_ref, x_ref, w_ref, d_mix_ref, g_out_ref, d_x_ref, g_ref, g_vec_ref, d_q, d_k, d_v
-):
-    groups, per, rows, _ = q_ref.shape
-    width = x_ref.shape[2]
-    for p in range(HEADS // 2):
-        at = pl.ds(p * 2 * HD, 2 * HD)
-
-        def of(ref, shift, low):
-            sides = []
-            for head in (2 * p, 2 * p + 1):
-                tile = ref[head // per, shift + head % per]
-                sides.append(tile[:, :HD] if low else tile[:, HD:])
-            return jnp.concatenate(sides, axis=1)
-
-        d_q[:rows, at] = of(q_ref, 0, True)
-        d_q[rows:, at] = of(q_ref, 0, False)
-        d_k[:rows, at] = of(kv_ref, 0, True)
-        d_v[:rows, at] = of(kv_ref, 0, False)
-        d_k[rows:, at] = of(kv_ref, per, False)
-        d_v[rows:, at] = of(kv_ref, per, True)
-    tokens = x_ref[...].reshape(2 * rows, width)
-    d_x = d_mix_ref[...]
-    for k, part in enumerate((d_q, d_k, d_v)):
-        at = slice(k * width, (k + 1) * width)
-        d_x = d_x + dot(part[...], w_ref[:, at], ROWS)
-        g_ref[:, at] = dot(tokens, part[...], COLS).astype(jnp.bfloat16)
-        if k != 1:
-            g_vec_ref[k // 2 : k // 2 + 1, :] = rows_sum(part[...].astype(jnp.float32))
-    g_ref[:, 3 * width :] = g_out_ref[...]
-    g_vec_ref[2:8, :] = jnp.zeros((6, width), jnp.float32)
-    d_x_ref[...] = d_x.astype(jnp.bfloat16).reshape(2, rows, width)
-
-
-def project_back_call(q, kv, tokens, mixed, d_mix, g_out):
-    micro, rows, width = tokens.shape
-    f32, bf16 = jnp.float32, jnp.bfloat16
-
-    def full(shape):
-        return pl.BlockSpec(shape, lambda i: (0,) * len(shape), pipeline_mode=pl.Buffered(1))
-
-    outs = (
-        jax.ShapeDtypeStruct(tokens.shape, bf16),
-        jax.ShapeDtypeStruct((width, 4 * width), bf16),
-        jax.ShapeDtypeStruct((8, width), f32),
-    )
-    return pl.pallas_call(
-        project_back_kernel,
-        out_shape=outs,
-        grid=(1,),
-        in_specs=[
-            full(q.shape),
-            full(kv.shape),
-            full(tokens.shape),
-            full((width, 3 * width)),
-            full(d_mix.shape),
-            full(g_out.shape),
-        ],
-        out_specs=tuple(full(o.shape) for o in outs),
-        scratch_shapes=[pltpu.VMEM((micro * rows, width), bf16)] * 3,
-        compiler_params=pltpu.CompilerParams(vmem_limit_bytes=56 * 2**20),
-        name="project_back",
-    )(q, kv, tokens, mixed, d_mix, g_out)
-
-
-def cut(axis, start, size):
-    return (axis, start, size)
-
-
 def near_body(inputs, cotangent, random_blocks, global_blocks, *shards):
     (
         query_weight, query_bias, key_weight, value_weight, value_bias, out_weight, out_bias, attn_gain,
@@ -1073,34 +1245,15 @@
     per = HEADS // groups
     in_place = rows // BLOCK
     blocks = groups * in_place
-    vectors = jnp.stack(
-        [query_bias, value_bias, out_bias, attn_gain, attn_shift, down_bias, ffn_gain, ffn_shift], axis=1
-    )
-    vectors = jnp.concatenate([vectors, up_bias.reshape(depth, -1)], axis=1)
-    vectors = jnp.pad(vectors, ((0, 0), (0, 128 - vectors.shape[1])))
-    mixed_shard = jnp.concatenate(
-        [query_weight, key_weight, value_weight, out_weight, vectors], axis=1
-    )
-    half = 2 * width
-    (mixed,) = gather_call(
-        [mixed_shard], [(False, True, (cut(1, 0, half), cut(1, half, half + 128)))], 1
-    )
-    mixed = mixed.reshape(width, -1)
-    rows_f32 = mixed[:, 4 * width : 4 * width + 16].astype(jnp.float32).T
-    bias = rows_f32[:8]
-    vec = rows_f32[2:10]
-    up_bias_row = mixed[:, 4 * width + 8 : 4 * width + 8 + ff // width].astype(jnp.float32).reshape(1, ff)
-    q_parts, kv_parts = project_call(inputs, mixed, bias, groups)
-    pairs = (cut(0, 0, per), cut(0, per, per))
-    q, kv, up, down = gather_call(
-        [q_parts, kv_parts, up_weight, down_weight],
-        [
-            (True, False, None),
-            (True, True, pairs),
-            (False, True, (cut(1, 0, ff), None)),
-            (False, True, (None, cut(1, 0, width))),
-        ],
-        2,
+    q, kv, up, down, mixed, vec, up_bias_row = front_call(
+        inputs,
+        (query_weight, key_weight, value_weight, out_weight),
+        up_weight,
+        down_weight,
+        (
+            query_bias, value_bias, out_bias, attn_gain, attn_shift, down_bias, ffn_gain, ffn_shift, up_bias,
+        ),
+        1,
     )
     up = up.reshape(width, ff)
     down = down.reshape(ff, width)
@@ -1121,46 +1274,28 @@
     kv = kv.reshape((devices, 2 * per) + split)
     packed = (groups, per, rows, 2 * HD)
     attended, lse = attend_call(table, q, kv)
-    (context,) = gather_call([attended.reshape(packed)], [(True, False, None)], 3)
+    context = swap_call(attended.reshape(packed), 3)
     layer_out, d_mix, d_context, g_out, g_up, g_down, g_vec, g_up_bias = dense_call(
         context, inputs, cotangent, mixed, up, down, vec, up_bias_row
     )
-    (d_context,) = gather_call([d_context], [(True, False, None)], 4)
+    d_context = swap_call(d_context, 4)
     d_q, d_kv = attend_back_call(table, q, kv, d_context.reshape(q.shape), attended, lse)
-    d_q, d_kv, grad_up, grad_down = scatter_call(
-        [
-            d_q.reshape(packed),
-            d_kv.reshape(devices, 2 * per, rows, 2 * HD),
-            g_up.reshape(devices, depth, ff),
-            g_down.reshape(devices, -1, width),
-        ],
-        [
-            (False, False, None),
-            (False, True, pairs),
-            (True, True, (cut(1, 0, ff), None)),
-            (True, True, (None, cut(1, 0, width))),
-        ],
+    results = back_call(
+        d_q.reshape(packed),
+        d_kv.reshape(devices, 2 * per, rows, 2 * HD),
+        g_up.reshape(devices, depth, ff),
+        g_down.reshape(devices, -1, width),
+        inputs,
+        mixed,
+        d_mix,
+        g_out,
+        g_vec,
+        g_up_bias,
         5,
     )
-    input_grad, g_mixed, g_vec_two = project_back_call(d_q, d_kv, inputs, mixed, d_mix, g_out)
-    sums = jnp.concatenate([g_vec_two[:2], g_vec[:6]], axis=0).reshape(8, devices, depth)
-    sums = jnp.concatenate(
-        [sums.transpose(1, 0, 2), g_up_bias.reshape(devices, ff // width, depth)], axis=1
-    )
-    sums = jnp.pad(sums, ((0, 0), (0, 16 - sums.shape[1]), (0, 128 - depth)))
-    grad_mixed, grad_vec = scatter_call(
-        [g_mixed.reshape(devices, depth, 4 * width), sums],
-        [
-            (True, True, (cut(1, 0, half), cut(1, half, half))),
-            (True, True, (cut(1, 0, 128), None)),
-        ],
-        6,
-    )
-    grad_query, grad_key, grad_value, grad_out = (
-        grad_mixed[:, k * width : (k + 1) * width] for k in range(4)
-    )
-    vector = [grad_vec[k, :depth] for k in range(8)]
-    grad_up_bias = grad_vec[8 : 8 + ff // width, :depth].reshape(-1)
+    (
+        input_grad, grad_query, grad_key, grad_value, grad_out, grad_up, grad_down, *vector, grad_up_bias,
+    ) = leave_call(*results)
     return (
         layer_out, input_grad, grad_query, vector[0], grad_key, grad_value, vector[1], grad_out,
         vector[2], vector[3], vector[4], grad_up, grad_up_bias, grad_down, vector[5], vector[6], vector[7],

time: 338 us -> 297 us (0.88)
  local copies, waits for them, and re-layouts: 21.1 us -> 1.1 us
  Pallas kernels: 311 us -> 294 us
  other arithmetic: 4.07 us -> 0.65 us
    pallas_call x8 -> x5, Pallas kernels: 262 us -> 246 us  [the longest x1 107 us: front_call(): pl.pallas_call(partial(front_kernel, kinds), out_shape=(jax.ShapeDtypeStr...]
    another operation x8 -> x0, local copies, waits for them, and re-layouts: 5.97 us -> none  [near_body(): jnp.stack([query_bias, value_bias, out_bias, attn_gain, attn_shift, down_...]
    unnamed x20 -> x2, local copies, waits for them, and re-layouts: 5.22 us -> 0.01 us
    slice x6 -> x0, local copies, waits for them, and re-layouts: 4.87 us -> none  [the longest x1 1.71 us: near_body(): grad_mixed[:, k * width:(k + 1) * width]]
where the time goes in v1:
time: 297 us
  Pallas kernels  294 us (99%)
    pallas_call x1, Pallas kernels, front_call(): pl.pallas_call(partial(front_kernel, kinds), out_shape=(jax.ShapeDtypeStr...  107 us
    pallas_call x1, Pallas kernels, back_call(): pl.pallas_call(partial(back_kernel, kinds, [len(s) for s in scratch]), ou...  106 us
    pallas_call x2, Pallas kernels, swap_call(): pl.pallas_call(swap_kernel, out_shape=jax.ShapeDtypeStruct(array.shape, a...  30.6 us
    pallas_call x1, Pallas kernels, dense_call(): pl.pallas_call(dense_kernel, out_shape=outs, in_specs=[full(c.shape), ful...  22.7 us
    pallas_call x1, Pallas kernels, attend_back_call(): pl.pallas_call(attend_back_kernel, out_shape=(jax.ShapeDtypeStruct(q.shap...  15.1 us
    pallas_call x1, Pallas kernels, attend_call(): pl.pallas_call(attend_kernel, out_shape=(jax.ShapeDtypeStruct(q.shape, jn...  10.5 us

profile of v1, /device:TPU:0, one launch (start us, length us, event | category | flops | bytes accessed | tf_op | source)
XLA Modules:
  0.0 296.9 jit_solution(7362822347999195511)
XLA Ops:
  0.7 0.0 copy-start
  0.7 0.8 reshape.71
  1.4 0.0 copy-done
  1.4 0.1 constant_dynamic-slice_fusion
  1.5 0.1 copy.36
  1.6 0.1 reshape.70
  1.8 0.6 pad_add_fusion.table_ref
  2.4 107.4 %front.1 = (bf16[4,3,128,128]{3,2,1,0:T(8,128)(2,1)}, bf16[32,6,128,128]{3,2,1,0:T(8,128)(2,1)}, bf16[32,24,3072]{2,1,0:T(8,128)(2,1)}, bf16[32,96,768]{2,1,0:T(...) custom-call(bf16[2,128,768]{2,1,0:T(8,128)(2,1)} %refs_4_.3, ...), custom_call_target="tpu_custom_call" | custom-call | tf_op jit(solution)/shard_map/front/pallas_call | solution.py:367
  109.8 10.5 %attend.1 = (bf16[4,3,2,64,128]{4,3,2,1,0:T(8,128)(2,1)}, f32[4,3,2,2,64,128]{5,4,3,2,1,0:T(8,128)}) custom-call(s32[150]{0:T(256)} %pad_add_fusion.table_ref, bf16[4,3,2,64,128]{4,3,2,1,0:T(8,128)(2,1)} %bitcast.18, bf16[32,6,2,64,128]{4,3,2,1,0:T(8,128)(2,1)} %bitcast.11), custom_call_target="tpu_custom_call" | custom-call | tf_op jit(solution)/shard_map/attend/pallas_call | solution.py:878
  120.3 17.1 %swap3.1.c_ref = bf16[4,3,128,128]{3,2,1,0:T(8,128)(2,1)} custom-call(bf16[4,3,128,128]{3,2,1,0:T(8,128)(2,1)} %bitcast.20), custom_call_target="tpu_custom_call" | custom-call | tf_op jit(solution)/shard_map/swap3/pallas_call | solution.py:210
  137.4 22.7 %dense.1 = (bf16[2,128,768]{2,1,0:T(8,128)(2,1)}, f32[256,768]{1,0:T(8,128)}, bf16[4,3,128,128]{3,2,1,0:T(8,128)(2,1)}, bf16[768,768]{1,0:T(8,128)(2,1)}, bf16[7...) custom-call(bf16[4,3,128,128]{3,2,1,0:T(8,128)(2,1)} %swap3.1.c_ref, ...), custom_call_target="tpu_custom_call" | custom-call | tf_op jit(solution)/shard_map/dense/pallas_call | solution.py:1196
  160.2 13.5 %swap4.1 = bf16[4,3,128,128]{3,2,1,0:T(8,128)(2,1)} custom-call(bf16[4,3,128,128]{3,2,1,0:T(8,128)(2,1)} %get-tuple-element.66.in_ref), custom_call_target="tpu_custom_call" | custom-call | tf_op jit(solution)/shard_map/swap4/pallas_call | solution.py:210
  173.7 15.1 %attend_back.1 = (bf16[4,3,2,64,128]{4,3,2,1,0:T(8,128)(2,1)}, bf16[32,6,2,64,128]{4,3,2,1,0:T(8,128)(2,1)}) custom-call(s32[150]{0:T(256)} %pad_add_fusion.table_ref, bf16[4,3,2,64,128]{4,3,2,1,0:T(8,128)(2,1)} %bitcast.19, bf16[32,6,2,64,128]{4,3,2,1,0:T(8,128)(2,1)} %bitcast.12, bf16[4,3,2,64,128]{4,3,2,1,0:T(8,128)(2,1)} %bitcast.21, ...), custom_call_target="tpu_custom_call" | custom-call | tf_op jit(solution)/shard_map/attend_back/pallas_call | solution.py:1038
  188.8 105.5 %back.1 = (bf16[2,128,768]{2,1,0:T(8,128)(2,1)}, f32[24,3072]{1,0:T(8,128)}, f32[24,3072]{1,0:T(8,128)}, f32[96,768]{1,0:T(8,128)}, f32[16,128]{1,0:T(8,128)}) custom-call(bf16[4,3,128,128]{3,2,1,0:T(8,128)(2,1)} %bitcast.22, bf16[32,6,128,128]{3,2,1,0:T(8,128)(2,1)} %bitcast.13, bf16[32,24,3072]{2,1,0:T(8,128)(2,1)} %bitcast.14, ...), custom_call_target="tpu_custom_call" | custom-call | tf_op jit(solution)/shard_map/back/pallas_call | solution.py:691
  294.4 2.3 leave.1
Async XLA Ops:
  0.7 0.8 copy-start

commit v2 on v1

--- a/solution.py
+++ b/solution.py
@@ -31,13 +31,131 @@
     return b, h, core, x, y, across_x, across_y, partner, line
 
 
-def meet(b, h, others, line):
+def meet(b, h):
     barrier = pltpu.get_barrier_semaphore()
-    for other in others:
-        pl.semaphore_signal(barrier, inc=1, device_id=(other, h), device_id_type=MESH)
-    for d in range(1, 4):
-        pl.semaphore_signal(barrier, inc=1, device_id=(b, line[d]), device_id_type=MESH)
-    pl.semaphore_wait(barrier, len(others) + 3)
+    count = lax.axis_size("blk") * lax.axis_size("head")
+
+    def tell(k, carry):
+        other = (b * 4 + h + k) % count
+        pl.semaphore_signal(barrier, inc=1, device_id=(other // 4, other % 4), device_id_type=MESH)
+        return carry
+
+    lax.fori_loop(1, count, tell, 0)
+    pl.semaphore_wait(barrier, count - 1)
+
+
+def pair_place(pair):
+    at, along = pair % 6, pair // 6
+    place = at + at // 3 + jnp.where(at > 3, 1, 0)
+    x = place // 2 % 2
+    return place + along % 2 * (2 - 4 * x), along
+
+
+def place_pair(b, h):
+    x = b // 2 % 2
+    place = b + h % 2 * (2 - 4 * x)
+    busy = jnp.logical_and(place != 3, place != 5)
+    at = place - jnp.where(place > 3, 1, 0) - jnp.where(place > 5, 1, 0)
+    return busy, jnp.minimum(h * 6 + at, 23)
+
+
+def exchange(to_pairs, src, dst, sems, rows=slice(None)):
+    send, recv, own = sems
+    b = lax.axis_index("blk")
+    h = lax.axis_index("head")
+    me = b * 4 + h
+    devices = lax.axis_size("blk") * lax.axis_size("head")
+    pairs = 24
+    busy, mine = place_pair(b, h)
+
+    def other(at):
+        if to_pairs:
+            return pair_place(at)
+        return at // 4, at % 4
+
+    def copy(at):
+        slot = me if to_pairs else mine
+        return remote(
+            src.at[at, rows], dst.at[slot, rows], send.at[at], recv.at[slot], other(at)
+        )
+
+    def away(at):
+        place, along = other(at)
+        return jnp.logical_not(jnp.logical_and(place == b, along == h))
+
+    count = pairs if to_pairs else devices
+    first = me * count // devices
+    kept = pltpu.make_async_copy(
+        src.at[mine if to_pairs else me, rows], dst.at[me if to_pairs else mine, rows], own
+    )
+
+    def begin():
+        def one(k, carry):
+            at = (first + k) % count
+
+            @pl.when(away(at))
+            def _():
+                copy(at).start()
+
+            return carry
+
+        def everything():
+            lax.fori_loop(0, count, one, 0)
+
+        if to_pairs:
+            everything()
+            pl.when(busy)(kept.start)
+        else:
+
+            @pl.when(busy)
+            def _():
+                everything()
+                kept.start()
+
+    def arrive():
+        def one(at, carry):
+            here = dst.at[at, rows]
+            landed = remote(here, here, send.at[0], recv.at[at], (b, h))
+            if to_pairs:
+                pl.when(at != me)(landed.wait_recv)
+            else:
+                place, along = pair_place(at)
+                own_pair = jnp.logical_and(place == b, along == h)
+                pl.when(jnp.logical_not(own_pair))(landed.wait_recv)
+            return carry
+
+        def everything():
+            lax.fori_loop(0, devices if to_pairs else pairs, one, 0)
+
+        if to_pairs:
+
+            @pl.when(busy)
+            def _():
+                everything()
+                kept.wait()
+        else:
+            everything()
+            pl.when(busy)(kept.wait)
+
+    def sent():
+        def one(at, carry):
+            pl.when(away(at))(copy(at).wait_send)
+            return carry
+
+        def everything():
+            lax.fori_loop(0, count, one, 0)
+
+        if to_pairs:
+            everything()
+        else:
+            pl.when(busy)(everything)
+
+    return begin, arrive, sent
+
+
+def exchange_semaphores():
+    dma = pltpu.SemaphoreType.DMA
+    return [dma((32,)), dma((32,)), dma]
 
 
 def remote(src, dst, send_sem, recv_sem, device):
@@ -65,7 +183,7 @@
     locals_ = []
 
     def enter():
-        meet(b, h, (across_x, across_y, partner), line)
+        meet(b, h)
 
     def piece(i, place):
         return ins[i].at[place] if kinds[i][0] else ins[i]
@@ -193,28 +311,24 @@
     return [dma((n,)), dma((n, 6)), dma((n, 4)), dma((n, 4, 8)), dma((n, 4, 8))]
 
 
-def swap_kernel(in_ref, out_ref, *sems):
-    enter, begin, along_done, _, _, _, kept, sent = gather_steps(
-        [(True, False, None)], [in_ref], [out_ref], sems
-    )
-    enter()
-    begin(0)
-    for d in range(1, 4):
-        along_done(0, d)
-    kept()
+def exchange_kernel(to_pairs, in_ref, out_ref, *sems):
+    begin, arrive, sent = exchange(to_pairs, in_ref, out_ref, sems)
+    meet(lax.axis_index("blk"), lax.axis_index("head"))
+    begin()
+    arrive()
     sent()
 
 
-def swap_call(array, collective):
+def exchange_call(to_pairs, array, collective):
     far = pl.BlockSpec(memory_space=pl.ANY)
     return pl.pallas_call(
-        swap_kernel,
-        out_shape=jax.ShapeDtypeStruct(array.shape, array.dtype),
+        partial(exchange_kernel, to_pairs),
+        out_shape=jax.ShapeDtypeStruct((32 if to_pairs else 24,) + array.shape[1:], array.dtype),
         in_specs=[far],
         out_specs=far,
-        scratch_shapes=gather_semaphores(1),
+        scratch_shapes=exchange_semaphores(),
         compiler_params=pltpu.CompilerParams(collective_id=collective, has_side_effects=True),
-        name=f"swap{collective}",
+        name=f"exchange{collective}",
     )(array)
 
 
@@ -234,19 +348,19 @@
         x_ref, wq_in, wk_in, wv_in, wo_in, up_in, down_in, *vectors,
     ) = refs[:16]
     (
-        q_out, kv_out, up_out, down_out, w_out, vec_ref, up_bias_ref,
-        tile, chunk, mixed, rows_wide, w_ref, q_parts, kv_parts, join_sem, w_sem,
-    ) = refs[16:32]
+        land_out, up_out, down_out, w_out, vec_ref, up_bias_ref,
+        tile, chunk, mixed, rows_wide, w_ref, parts, join_sem, w_sem,
+    ) = refs[16:30]
     rows = x_ref.shape[1]
     width = x_ref.shape[2]
     shards, depth, _ = mixed.shape
-    groups, per, _, _ = q_parts.shape
     enter, begin, along_done, pass_on, corner, finish, kept, sent = gather_steps(
         kinds,
-        [chunk, up_in, down_in, kv_parts, q_parts],
-        [mixed, up_out, down_out, kv_out, q_out],
-        refs[32:],
-    )
+        [chunk, up_in, down_in],
+        [mixed, up_out, down_out],
+        refs[33:],
+    )
+    begin_pairs, arrive_pairs, sent_pairs = exchange(True, parts, land_out, refs[30:33])
     joins = [
         pltpu.make_async_copy(ref, chunk.at[:, pl.ds(k * width, width)], join_sem.at[k])
         for k, ref in enumerate((wq_in, wk_in, wv_in, wo_in))
@@ -299,52 +413,36 @@
             part = part + vec_ref[k // 2 : k // 2 + 1, :]
         made.append(part.astype(jnp.bfloat16))
     q, k, v = made
-    for g in range(groups):
-        for j in range(per):
-            col = (g * per + j) * HD
-            kv_parts[g, j] = jnp.concatenate([halves(k[:rows], col), halves(v[:rows], col)], axis=1)
-            kv_parts[g, per + j] = jnp.concatenate([halves(v[rows:], col), halves(k[rows:], col)], axis=1)
-    begin(3)
-    for g in range(groups):
-        for j in range(per):
-            col = (g * per + j) * HD
-            q_parts[g, j] = jnp.concatenate([halves(q[:rows], col), halves(q[rows:], col)], axis=1)
-    pass_on(1, 1)
-    pass_on(2, 1)
-    corner(1, 0)
-    corner(2, 0)
-    along_done(3, 1)
-    pass_on(3, 0)
-    begin(4)
-    along_done(3, 2)
-    corner(3, 0)
-    pass_on(3, 1)
-    along_done(3, 3)
-    along_done(1, 3)
-    along_done(2, 3)
-    corner(3, 1)
-    pass_on(3, 2)
-    pass_on(1, 2)
-    pass_on(2, 2)
-    corner(1, 1)
-    corner(2, 1)
-    corner(3, 2)
-    pass_on(3, 3)
-    corner(3, 3)
-    corner(1, 2)
-    corner(2, 2)
-    pass_on(1, 3)
-    pass_on(2, 3)
-    corner(1, 3)
-    corner(2, 3)
-    for d in range(1, 4):
-        along_done(4, d)
-    finish(3)
+    for pair in range(parts.shape[0]):
+        col, at = pair // 2 * HD, pair % 2 * rows
+        mid = at + rows // 2
+        parts[pair, :rows] = jnp.concatenate(
+            [halves(k[at : at + rows], col), halves(v[at : at + rows], col)], axis=1
+        )
+        parts[pair, rows:] = jnp.concatenate(
+            [halves(q[at:mid], col), halves(q[mid : at + rows], col)], axis=1
+        )
+    begin_pairs()
+    for i in (1, 2):
+        pass_on(i, 1)
+        corner(i, 0)
+    for i in (1, 2):
+        along_done(i, 3)
+    for i in (1, 2):
+        pass_on(i, 2)
+        corner(i, 1)
+    for i in (1, 2):
+        pass_on(i, 3)
+        corner(i, 2)
+    for i in (1, 2):
+        corner(i, 3)
+    arrive_pairs()
     finish(1)
     finish(2)
     kept()
     leave.wait()
     sent()
+    sent_pairs()
 
 
 def front_call(tokens, matrices, up, down, vectors, collective):
@@ -352,23 +450,19 @@
     depth, ff = up.shape
     groups = lax.axis_size("head")
     devices = groups * lax.axis_size("blk")
-    per = HEADS // groups
     f32, bf16 = jnp.float32, jnp.bfloat16
     half = 2 * width
     kinds = [
         (False, True, (cut(1, 0, half), cut(1, half, half + 128))),
         (False, True, (cut(1, 0, ff), None)),
         (False, True, (None, cut(1, 0, width))),
-        (True, True, (cut(0, 0, per), cut(0, per, per))),
-        (True, False, None),
     ]
     near = pl.BlockSpec(memory_space=pltpu.VMEM)
     far = pl.BlockSpec(memory_space=pl.ANY)
     return pl.pallas_call(
         partial(front_kernel, kinds),
         out_shape=(
-            jax.ShapeDtypeStruct((groups, per, rows, 2 * HD), bf16),
-            jax.ShapeDtypeStruct((devices, 2 * per, rows, 2 * HD), bf16),
+            jax.ShapeDtypeStruct((devices, rows + rows // 2, 2 * HD), bf16),
             jax.ShapeDtypeStruct((devices,) + up.shape, bf16),
             jax.ShapeDtypeStruct((devices,) + down.shape, bf16),
             jax.ShapeDtypeStruct((width, 4 * width), bf16),
@@ -376,19 +470,19 @@
             jax.ShapeDtypeStruct((1, ff), f32),
         ),
         in_specs=[near] + [far] * 6 + [near] * 9,
-        out_specs=(far,) * 5 + (near,) * 2,
+        out_specs=(far,) * 4 + (near,) * 2,
         scratch_shapes=[
             pltpu.VMEM((depth, 128), f32),
             pltpu.VMEM((depth, 4 * width + 128), bf16),
             pltpu.VMEM((devices, depth, 4 * width + 128), bf16),
             pltpu.VMEM((devices, depth, 128), f32),
             pltpu.VMEM((width, 4 * width), bf16),
-            pltpu.VMEM((groups, per, rows, 2 * HD), bf16),
-            pltpu.VMEM((groups, 2 * per, rows, 2 * HD), bf16),
+            pltpu.VMEM((HEADS * micro, rows + rows // 2, 2 * HD), bf16),
             pltpu.SemaphoreType.DMA((4,)),
             pltpu.SemaphoreType.DMA,
         ]
-        + gather_semaphores(5),
+        + exchange_semaphores()
+        + gather_semaphores(3),
         compiler_params=pltpu.CompilerParams(
             collective_id=collective, has_side_effects=True, vmem_limit_bytes=56 * 2**20
         ),
@@ -396,14 +490,13 @@
     )(tokens, *matrices, up, down, *vectors)
 
 
-def scatter_steps(kinds, ins, lands, bufs, sems):
-    local_sem, own_sem, line_send, line_recv, core_send, core_recv, send, recv = sems
+def scatter_steps(cuts, ins, bufs, sems):
+    local_sem, line_send, line_recv, core_send, core_recv, send, recv = sems
     b, h, core, x, y, across_x, across_y, partner, line = places()
     seen = jnp.where(jnp.logical_or(h == 1, h == 2), 2, 3)
     chip = b // 2
     targets = (3 - chip, chip + 1 - 2 * x, chip + 2 - 4 * y, chip)
     started = []
-    locals_ = []
     loads = {}
     order = (3, 2, 1, 0)
 
@@ -422,19 +515,9 @@
             )
         )
 
-    def keep(src, i):
-        own = pltpu.make_async_copy(src, lands[i].at[h], own_sem.at[i])
-        own.start()
-        locals_.append(own)
-
-    def begin(i):
-        if not kinds[i][1]:
-            for d in (3, 2, 1):
-                along(i, ins[i].at[line[d]], lands[i].at[h], d)
-            keep(ins[i].at[h], i)
-            return
+    def begin(i, some=(0, 1, 2, 3)):
         from_partner, total = bufs[i][0], bufs[i][1]
-        for t in range(4):
+        for t in some:
             go(
                 remote(
                     ins[i].at[pl.ds((targets[t] * 2 + 1 - core) * 4, 4)],
@@ -475,7 +558,7 @@
 
     def corner(i):
         total = bufs[i][1]
-        first, second = kinds[i][2]
+        first, second = cuts[i]
         ready(i, 0)
         for d in order:
             both_cores(i, 0, d)
@@ -487,7 +570,7 @@
 
     def sides(i):
         total = bufs[i][1]
-        first, second = kinds[i][2]
+        first, second = cuts[i]
         ready(i, 1)
         ready(i, 2)
         for d in order:
@@ -503,7 +586,6 @@
             go(remote(total.at[2, line[d]], bufs[i][5].at[d], send.at[i, d, 3], recv.at[i, d, 3], (across_y, h)))
 
     def own(i):
-        summed = kinds[i][0]
         total = bufs[i][1]
         ready(i, 3)
         for d in order:
@@ -511,233 +593,225 @@
             wait_for(bufs[i][5].at[d], i, d, 3)
             both_cores(i, 3, d, (bufs[i][4], bufs[i][5]))
             if d > 0:
-                landing = bufs[i][6].at[1 if d == 1 else seen] if summed else lands[i].at[h]
-                along(i, total.at[3, line[d]], landing, d)
-            elif not summed:
-                keep(total.at[3, h], i)
+                along(i, total.at[3, line[d]], bufs[i][6].at[1 if d == 1 else seen], d)
 
     def finish(i):
-        summed = kinds[i][0]
+        value = bufs[i][1][3, h].astype(jnp.float32)
         for d in range(1, 4):
-            landing = bufs[i][6].at[d] if summed else lands[i].at[line[d]]
+            landing = bufs[i][6].at[d]
             remote(
                 landing, landing, line_send.at[i, d], line_recv.at[i, d], (b, line[d])
             ).wait_recv()
-        if not summed:
-            return None
-        value = bufs[i][1][3, h].astype(jnp.float32)
-        for d in range(1, 4):
             value = value + bufs[i][6][d].astype(jnp.float32)
         return value
-
-    def kept():
-        for copy in locals_:
-            copy.wait()
-        locals_.clear()
 
     def sent():
         for copy in started:
             copy.wait_send()
 
     def enter():
-        meet(b, h, (across_x, across_y, partner), line)
-
-    return enter, begin, corner, sides, own, finish, kept, sent
-
-
-def scatter_scratch(chunk, dtype, kind):
-    summed, spread, cuts = kind
-    if not spread:
-        return []
-    scratch = [pltpu.VMEM((4, 4) + chunk, dtype), pltpu.VMEM((4, 4) + chunk, dtype)]
+        meet(b, h)
+
+    return enter, begin, corner, sides, own, finish, sent
+
+
+def scatter_scratch(chunk, dtype, cuts):
+    shapes = [(4, 4) + chunk, (4, 4) + chunk]
     for cut_ in cuts:
-        size = list(chunk)
+        size = [16, 128]
         if cut_ is not None:
+            size = list(chunk)
             size[cut_[0]] = cut_[2]
-        else:
-            size = [8, 128]
-        scratch.append(pltpu.VMEM((4,) + tuple(size), dtype))
-    scratch += [pltpu.VMEM((4,) + chunk, dtype)] * 2
-    if summed:
-        scratch.append(pltpu.VMEM((4,) + chunk, dtype))
-    return scratch
+        shapes.append((4,) + tuple(size))
+    shapes += [(4,) + chunk] * 3
+    return [pltpu.VMEM(shape, dtype) for shape in shapes]
 
 
 def scatter_semaphores(n):
     dma = pltpu.SemaphoreType.DMA
-    return [dma((n, 4)), dma((n,))] + [dma((n, 4))] * 4 + [dma((n, 4, 4))] * 2
-
-
-def back_kernel(kinds, counts, *refs):
+    return [dma((n, 4))] * 5 + [dma((n, 4, 4))] * 2
+
+
+UP, DOWN, OUT, QUERY, KEY, VALUE, SMALL = range(7)
+
+
+def back_kernel(cuts, *refs):
     (
-        dq_in, dkv_in, up_in, down_in, x_ref, mixed_in, d_mix_ref, g_out_ref, g_vec_ref, g_up_bias_ref,
-        d_x_ref, g_mixed_ref, g_up_ref, g_down_ref, g_small_ref,
-        dq_land, dkv_land, terms, small, w_ref, d_q, d_k, d_v, w_sem,
-    ), rest = refs[:24], list(refs[24:])
-    bufs = []
-    for count in counts:
-        bufs.append(rest[:count])
-        rest = rest[count:]
-    groups, per, rows, _ = dq_land.shape
+        parts_in, up_in, down_in, x_ref, mixed_in, d_mix_ref, g_out_ref, g_vec_ref, g_up_bias_ref,
+        d_x_ref, g_outw_ref, g_query_ref, g_key_ref, g_value_ref, g_up_ref, g_down_ref, g_small_ref,
+        land, terms, small, w_ref, d_q, d_k, d_v, w_sem,
+    ), rest = refs[:25], list(refs[25:])
+    q_sems, kv_sems, rest = rest[:3], rest[3:6], rest[6:]
+    bufs = [rest[7 * i : 7 * i + 7] for i in range(len(cuts))]
+    rows = x_ref.shape[1]
     width = x_ref.shape[2]
-    depth = terms.shape[1]
-    shards = terms.shape[0]
-    ins = (dq_in, dkv_in, up_in, down_in, terms, small)
-    enter, begin, corner, sides, own, finish, kept, sent = scatter_steps(
-        kinds, ins, (dq_land, dkv_land, None, None, None, None), bufs, rest
-    )
+    _, shards, depth, _ = terms.shape
+    ins = (up_in, down_in, terms.at[0], terms.at[1], terms.at[2], terms.at[3], small)
+    enter, begin, corner, sides, own, finish, sent = scatter_steps(
+        cuts, ins, bufs, rest[7 * len(cuts) :]
+    )
+    begin_q, arrive_q, sent_q = exchange(False, parts_in, land, q_sems, pl.ds(rows, rows // 2))
+    begin_kv, arrive_kv, sent_kv = exchange(False, parts_in, land, kv_sems, pl.ds(0, rows))
     load = pltpu.make_async_copy(mixed_in.at[:, pl.ds(0, 3 * width)], w_ref, w_sem)
     load.start()
+    def keep_term(at, value):
+        terms[at] = value.reshape(shards, depth, width).astype(jnp.bfloat16)
+
     enter()
-    for i in (1, 0, 2, 3):
-        begin(i)
+    begin_q()
+    begin_kv()
+    keep_term(0, g_out_ref[...].astype(jnp.float32))
     small[...] = jnp.zeros(small.shape, jnp.float32)
-    out_terms = g_out_ref[...].astype(jnp.float32).reshape(shards, depth, width)
-    terms[:, :, 3 * width :] = out_terms.astype(jnp.bfloat16)
-    corner(1)
-    sides(1)
-    corner(2)
-    corner(3)
-    own(1)
-    sides(2)
-    sides(3)
-    finish(0)
-    finish(1)
-    kept()
+    arrive_q()
+    begin(UP, (0,))
+    begin(DOWN, (0,))
+    corner(UP)
+    corner(DOWN)
+    begin(UP, (1, 2, 3,))
+    begin(DOWN, (1, 2, 3,))
+    arrive_kv()
+    spans = []
+    for m in range(2):
+        top, mid = m * rows, m * rows + rows // 2
+        spans.append((m, slice(top, top + rows), slice(top, mid), slice(mid, top + rows)))
+    tokens = x_ref[...].reshape(2 * rows, width)
     for p in range(HEADS // 2):
         at = pl.ds(p * 2 * HD, 2 * HD)
-
-        def of(ref, shift, low):
-            both = []
-            for head in (2 * p, 2 * p + 1):
-                tile = ref[head // per, shift + head % per]
-                both.append(tile[:, :HD] if low else tile[:, HD:])
-            return jnp.concatenate(both, axis=1)
-
-        d_q[:rows, at] = of(dq_land, 0, True)
-        d_q[rows:, at] = of(dq_land, 0, False)
-        d_k[:rows, at] = of(dkv_land, 0, True)
-        d_v[:rows, at] = of(dkv_land, 0, False)
-        d_k[rows:, at] = of(dkv_land, per, False)
-        d_v[rows:, at] = of(dkv_land, per, True)
-    load.wait()
-    tokens = x_ref[...].reshape(2 * rows, width)
-    sums = []
-    for k, half_ref in enumerate((d_q, d_k, d_v)):
-        at = slice(k * width, (k + 1) * width)
-        term = dot(tokens, half_ref[...], COLS).reshape(shards, depth, width)
-        terms[:, :, at] = term.astype(jnp.bfloat16)
-        if k != 1:
-            sums.append(rows_sum(half_ref[...].astype(jnp.float32)))
-    vectors = jnp.concatenate(sums + [g_vec_ref[:6, :]], axis=0)
+        for m, _, early, late in spans:
+            one, two = land[4 * p + m, rows:], land[4 * p + 2 + m, rows:]
+            d_q[early, at] = jnp.concatenate([one[:, :HD], two[:, :HD]], axis=1)
+            d_q[late, at] = jnp.concatenate([one[:, HD:], two[:, HD:]], axis=1)
+    for p in range(HEADS // 2):
+        at = pl.ds(p * 2 * HD, 2 * HD)
+        for m, both, _, _ in spans:
+            one, two = land[4 * p + m, :rows], land[4 * p + 2 + m, :rows]
+            d_k[both, at] = jnp.concatenate([one[:, :HD], two[:, :HD]], axis=1)
+            d_v[both, at] = jnp.concatenate([one[:, HD:], two[:, HD:]], axis=1)
+    keep_term(1, dot(tokens, d_q[...], COLS))
+    keep_term(2, dot(tokens, d_k[...], COLS))
+    keep_term(3, dot(tokens, d_v[...], COLS))
+    vectors = jnp.concatenate(
+        [
+            rows_sum(d_q[...].astype(jnp.float32)),
+            rows_sum(d_v[...].astype(jnp.float32)),
+            g_vec_ref[:6, :],
+        ],
+        axis=0,
+    )
     up_bias = g_up_bias_ref[...]
     up_depth = up_bias.shape[1] // shards
     for s in range(shards):
         small[s, :8, :depth] = vectors[:, s * depth : (s + 1) * depth]
         small[s, 8:9, :up_depth] = up_bias[:, s * up_depth : (s + 1) * up_depth]
-    begin(4)
-    begin(5)
-    own(2)
-    corner(4)
-    corner(5)
-    own(3)
+    begin(OUT)
+    begin(QUERY)
+    begin(KEY)
+    begin(VALUE)
+    begin(SMALL)
+    corner(OUT)
+    corner(QUERY)
+    corner(KEY)
+    corner(VALUE)
+    corner(SMALL)
+    sides(UP)
+    sides(DOWN)
+    sides(OUT)
+    sides(QUERY)
+    sides(KEY)
+    sides(VALUE)
+    sides(SMALL)
+    own(UP)
+    load.wait()
     d_x = d_mix_ref[...]
     for k, half_ref in enumerate((d_q, d_k, d_v)):
         d_x = d_x + dot(half_ref[...], w_ref[:, k * width : (k + 1) * width], ROWS)
     d_x_ref[...] = d_x.astype(jnp.bfloat16).reshape(2, rows, width)
-    sides(4)
-    sides(5)
-    g_up_ref[...] = finish(2)
-    own(4)
-    own(5)
-    g_down_ref[...] = finish(3)
-    g_mixed_ref[...] = finish(4)
-    g_small_ref[...] = finish(5)
+    own(DOWN)
+    g_up_ref[...] = finish(UP)
+    own(OUT)
+    own(QUERY)
+    own(KEY)
+    own(VALUE)
+    own(SMALL)
+    g_down_ref[...] = finish(DOWN)
+    g_outw_ref[...] = finish(OUT)
+    g_query_ref[...] = finish(QUERY)
+    g_key_ref[...] = finish(KEY)
+    g_value_ref[...] = finish(VALUE)
+    g_small_ref[...] = finish(SMALL)
+    sent_q()
     sent()
-
-
-def back_call(d_q, d_kv, g_up, g_down, tokens, mixed, d_mix, g_out, g_vec, g_up_bias, collective):
+    sent_kv()
+
+
+def back_call(parts, g_up, g_down, tokens, mixed, d_mix, g_out, g_vec, g_up_bias, collective):
     micro, rows, width = tokens.shape
     devices, depth, ff = g_up.shape
-    groups, per = d_q.shape[:2]
     f32, bf16 = jnp.float32, jnp.bfloat16
-    half = 2 * width
-    kinds = [
-        (False, False, None),
-        (False, True, (cut(0, 0, per), cut(0, per, per))),
-        (True, True, (cut(1, 0, ff), None)),
-        (True, True, (None, cut(1, 0, width))),
-        (True, True, (cut(1, 0, half), cut(1, half, half))),
-        (True, True, (cut(1, 0, 128), None)),
+    one_way, other_way = (cut(1, 0, width), None), (None, cut(1, 0, width))
+    cuts = [(cut(1, 0, ff), None), other_way, one_way, other_way, one_way, other_way, (cut(1, 0, 128), None)]
+    square = (depth, width)
+    chunks = [(g_up.shape[1:], bf16), (g_down.shape[1:], bf16)] + [(square, bf16)] * 4
+    chunks += [((16, 128), f32)]
+    scratch = [
+        one for (chunk, dtype), c in zip(chunks, cuts) for one in scatter_scratch(chunk, dtype, c)
     ]
-    chunks = [
-        (d_q.shape[1:], bf16),
-        (d_kv.shape[1:], bf16),
-        (g_up.shape[1:], bf16),
-        (g_down.shape[1:], bf16),
-        ((depth, 4 * width), bf16),
-        ((16, 128), f32),
-    ]
-    scratch = [scatter_scratch(chunk, dtype, kind) for (chunk, dtype), kind in zip(chunks, kinds)]
     near = pl.BlockSpec(memory_space=pltpu.VMEM)
     far = pl.BlockSpec(memory_space=pl.ANY)
     outs = [jax.ShapeDtypeStruct(tokens.shape, bf16)]
+    outs += [jax.ShapeDtypeStruct(square, f32)] * 4
     outs += [
-        jax.ShapeDtypeStruct((depth, 4 * width), f32),
         jax.ShapeDtypeStruct((depth, ff), f32),
         jax.ShapeDtypeStruct(g_down.shape[1:], f32),
         jax.ShapeDtypeStruct((16, 128), f32),
     ]
     return pl.pallas_call(
-        partial(back_kernel, kinds, [len(s) for s in scratch]),
+        partial(back_kernel, cuts),
         out_shape=tuple(outs),
-        in_specs=[far] * 4 + [near, far] + [near] * 4,
-        out_specs=(near,) * 5,
+        in_specs=[far] * 3 + [near, far] + [near] * 4,
+        out_specs=(near,) * len(outs),
         scratch_shapes=[
-            pltpu.VMEM(d_q.shape, bf16),
-            pltpu.VMEM((groups,) + d_kv.shape[1:], bf16),
-            pltpu.VMEM((devices, depth, 4 * width), bf16),
+            pltpu.VMEM((HEADS * micro,) + parts.shape[1:], bf16),
+            pltpu.VMEM((4, devices) + square, bf16),
             pltpu.VMEM((devices, 16, 128), f32),
             pltpu.VMEM((width, 3 * width), bf16),
         ]
         + [pltpu.VMEM((micro * rows, width), bf16)] * 3
         + [pltpu.SemaphoreType.DMA]
-        + [one for some in scratch for one in some]
-        + scatter_semaphores(6),
+        + exchange_semaphores() * 2
+        + scratch
+        + scatter_semaphores(len(cuts)),
         compiler_params=pltpu.CompilerParams(
             collective_id=collective, has_side_effects=True, vmem_limit_bytes=61 * 2**20
         ),
         name="back",
-    )(d_q, d_kv, g_up, g_down, tokens, mixed, d_mix, g_out, g_vec, g_up_bias)
-
-
-def leave_kernel(d_x_in, mixed_in, up_in, down_in, small_in, d_x_ref, *refs):
-    d_x_ref[...] = d_x_in[...]
-    width = d_x_in.shape[2]
-    for k in range(4):
-        refs[k][...] = mixed_in[:, k * width : (k + 1) * width]
-    refs[4][...] = up_in[...]
-    refs[5][...] = down_in[...]
-    for k, ref in enumerate(refs[6:]):
+    )(parts, g_up, g_down, tokens, mixed, d_mix, g_out, g_vec, g_up_bias)
+
+
+def leave_kernel(*refs):
+    *wholes, small_in = refs[:8]
+    outs = refs[8:]
+    for from_ref, to_ref in zip(wholes, outs):
+        to_ref[...] = from_ref[...]
+    for k, ref in enumerate(outs[7:]):
         ref[...] = small_in[k, : ref.shape[0]]
 
 
-def leave_call(d_x, mixed, up, down, small):
-    depth, wide_ = mixed.shape
+def leave_call(*arrays):
+    *wholes, _ = arrays
+    depth, width = wholes[1].shape
     f32 = jnp.float32
-    outs = [jax.ShapeDtypeStruct(d_x.shape, d_x.dtype)]
-    outs += [jax.ShapeDtypeStruct((depth, wide_ // 4), f32)] * 4
-    outs += [jax.ShapeDtypeStruct(up.shape, f32), jax.ShapeDtypeStruct(down.shape, f32)]
+    outs = [jax.ShapeDtypeStruct(a.shape, a.dtype) for a in wholes]
     outs += [jax.ShapeDtypeStruct((depth,), f32)] * 8
-    outs += [jax.ShapeDtypeStruct((down.shape[0],), f32)]
+    outs += [jax.ShapeDtypeStruct((wholes[6].shape[0],), f32)]
     near = pl.BlockSpec(memory_space=pltpu.VMEM)
     return pl.pallas_call(
         leave_kernel,
         out_shape=tuple(outs),
-        in_specs=[near] * 5,
+        in_specs=[near] * 8,
         out_specs=(near,) * len(outs),
         name="leave",
-    )(d_x, mixed, up, down, small)
+    )(*arrays)
 
 
 def cut(axis, start, size):
@@ -765,21 +839,10 @@
     return array[:, col : col + HD]
 
 
-def listed_rows(table_ref, blocks, per, m, n, j):
-    shard = table_ref[2 * blocks * per * RAND + 2 * GLOB]
-    total = table_ref[2 * blocks * per * RAND + 2 * GLOB + 1]
-    here = shard * blocks + n
-    rows = [jnp.maximum(here - 1, 0), here, jnp.minimum(here + 1, total - 1)]
-    for r in range(RAND):
-        rows.append(table_ref[((m * blocks + n) * per + j) * RAND + r])
-    for g in range(GLOB):
-        rows.append(table_ref[2 * blocks * per * RAND + m * GLOB + g])
-    return rows, here, total
-
-
-def global_of(table_ref, blocks, per, at):
-    base = 2 * blocks * per * RAND
-    return table_ref[base + at], table_ref[base + 2 * GLOB]
+def listed_rows(table_ref, blocks, n):
+    rows = [jnp.maximum(n - 1, 0), n, jnp.minimum(n + 1, blocks - 1)]
+    rows += [table_ref[n * RAND + r] for r in range(RAND)]
+    return rows + [table_ref[blocks * RAND + g] for g in range(GLOB)]
 
 
 def outside(here, total, listed):
@@ -795,263 +858,211 @@
     return jnp.where(lanes_of(value.shape, low), value, jnp.zeros_like(value))
 
 
-def attend_kernel(table_ref, q_ref, kv_ref, out_ref, lse_ref):
-    places_, per, in_place, block, _ = q_ref.shape
-    blocks = places_ * in_place
+def turned(value):
+    return jnp.concatenate([value[:, HD:], value[:, :HD]], axis=1)
+
+
+def to_side(value, odd, low):
+    if isinstance(odd, bool):
+        return only(turned(value) if odd == low else value, low)
+    return only(jnp.where((odd == 1) == low, turned(value), value), low)
+
+
+def key_rows(ref, spot, step):
+    return ref[pl.ds(spot, step), :2].reshape(step * 2 * BLOCK, 2 * HD)
+
+
+GROUP = 8
+STEP = 8
+
+
+def attend_kernel(table_ref, land_ref, out_ref, lse_ref):
+    devices = land_ref.shape[0]
+    blocks = 2 * devices
     scale = jnp.bfloat16(HD ** (-0.5))
-    units = [(j, m) for j in range(per) for m in range(2)]
-
-    def query_block(n, carry):
+
+    def query_blocks(group, carry):
         kvs, scores = [], []
-        for j, m in units:
-            rows, here, total = listed_rows(table_ref, blocks, per, m, n, j)
-            kvs.append(
-                jnp.concatenate(
-                    [kv_ref[r // in_place, m * per + j, r % in_place] for r in rows], axis=0
-                )
+        for u in range(GROUP):
+            n = group * GROUP + u
+            rows = listed_rows(table_ref, blocks, n)
+            kvs.append(jnp.concatenate([land_ref[r // 2, r % 2] for r in rows], axis=0))
+            q = to_side(land_ref[group * (GROUP // 2) + u // 2, 2], u % 2 == 1, True) * scale
+            scores.append(dot(q, kvs[-1], ROWS) + outside(n, blocks, len(rows)))
+        raised = []
+        for u, score in enumerate(scores):
+            top = jnp.max(score, axis=1, keepdims=True)
+            probs = jnp.exp(score - top)
+            total_sum = jnp.sum(probs, axis=1, keepdims=True)
+            raised.append((probs * (1.0 / total_sum)).astype(jnp.bfloat16))
+            lse_ref[group * GROUP + u] = jnp.broadcast_to(
+                top + jnp.log(total_sum), lse_ref.shape[1:]
             )
-            q = only(q_ref[n // in_place, j, n % in_place], m == 0) * scale
-            scores.append(dot(q, kvs[-1], ROWS) + outside(here, total, len(rows)))
-        raised = []
-        for (j, m), score in zip(units, scores):
-            top = jnp.max(score, axis=1, keepdims=True)
-            raised.append(jnp.exp(score - top))
-            total_sum = jnp.sum(raised[-1], axis=1, keepdims=True)
-            raised[-1] = raised[-1] * (1.0 / total_sum)
-            lse_ref[n // in_place, j, m, n % in_place] = jnp.broadcast_to(
-                top + jnp.log(total_sum), (block, 2 * HD)
-            )
-        outs = [dot(r.astype(jnp.bfloat16), kv) for r, kv in zip(raised, kvs)]
-        for j in range(per):
-            out_ref[n // in_place, j, n % in_place] = jnp.where(
-                lanes_of(outs[0].shape, True), outs[2 * j + 1], outs[2 * j]
+        outs = [dot(r, kv) for r, kv in zip(raised, kvs)]
+        for u in range(0, GROUP, 2):
+            out_ref[group * (GROUP // 2) + u // 2] = jnp.where(
+                lanes_of(outs[u].shape, True), turned(outs[u]), outs[u + 1]
             ).astype(jnp.bfloat16)
         return carry
 
-    lax.fori_loop(0, blocks, query_block, 0)
-    step = 8
-    heads = range(per)
-
-    def global_rows(at, carry):
-        m = at // GLOB
-        row, shard = global_of(table_ref, blocks, per, at)
-        local = row % blocks
-        at_place, at_row = local // in_place, local % in_place
-
-        @pl.when(row // blocks == shard)
-        def _():
-            def keys(j, spot):
-                return kv_ref[pl.ds(spot, step), m * per + j].reshape(
-                    step * in_place * block, 2 * HD
-                )
-
-            spots = range(0, kv_ref.shape[0], step)
-            qs = [only(q_ref[at_place, j, at_row], m == 0) * scale for j in heads]
-            scores = [[dot(qs[j], keys(j, spot), ROWS) for spot in spots] for j in heads]
-            raised, sums = [], []
-            for j in heads:
-                top = scores[j][0].max(axis=1, keepdims=True)
-                for s in scores[j][1:]:
-                    top = jnp.maximum(top, s.max(axis=1, keepdims=True))
-                raised.append([jnp.exp(s - top) for s in scores[j]])
-                sums.append(sum(jnp.sum(r, axis=1, keepdims=True) for r in raised[j]))
-                lse_ref[at_place, j, m, at_row] = jnp.broadcast_to(
-                    top + jnp.log(sums[j]), (block, 2 * HD)
-                )
-            for j in heads:
-                out = sum(
-                    dot(r.astype(jnp.bfloat16), keys(j, spot)) for r, spot in zip(raised[j], spots)
-                )
-                old = out_ref[at_place, j, at_row]
-                out_ref[at_place, j, at_row] = jnp.where(
-                    lanes_of(old.shape, m == 1), (out / sums[j]).astype(jnp.bfloat16), old
-                )
-
-        return carry
-
-    lax.fori_loop(0, 2 * GLOB, global_rows, 0)
-
-
-def attend_call(table, q, kv):
+    def everything():
+        lax.fori_loop(0, blocks // GROUP, query_blocks, 0)
+        spots = range(0, devices, STEP)
+        chosen = [table_ref[blocks * RAND + g] for g in range(GLOB)]
+        q = jnp.concatenate(
+            [to_side(land_ref[row // 2, 2], row % 2, True) for row in chosen], axis=0
+        )
+        scores = [dot(q * scale, key_rows(land_ref, spot, STEP), ROWS) for spot in spots]
+        top = scores[0].max(axis=1, keepdims=True)
+        for score in scores[1:]:
+            top = jnp.maximum(top, score.max(axis=1, keepdims=True))
+        raised = [jnp.exp(score - top) for score in scores]
+        total_sum = sum(jnp.sum(r, axis=1, keepdims=True) for r in raised)
+        out = sum(
+            dot(r.astype(jnp.bfloat16), key_rows(land_ref, spot, STEP))
+            for r, spot in zip(raised, spots)
+        )
+        out = out / total_sum
+        lse = jnp.broadcast_to(top + jnp.log(total_sum), out.shape)
+        for g, row in enumerate(chosen):
+            at = slice(g * BLOCK, (g + 1) * BLOCK)
+            lse_ref[row] = lse[at]
+            new = jnp.where(row % 2 == 0, turned(out[at]), out[at]).astype(jnp.bfloat16)
+            old = out_ref[row // 2]
+            out_ref[row // 2] = jnp.where(lanes_of(old.shape, row % 2 == 0), new, old)
+
+    pl.when(table_ref[blocks * RAND + GLOB] == 1)(everything)
+
+
+def attend_call(table, land):
     spec = pl.BlockSpec(memory_space=pltpu.VMEM)
-    places_, per, in_place, block, lanes = q.shape
+    devices, _, block, lanes = land.shape
     return pl.pallas_call(
         attend_kernel,
         out_shape=(
-            jax.ShapeDtypeStruct(q.shape, jnp.bfloat16),
-            jax.ShapeDtypeStruct((places_, per, 2, in_place, block, lanes), jnp.float32),
+            jax.ShapeDtypeStruct((devices, block, lanes), jnp.bfloat16),
+            jax.ShapeDtypeStruct((2 * devices, block, lanes), jnp.float32),
         ),
-        in_specs=[pl.BlockSpec(memory_space=pltpu.SMEM), spec, spec],
+        in_specs=[pl.BlockSpec(memory_space=pltpu.SMEM), spec],
         out_specs=(spec, spec),
         compiler_params=pltpu.CompilerParams(vmem_limit_bytes=56 * 2**20),
         name="attend",
-    )(table, q, kv)
-
-
-def attend_back_kernel(
-    table_ref, q_ref, kv_in, d_ref, out_ref, lse_ref, dq_ref, dkv_out, total_ref, kv_ref, in_sem, out_sem
-):
-    places_, per, in_place, block, _ = q_ref.shape
-    blocks = places_ * in_place
+    )(table, land)
+
+
+def attend_back_kernel(table_ref, land_ref, d_ref, out_ref, lse_ref, parts_ref, total_ref):
+    devices = land_ref.shape[0]
+    blocks = 2 * devices
     scale = jnp.bfloat16(HD ** (-0.5))
-    units = [(j, m) for j in range(per) for m in range(2)]
-
-    step = 8
-    fetch = pltpu.make_async_copy(kv_in, kv_ref, in_sem)
-    fetch.start()
-
-    def clear(i, carry):
-        total_ref[i] = jnp.zeros(total_ref.shape[1:], jnp.float32)
-        return carry
-
-    lax.fori_loop(0, total_ref.shape[0], clear, 0)
-    fetch.wait()
-
-    def pair_of(n, j, m, keep):
-        at = (n // in_place, j, n % in_place)
-        q = only(q_ref[at], m == 0) * scale
-        d = only(d_ref[at], m == 1)
+
+    def wide(column, width):
+        return jnp.concatenate([column] * (width // column.shape[1]), axis=1)
+
+    def pair_of(place, odd, keep):
+        q = to_side(land_ref[place, 2], odd, True) * scale
+        d = to_side(d_ref[place], odd, False)
         if keep is not None:
             d = d * keep
-        delta = jnp.sum(
-            d.astype(jnp.float32) * out_ref[at].astype(jnp.float32), axis=1, keepdims=True
-        )
-        return jnp.concatenate([q, d], axis=0), delta
-
-    def wide(column, width):
-        return jnp.concatenate([column] * (width // column.shape[1]), axis=1)
-
-    def query_block(n, carry):
+        out = to_side(out_ref[place], odd, False)
+        delta = jnp.sum(d.astype(jnp.float32) * out.astype(jnp.float32), axis=1, keepdims=True)
+        return q, d, delta
+
+    def query_blocks(group, carry):
         listed, kvs, pairs, deltas, boths = [], [], [], [], []
-        for j, m in units:
-            rows, here, total = listed_rows(table_ref, blocks, per, m, n, j)
-            is_global = jnp.logical_or(here == rows[-1], here == rows[-2])
+        for u in range(GROUP):
+            n = group * GROUP + u
+            rows = listed_rows(table_ref, blocks, n)
+            is_global = jnp.logical_or(n == rows[-1], n == rows[-2])
             keep = jnp.where(is_global, 0.0, 1.0).astype(jnp.bfloat16)
-            kv = jnp.concatenate(
-                [kv_ref[r // in_place, m * per + j, r % in_place] for r in rows], axis=0
-            )
-            pair, delta = pair_of(n, j, m, keep)
+            kv = jnp.concatenate([land_ref[r // 2, r % 2] for r in rows], axis=0)
+            q, d, delta = pair_of(group * (GROUP // 2) + u // 2, u % 2 == 1, keep)
             listed.append(rows)
             kvs.append(kv)
-            pairs.append(pair)
+            pairs.append(jnp.concatenate([q, d], axis=0))
             deltas.append(delta)
-            boths.append(dot(pair, kv, ROWS))
+            boths.append(dot(pairs[-1], kv, ROWS))
         weights = []
-        for (j, m), both, delta, kv, rows in zip(units, boths, deltas, kvs, listed):
+        for u, both in enumerate(boths):
+            n = group * GROUP + u
             width = both.shape[1]
-            lse = lse_ref[n // in_place, j, m, n % in_place]
-            scores = both[:block] + outside(here, total, len(rows))
-            probs = jnp.exp(scores - wide(lse, width))
-            d_scores = probs * (both[block:] - delta)
+            scores = both[:BLOCK] + outside(n, blocks, width // BLOCK)
+            probs = jnp.exp(scores - wide(lse_ref[n], width))
+            d_scores = probs * (both[BLOCK:] - deltas[u])
             weights.append(
                 jnp.concatenate(
                     [d_scores.astype(jnp.bfloat16), probs.astype(jnp.bfloat16)], axis=0
                 )
             )
         outs = []
-        for (j, m), weight, pair, kv, rows in zip(units, weights, pairs, kvs, listed):
-            d_kv = dot(weight, pair, COLS)
-            for at, r in enumerate(rows):
-                total_ref[r // in_place, m * per + j, r % in_place] += d_kv[
-                    at * block : (at + 1) * block
-                ]
-            outs.append(dot(weight[:block], kv) * HD ** (-0.5))
-        for j in range(per):
-            dq_ref[n // in_place, j, n % in_place] = jnp.where(
-                lanes_of(outs[0].shape, True), outs[2 * j], outs[2 * j + 1]
+        for u, weight in enumerate(weights):
+            d_kv = dot(weight, pairs[u], COLS)
+            for at, r in enumerate(listed[u]):
+                total_ref[r // 2, r % 2] += d_kv[at * BLOCK : (at + 1) * BLOCK]
+            outs.append(dot(weight[:BLOCK], kvs[u]) * HD ** (-0.5))
+        for u in range(0, GROUP, 2):
+            parts_ref[group * (GROUP // 2) + u // 2, 2] = jnp.where(
+                lanes_of(outs[u].shape, True), outs[u], turned(outs[u + 1])
             ).astype(jnp.bfloat16)
         return carry
 
-    lax.fori_loop(0, blocks, query_block, 0)
-
-    heads = range(per)
-
-    def global_rows(at, carry):
-        m = at // GLOB
-        row, shard = global_of(table_ref, blocks, per, at)
-        local = row % blocks
-        at_place, at_row = local // in_place, local % in_place
-
-        @pl.when(row // blocks == shard)
-        def _():
-            pairs = [pair_of(local, j, m, None) for j in heads]
-
-            def some_keys(spot, d_qs):
-                at_keys = pl.ds(spot * step, step)
-                kvs = [
-                    kv_ref[at_keys, m * per + j].reshape(step * in_place * block, 2 * HD)
-                    for j in heads
-                ]
-                boths = [dot(pairs[j][0], kvs[j], ROWS) for j in heads]
-                weights = []
-                for j in heads:
-                    lse = lse_ref[at_place, j, m, at_row]
-                    probs = jnp.exp(boths[j][:block] - wide(lse, boths[j].shape[1]))
-                    d_scores = probs * (boths[j][block:] - pairs[j][1])
-                    weights.append(
-                        jnp.concatenate(
-                            [d_scores.astype(jnp.bfloat16), probs.astype(jnp.bfloat16)], axis=0
-                        )
-                    )
-                for j in heads:
-                    total_ref[at_keys, m * per + j] += dot(weights[j], pairs[j][0], COLS).reshape(
-                        step, in_place, block, 2 * HD
-                    )
-                return tuple(d_qs[j] + dot(weights[j][:block], kvs[j]) for j in heads)
-
-            d_qs = lax.fori_loop(
-                0,
-                kv_ref.shape[0] // step,
-                some_keys,
-                tuple(jnp.zeros((block, 2 * HD), jnp.float32) for _ in heads),
+    def everything():
+        def clear(i, carry):
+            total_ref[i] = jnp.zeros(total_ref.shape[1:], jnp.float32)
+            return carry
+
+        lax.fori_loop(0, devices, clear, 0)
+        lax.fori_loop(0, blocks // GROUP, query_blocks, 0)
+        chosen = [table_ref[blocks * RAND + g] for g in range(GLOB)]
+        found = [pair_of(row // 2, row % 2, None) for row in chosen]
+        both_rows = GLOB * BLOCK
+        pairs = jnp.concatenate([f[0] for f in found] + [f[1] for f in found], axis=0)
+        delta = jnp.concatenate([f[2] for f in found], axis=0)
+        lse = jnp.concatenate([lse_ref[row] for row in chosen], axis=0)
+
+        def some_keys(spot, d_q):
+            kv = key_rows(land_ref, spot * STEP, STEP)
+            both = dot(pairs, kv, ROWS)
+            probs = jnp.exp(both[:both_rows] - wide(lse, both.shape[1]))
+            d_scores = probs * (both[both_rows:] - delta)
+            weight = jnp.concatenate(
+                [d_scores.astype(jnp.bfloat16), probs.astype(jnp.bfloat16)], axis=0
             )
-            for j in heads:
-                old = dq_ref[at_place, j, at_row]
-                dq_ref[at_place, j, at_row] = jnp.where(
-                    lanes_of(old.shape, m == 0), (d_qs[j] * HD ** (-0.5)).astype(jnp.bfloat16), old
-                )
-
-        return carry
-
-    lax.fori_loop(0, 2 * GLOB, global_rows, 0)
-
-    def give(i, carry):
-        kv_ref[i] = total_ref[i].astype(jnp.bfloat16)
-        return carry
-
-    gives = []
-    for at, s in enumerate(range(0, total_ref.shape[0], step)):
-        lax.fori_loop(s, s + step, give, 0)
-        gives.append(
-            pltpu.make_async_copy(
-                kv_ref.at[pl.ds(s, step)], dkv_out.at[pl.ds(s, step)], out_sem.at[at]
+            total_ref[pl.ds(spot * STEP, STEP)] += dot(weight, pairs, COLS).reshape(
+                STEP, 2, BLOCK, 2 * HD
             )
+            return d_q + dot(weight[:both_rows], kv)
+
+        d_q = lax.fori_loop(
+            0, devices // STEP, some_keys, jnp.zeros((both_rows, 2 * HD), jnp.float32)
         )
-        gives[-1].start()
-    for copy in gives:
-        copy.wait()
-
-
-def attend_back_call(table, q, kv, d, out, lse):
+        d_q = d_q * HD ** (-0.5)
+        for g, row in enumerate(chosen):
+            part = d_q[g * BLOCK : (g + 1) * BLOCK]
+            new = jnp.where(row % 2 == 0, part, turned(part)).astype(jnp.bfloat16)
+            old = parts_ref[row // 2, 2]
+            parts_ref[row // 2, 2] = jnp.where(lanes_of(old.shape, row % 2 == 0), new, old)
+
+        def give(i, carry):
+            parts_ref[i, :2] = total_ref[i].astype(jnp.bfloat16)
+            return carry
+
+        lax.fori_loop(0, devices, give, 0)
+
+    pl.when(table_ref[blocks * RAND + GLOB] == 1)(everything)
+
+
+def attend_back_call(table, land, d, out, lse):
     spec = pl.BlockSpec(memory_space=pltpu.VMEM)
-    far = pl.BlockSpec(memory_space=pl.ANY)
+    devices, _, block, lanes = land.shape
     return pl.pallas_call(
         attend_back_kernel,
-        out_shape=(
-            jax.ShapeDtypeStruct(q.shape, jnp.bfloat16),
-            jax.ShapeDtypeStruct(kv.shape, jnp.bfloat16),
-        ),
-        in_specs=[pl.BlockSpec(memory_space=pltpu.SMEM), spec, far, spec, spec, spec],
-        out_specs=(spec, far),
-        scratch_shapes=[
-            pltpu.VMEM(kv.shape, jnp.float32),
-            pltpu.VMEM(kv.shape, jnp.bfloat16),
-            pltpu.SemaphoreType.DMA,
-            pltpu.SemaphoreType.DMA((kv.shape[0] // 8,)),
-        ],
+        out_shape=jax.ShapeDtypeStruct(land.shape, jnp.bfloat16),
+        in_specs=[pl.BlockSpec(memory_space=pltpu.SMEM)] + [spec] * 4,
+        out_specs=spec,
+        scratch_shapes=[pltpu.VMEM((devices, 2, block, lanes), jnp.float32)],
         compiler_params=pltpu.CompilerParams(vmem_limit_bytes=60 * 2**20),
         name="attend_back",
-    )(table, q, kv, d, out, lse)
+    )(table, land, d, out, lse)
 
 
 def centre(values):
@@ -1074,31 +1085,37 @@
     return jnp.sum(values, axis=0, keepdims=True)
 
 
+WEIGHT_CHUNK = 1024
+
+
 def dense_kernel(
     c_ref, x_ref, cot_ref, wo_in, up_in, down_in, vec_ref, up_bias_ref,
     out_ref, d_mix_ref, d_c_ref, g_out_ref, g_up_out, g_down_out, g_vec_ref, g_up_bias_ref,
     ctx, first, hat, low, low_t, act, slope, ffn, wo_ref, up_ref, down_ref, g_up_ref, g_down_ref, in_sem, out_sem,
 ):
-    groups, per, rows, _ = c_ref.shape
+    rows = x_ref.shape[1]
     width = x_ref.shape[2]
     ff = up_ref.shape[1]
-    chunk = 384
+    chunk = WEIGHT_CHUNK
     fetches = [
         pltpu.make_async_copy(wo_in.at[:, pl.ds(3 * width, width)], wo_ref, in_sem.at[0]),
-        pltpu.make_async_copy(up_in, up_ref, in_sem.at[1]),
-        pltpu.make_async_copy(down_in, down_ref, in_sem.at[2]),
     ]
+    for i in range(ff // chunk):
+        at = pl.ds(i * chunk, chunk)
+        fetches.append(pltpu.make_async_copy(up_in.at[:, at], up_ref.at[:, at], in_sem.at[2 * i + 1]))
+        fetches.append(pltpu.make_async_copy(down_in.at[at], down_ref.at[at], in_sem.at[2 * i + 2]))
     for copy in fetches:
         copy.start()
     out_bias, attn_gain, attn_shift, down_bias, ffn_gain, ffn_shift = (
         vec_ref[k : k + 1, :] for k in range(2, 8)
     )
     for p in range(HEADS // 2):
-        one = c_ref[(2 * p) // per, (2 * p) % per]
-        two = c_ref[(2 * p + 1) // per, (2 * p + 1) % per]
         at = pl.ds(p * 2 * HD, 2 * HD)
-        ctx[:rows, at] = jnp.concatenate([one[:, HD:], two[:, HD:]], axis=1)
-        ctx[rows:, at] = jnp.concatenate([one[:, :HD], two[:, :HD]], axis=1)
+        for m in range(2):
+            one, two = c_ref[4 * p + m], c_ref[4 * p + 2 + m]
+            top, mid = m * rows, m * rows + rows // 2
+            ctx[top:mid, at] = jnp.concatenate([one[:, :HD], two[:, :HD]], axis=1)
+            ctx[mid : top + rows, at] = jnp.concatenate([one[:, HD:], two[:, HD:]], axis=1)
     tokens = x_ref[...].reshape(2 * rows, width).astype(jnp.float32)
     fetches[0].wait()
     hat_first, inverse_first = centre(tokens + dot(ctx[...], wo_ref[...]) + out_bias)
@@ -1107,11 +1124,11 @@
     low[...] = first[...].astype(jnp.bfloat16)
     low_t[...] = first[...].T.astype(jnp.bfloat16)
     ffn[...] = first[...] + down_bias
-    fetches[1].wait()
-    fetches[2].wait()
-
-    def forward(i, carry):
-        at = pl.ds(pl.multiple_of(i * chunk, chunk), chunk)
+
+    def forward(i):
+        at = pl.ds(i * chunk, chunk)
+        fetches[2 * i + 1].wait()
+        fetches[2 * i + 2].wait()
         hidden = dot(low[...], up_ref[:, at]) + up_bias_ref[:, at]
         share = 0.5 * (1.0 + lax.erf(hidden * 0.7071067811865476))
         bell = jnp.exp(-0.5 * hidden * hidden) * 0.3989422804014327
@@ -1119,9 +1136,9 @@
         act_low = (hidden * share).astype(jnp.bfloat16)
         act[:, at] = act_low
         ffn[...] += dot(act_low, down_ref[at, :])
-        return carry
-
-    lax.fori_loop(0, ff // chunk, forward, 0)
+
+    for i in range(ff // chunk):
+        forward(i)
     hat_second, inverse_second = centre(ffn[...])
     out_ref[...] = (
         (hat_second * ffn_gain + ffn_shift).astype(jnp.bfloat16).reshape(2, rows, width)
@@ -1164,9 +1181,11 @@
     g_vec_ref[6:8, :] = jnp.zeros((2, width), jnp.float32)
     g_out_ref[...] = dot(ctx[...], d_branch, COLS).astype(jnp.bfloat16)
     d_ctx = dot(d_branch, wo_ref[...], ROWS).astype(jnp.bfloat16)
-    for head in range(HEADS):
-        d_c_ref[head // per, head % per] = jnp.concatenate(
-            [halves(d_ctx[rows:], head * HD), halves(d_ctx[:rows], head * HD)], axis=1
+    for pair in range(d_c_ref.shape[0]):
+        col, top = pair // 2 * HD, pair % 2 * rows
+        mid = top + rows // 2
+        d_c_ref[pair] = jnp.concatenate(
+            [halves(d_ctx[top:mid], col), halves(d_ctx[mid : top + rows], col)], axis=1
         )
     for i in range(ff // chunk):
         for copy in leave(i):
@@ -1221,8 +1240,8 @@
             pltpu.VMEM((ff, width), bf16),
             pltpu.VMEM((width, ff), bf16),
             pltpu.VMEM((ff, width), bf16),
-            pltpu.SemaphoreType.DMA((3,)),
-            pltpu.SemaphoreType.DMA((2, ff // 384)),
+            pltpu.SemaphoreType.DMA((1 + 2 * (ff // WEIGHT_CHUNK),)),
+            pltpu.SemaphoreType.DMA((2, ff // WEIGHT_CHUNK)),
         ],
         compiler_params=pltpu.CompilerParams(vmem_limit_bytes=60 * 2**20),
         name="dense",
@@ -1234,18 +1253,11 @@
         query_weight, query_bias, key_weight, value_weight, value_bias, out_weight, out_bias, attn_gain,
         attn_shift, up_weight, up_bias, down_weight, down_bias, ffn_gain, ffn_shift,
     ) = shards
-    groups = lax.axis_size("head")
-    shard_count = lax.axis_size("blk")
-    devices = groups * shard_count
-    shard = lax.axis_index("blk")
-    group = lax.axis_index("head")
+    devices = lax.axis_size("head") * lax.axis_size("blk")
     micro, rows, width = inputs.shape
     depth = query_weight.shape[0]
     ff = up_weight.shape[1]
-    per = HEADS // groups
-    in_place = rows // BLOCK
-    blocks = groups * in_place
-    q, kv, up, down, mixed, vec, up_bias_row = front_call(
+    land, up, down, mixed, vec, up_bias_row = front_call(
         inputs,
         (query_weight, key_weight, value_weight, out_weight),
         up_weight,
@@ -1257,32 +1269,27 @@
     )
     up = up.reshape(width, ff)
     down = down.reshape(ff, width)
-    mine = lax.dynamic_slice(
-        random_blocks,
-        (0, shard * blocks, group * per, 0),
-        (micro, blocks, per, RAND),
-    )
+    busy, pair = place_pair(lax.axis_index("blk"), lax.axis_index("head"))
+    head, at = pair // micro, pair % micro
     table = jnp.concatenate(
         [
-            mine.reshape(-1),
-            global_blocks.reshape(-1),
-            jnp.stack([shard, shard_count * blocks]).astype(jnp.int32),
+            lax.dynamic_slice(
+                random_blocks, (at, 0, head, 0), (1, random_blocks.shape[1], 1, RAND)
+            ).reshape(-1),
+            lax.dynamic_slice(global_blocks, (at, 0), (1, GLOB)).reshape(-1),
+            busy.astype(jnp.int32)[None],
         ]
     )
-    split = (in_place, BLOCK, 2 * HD)
-    q = q.reshape((groups, per) + split)
-    kv = kv.reshape((devices, 2 * per) + split)
-    packed = (groups, per, rows, 2 * HD)
-    attended, lse = attend_call(table, q, kv)
-    context = swap_call(attended.reshape(packed), 3)
+    land = land.reshape(devices, 3, rows // 2, 2 * HD)
+    attended, lse = attend_call(table, land)
+    context = exchange_call(False, attended, 3)
     layer_out, d_mix, d_context, g_out, g_up, g_down, g_vec, g_up_bias = dense_call(
         context, inputs, cotangent, mixed, up, down, vec, up_bias_row
     )
-    d_context = swap_call(d_context, 4)
-    d_q, d_kv = attend_back_call(table, q, kv, d_context.reshape(q.shape), attended, lse)
+    d_context = exchange_call(True, d_context, 4)
+    parts = attend_back_call(table, land, d_context, attended, lse)
     results = back_call(
-        d_q.reshape(packed),
-        d_kv.reshape(devices, 2 * per, rows, 2 * HD),
+        parts.reshape(devices, 3 * rows // 2, 2 * HD),
         g_up.reshape(devices, depth, ff),
         g_down.reshape(devices, -1, width),
         inputs,
@@ -1294,7 +1301,7 @@
         5,
     )
     (
-        input_grad, grad_query, grad_key, grad_value, grad_out, grad_up, grad_down, *vector, grad_up_bias,
+        input_grad, grad_out, grad_query, grad_key, grad_value, grad_up, grad_down, *vector, grad_up_bias,
     ) = leave_call(*results)
     return (
         layer_out, input_grad, grad_query, vector[0], grad_key, grad_value, vector[1], grad_out,

time: 297 us -> 278 us (0.936)
  Pallas kernels: 294 us -> 275 us
    pallas_call x1, Pallas kernels: 107 us -> 96.9 us  [front_call(): pl.pallas_call(partial(front_kernel, kinds), out_shape=(jax.ShapeDtypeStr...]
    pallas_call x1, Pallas kernels: 22.7 us -> 16.5 us  [dense_call(): pl.pallas_call(dense_kernel, out_shape=outs, in_specs=[full(c.shape), ful...]
where the time goes in v2:
time: 278 us
  Pallas kernels  275 us (99%)
    pallas_call x1, Pallas kernels, back_call(): pl.pallas_call(partial(back_kernel, cuts), out_shape=tuple(outs), in_spec...  98.6 us
    pallas_call x1, Pallas kernels, front_call(): pl.pallas_call(partial(front_kernel, kinds), out_shape=(jax.ShapeDtypeStr...  96.9 us
    pallas_call x2, Pallas kernels, exchange_call(): pl.pallas_call(partial(exchange_kernel, to_pairs), out_shape=jax.ShapeDty...  32.5 us
    pallas_call x1, Pallas kernels, attend_back_call(): pl.pallas_call(attend_back_kernel, out_shape=jax.ShapeDtypeStruct(land.sh...  16.8 us
    pallas_call x1, Pallas kernels, dense_call(): pl.pallas_call(dense_kernel, out_shape=outs, in_specs=[full(c.shape), ful...  16.5 us
    pallas_call x1, Pallas kernels, attend_call(): pl.pallas_call(attend_kernel, out_shape=(jax.ShapeDtypeStruct((devices, b...  11.8 us

profile of v2, /device:TPU:0, one launch (start us, length us, event | category | flops | bytes accessed | tf_op | source)
XLA Modules:
  0.0 277.9 jit_solution(5381175166099829658)
XLA Ops:
  0.7 0.0 copy-start
  0.8 0.7 dynamic-slice_bitcast_fusion
  1.5 0.0 copy-done
  1.5 0.1 copy.36
  1.6 0.1 reshape.58
  1.7 0.6 pad_add_fusion.table_ref
  2.3 96.9 %front.1 = (bf16[32,192,128]{2,1,0:T(8,128)(2,1)}, bf16[32,24,3072]{2,1,0:T(8,128)(2,1)}, bf16[32,96,768]{2,1,0:T(8,128)(2,1)}, bf16[768,3072]{1,0:T(8,128)(2,1)}, f32[8,768]{1,0:T(8,128)}, /*index=5*/f32[1,3072]{1,0:T(1,128)}) custom-call(bf16[2,128,768]{2,1,0:T(8,128)(2,1)} %refs_3_.3, bf16[24,768]{1,0:T(8,128)(2,1)} %refs_1_.1, bf16[24,768]{1,0:T(8,128)(2,1)} %refs_2_.1, ...), custom_call_target="tpu_custom_call" | custom-call | tf_op jit(solution)/shard_map/front/pallas_call | solution.py:462
  99.3 11.8 %attend.1 = (bf16[32,64,128]{2,1,0:T(8,128)(2,1)}, f32[64,64,128]{2,1,0:T(8,128)}) custom-call(s32[195]{0:T(256)} %pad_add_fusion.table_ref, bf16[32,3,64,128]{3,2,1,0:T(8,128)(2,1)} %bitcast.14), custom_call_target="tpu_custom_call" | custom-call | tf_op jit(solution)/shard_map/attend/pallas_call | solution.py:940
  111.0 15.6 %exchange3.1.c_ref = bf16[24,64,128]{2,1,0:T(8,128)(2,1)} custom-call(bf16[32,64,128]{2,1,0:T(8,128)(2,1)} %get-tuple-element.58.in_ref.out_ref), custom_call_target="tpu_custom_call" | custom-call | tf_op jit(solution)/shard_map/exchange3/pallas_call | solution.py:324
  126.6 16.5 %dense.1 = (bf16[2,128,768]{2,1,0:T(8,128)(2,1)}, f32[256,768]{1,0:T(8,128)}, bf16[24,64,128]{2,1,0:T(8,128)(2,1)}, bf16[768,768]{1,0:T(8,128)(2,1)}, bf16[768,3...) custom-call(bf16[24,64,128]{2,1,0:T(8,128)(2,1)} %exchange3.1.c_ref, ...), custom_call_target="tpu_custom_call" | custom-call | tf_op jit(solution)/shard_map/dense/pallas_call | solution.py:1215
  143.1 16.9 %exchange4.1.d_ref = bf16[32,64,128]{2,1,0:T(8,128)(2,1)} custom-call(bf16[24,64,128]{2,1,0:T(8,128)(2,1)} %get-tuple-element.65.in_ref), custom_call_target="tpu_custom_call" | custom-call | tf_op jit(solution)/shard_map/exchange4/pallas_call | solution.py:324
  160.0 16.8 %attend_back.1 = bf16[32,3,64,128]{3,2,1,0:T(8,128)(2,1)} custom-call(s32[195]{0:T(256)} %pad_add_fusion.table_ref, bf16[32,3,64,128]{3,2,1,0:T(8,128)(2,1)} %bitcast.15, bf16[32,64,128]{2,1,0:T(8,128)(2,1)} %exchange4.1.d_ref, bf16[32,64,128]{2,1,0:T(8,128)(2,1)} %get-tuple-element.58.in_ref.out_ref, f32[64,64,128]{2,1,0:T(8,128)} %get-tuple-element.66.lse_ref), custom_call_target="tpu_custom_call" | custom-call | tf_op jit(solution)/shard_map/attend_back/pallas_call | solution.py:1057
  176.8 98.6 %back.1 = (bf16[2,128,768]{2,1,0:T(8,128)(2,1)}, f32[24,768]{1,0:T(8,128)}, f32[24,768]{1,0:T(8,128)}, f32[24,768]{1,0:T(8,128)}, f32[24,768]{1,0:T(8,128)}, /*i...) custom-call(bf16[32,192,128]{2,1,0:T(8,128)(2,1)} %bitcast.13, bf16[32,24,3072]{2,1,0:T(8,128)(2,1)} %bitcast.16, ...), custom_call_target="tpu_custom_call" | custom-call | tf_op jit(solution)/shard_map/back/pallas_call | solution.py:768
  275.4 2.4 leave.1
  (1 shorter events, 0.0 us)
Async XLA Ops:
  0.7 0.8 copy-start

commit v3 on v2

--- a/solution.py
+++ b/solution.py
@@ -309,27 +309,6 @@
 def gather_semaphores(n):
     dma = pltpu.SemaphoreType.DMA
     return [dma((n,)), dma((n, 6)), dma((n, 4)), dma((n, 4, 8)), dma((n, 4, 8))]
-
-
-def exchange_kernel(to_pairs, in_ref, out_ref, *sems):
-    begin, arrive, sent = exchange(to_pairs, in_ref, out_ref, sems)
-    meet(lax.axis_index("blk"), lax.axis_index("head"))
-    begin()
-    arrive()
-    sent()
-
-
-def exchange_call(to_pairs, array, collective):
-    far = pl.BlockSpec(memory_space=pl.ANY)
-    return pl.pallas_call(
-        partial(exchange_kernel, to_pairs),
-        out_shape=jax.ShapeDtypeStruct((32 if to_pairs else 24,) + array.shape[1:], array.dtype),
-        in_specs=[far],
-        out_specs=far,
-        scratch_shapes=exchange_semaphores(),
-        compiler_params=pltpu.CompilerParams(collective_id=collective, has_side_effects=True),
-        name=f"exchange{collective}",
-    )(array)
 
 
 def spread_of(rows, width):
@@ -1089,9 +1068,10 @@
 
 
 def dense_kernel(
-    c_ref, x_ref, cot_ref, wo_in, up_in, down_in, vec_ref, up_bias_ref,
-    out_ref, d_mix_ref, d_c_ref, g_out_ref, g_up_out, g_down_out, g_vec_ref, g_up_bias_ref,
+    c_in, x_ref, cot_ref, wo_in, up_in, down_in, vec_ref, up_bias_ref,
+    out_ref, d_mix_ref, d_land, g_out_ref, g_up_out, g_down_out, g_vec_ref, g_up_bias_ref,
     ctx, first, hat, low, low_t, act, slope, ffn, wo_ref, up_ref, down_ref, g_up_ref, g_down_ref, in_sem, out_sem,
+    c_ref, d_c_ref, *pair_sems,
 ):
     rows = x_ref.shape[1]
     width = x_ref.shape[2]
@@ -1106,6 +1086,11 @@
         fetches.append(pltpu.make_async_copy(down_in.at[at], down_ref.at[at], in_sem.at[2 * i + 2]))
     for copy in fetches:
         copy.start()
+    begin_c, arrive_c, sent_c = exchange(False, c_in, c_ref, pair_sems[:3])
+    begin_d, arrive_d, sent_d = exchange(True, d_c_ref, d_land, pair_sems[3:])
+    meet(lax.axis_index("blk"), lax.axis_index("head"))
+    begin_c()
+    arrive_c()
     out_bias, attn_gain, attn_shift, down_bias, ffn_gain, ffn_shift = (
         vec_ref[k : k + 1, :] for k in range(2, 8)
     )
@@ -1187,12 +1172,16 @@
         d_c_ref[pair] = jnp.concatenate(
             [halves(d_ctx[top:mid], col), halves(d_ctx[mid : top + rows], col)], axis=1
         )
+    begin_d()
     for i in range(ff // chunk):
         for copy in leave(i):
             copy.wait()
-
-
-def dense_call(c, tokens, cot, mixed, up, down, vec, up_bias):
+    arrive_d()
+    sent_c()
+    sent_d()
+
+
+def dense_call(c, tokens, cot, mixed, up, down, vec, up_bias, collective):
     micro, rows, width = tokens.shape
     ff = up.shape[1]
     both = micro * rows
@@ -1216,7 +1205,7 @@
         dense_kernel,
         out_shape=outs,
         in_specs=[
-            full(c.shape),
+            far,
             full(tokens.shape),
             full(cot.shape),
             far,
@@ -1225,7 +1214,7 @@
             full(vec.shape),
             full(up_bias.shape),
         ],
-        out_specs=tuple(far if k in (4, 5) else full(o.shape) for k, o in enumerate(outs)),
+        out_specs=tuple(far if k in (2, 4, 5) else full(o.shape) for k, o in enumerate(outs)),
         scratch_shapes=[
             pltpu.VMEM((both, width), bf16),
             pltpu.VMEM((both, width), f32),
@@ -1242,8 +1231,13 @@
             pltpu.VMEM((ff, width), bf16),
             pltpu.SemaphoreType.DMA((1 + 2 * (ff // WEIGHT_CHUNK),)),
             pltpu.SemaphoreType.DMA((2, ff // WEIGHT_CHUNK)),
-        ],
-        compiler_params=pltpu.CompilerParams(vmem_limit_bytes=60 * 2**20),
+            pltpu.VMEM((HEADS * micro,) + c.shape[1:], bf16),
+            pltpu.VMEM((HEADS * micro,) + c.shape[1:], bf16),
+        ]
+        + exchange_semaphores() * 2,
+        compiler_params=pltpu.CompilerParams(
+            collective_id=collective, has_side_effects=True, vmem_limit_bytes=60 * 2**20
+        ),
         name="dense",
     )(c, tokens, cot, mixed, up, down, vec, up_bias)
 
@@ -1282,11 +1276,9 @@
     )
     land = land.reshape(devices, 3, rows // 2, 2 * HD)
     attended, lse = attend_call(table, land)
-    context = exchange_call(False, attended, 3)
     layer_out, d_mix, d_context, g_out, g_up, g_down, g_vec, g_up_bias = dense_call(
-        context, inputs, cotangent, mixed, up, down, vec, up_bias_row
-    )
-    d_context = exchange_call(True, d_context, 4)
+        attended, inputs, cotangent, mixed, up, down, vec, up_bias_row, 3
+    )
     parts = attend_back_call(table, land, d_context, attended, lse)
     results = back_call(
         parts.reshape(devices, 3 * rows // 2, 2 * HD),

time: 278 us -> 273 us (0.982)
  Pallas kernels: 275 us -> 269 us
    pallas_call x3 -> x1, Pallas kernels: 48.9 us -> 42.6 us  [dense_call(): pl.pallas_call(dense_kernel, out_shape=outs, in_specs=[far, full(tokens.s...]
where the time goes in v3:
time: 273 us; the launch traced here: 272 us
  Pallas kernels  269 us (99%)
    pallas_call x1, Pallas kernels, back_call(): pl.pallas_call(partial(back_kernel, cuts), out_shape=tuple(outs), in_spec...  98.5 us
    pallas_call x1, Pallas kernels, front_call(): pl.pallas_call(partial(front_kernel, kinds), out_shape=(jax.ShapeDtypeStr...  96.9 us
    pallas_call x1, Pallas kernels, dense_call(): pl.pallas_call(dense_kernel, out_shape=outs, in_specs=[far, full(tokens.s...  42.6 us
    pallas_call x1, Pallas kernels, attend_back_call(): pl.pallas_call(attend_back_kernel, out_shape=jax.ShapeDtypeStruct(land.sh...  16.9 us
    pallas_call x1, Pallas kernels, attend_call(): pl.pallas_call(attend_kernel, out_shape=(jax.ShapeDtypeStruct((devices, b...  11.8 us

profile of v3, /device:TPU:0, one launch (start us, length us, event | category | flops | bytes accessed | tf_op | source)
XLA Modules:
  0.0 272.1 jit_solution(9622273697883928597)
XLA Ops:
  0.7 0.0 copy-start
  0.8 0.7 dynamic-slice_bitcast_fusion
  1.5 0.0 copy-done
  1.5 0.1 copy.36
  1.6 0.1 reshape.58
  1.7 0.6 pad_add_fusion.table_ref
  2.3 96.9 %front.1 = (bf16[32,192,128]{2,1,0:T(8,128)(2,1)}, bf16[32,24,3072]{2,1,0:T(8,128)(2,1)}, bf16[32,96,768]{2,1,0:T(8,128)(2,1)}, bf16[768,3072]{1,0:T(8,128)(2,1)}, f32[8,768]{1,0:T(8,128)}, /*index=5*/f32[1,3072]{1,0:T(1,128)}) custom-call(bf16[2,128,768]{2,1,0:T(8,128)(2,1)} %refs_3_.3, bf16[24,768]{1,0:T(8,128)(2,1)} %refs_1_.1, bf16[24,768]{1,0:T(8,128)(2,1)} %refs_2_.1, ...), custom_call_target="tpu_custom_call" | custom-call | tf_op jit(solution)/shard_map/front/pallas_call | solution.py:441
  99.3 11.8 %attend.1 = (bf16[32,64,128]{2,1,0:T(8,128)(2,1)}, f32[64,64,128]{2,1,0:T(8,128)}) custom-call(s32[195]{0:T(256)} %pad_add_fusion.table_ref, bf16[32,3,64,128]{3,2,1,0:T(8,128)(2,1)} %bitcast.14), custom_call_target="tpu_custom_call" | custom-call | tf_op jit(solution)/shard_map/attend/pallas_call | solution.py:919
  111.0 42.6 %dense.1 = (bf16[2,128,768]{2,1,0:T(8,128)(2,1)}, f32[256,768]{1,0:T(8,128)}, bf16[32,64,128]{2,1,0:T(8,128)(2,1)}, bf16[768,768]{1,0:T(8,128)(2,1)}, bf16[768,3...) custom-call(bf16[32,64,128]{2,1,0:T(8,128)(2,1)} %get-tuple-element.58.c_in.out_ref, ...), custom_call_target="tpu_custom_call" | custom-call | tf_op jit(solution)/shard_map/dense/pallas_call | solution.py:1204
  153.7 16.9 %attend_back.1 = bf16[32,3,64,128]{3,2,1,0:T(8,128)(2,1)} custom-call(s32[195]{0:T(256)} %pad_add_fusion.table_ref, bf16[32,3,64,128]{3,2,1,0:T(8,128)(2,1)} %bitcast.15, bf16[32,64,128]{2,1,0:T(8,128)(2,1)} %get-tuple-element.65.d_ref, bf16[32,64,128]{2,1,0:T(8,128)(2,1)} %get-tuple-element.58.c_in.out_ref, f32[64,64,128]{2,1,0:T(8,128)} %get-tuple-element.66.lse_ref), custom_call_target="tpu_custom_call" | custom-call | tf_op jit(solution)/shard_map/attend_back/pallas_call | solution.py:1036
  170.5 0.0 copy-start.1
  170.5 98.5 %back.1 = (bf16[2,128,768]{2,1,0:T(8,128)(2,1)}, f32[24,768]{1,0:T(8,128)}, f32[24,768]{1,0:T(8,128)}, f32[24,768]{1,0:T(8,128)}, f32[24,768]{1,0:T(8,128)}, /*i...) custom-call(bf16[32,192,128]{2,1,0:T(8,128)(2,1)} %bitcast.13, bf16[32,24,3072]{2,1,0:T(8,128)(2,1)} %bitcast.16, ...), custom_call_target="tpu_custom_call" | custom-call | tf_op jit(solution)/shard_map/back/pallas_call | solution.py:747
  269.0 2.4 leave.1
  271.4 0.0 copy-done.1
  271.4 0.7 copy.38
  (1 shorter events, 0.0 us)
Async XLA Ops:
  0.7 0.8 copy-start
  170.5 100.8 %copy-start.1 = (bf16[2,128,768]{2,1,0:T(8,128)(2,1)S(1)}, bf16[2,128,768]{2,1,0:T(8,128)(2,1)}, u32[]{:S(2)}) copy-start(bf16[2,128,768]{2,1,0:T(8,128)(2,1)} %get-tuple-element.114) | copy-start | bytes 1179652

commit v4 on v3

--- a/solution.py
+++ b/solution.py
@@ -469,7 +469,7 @@
     )(tokens, *matrices, up, down, *vectors)
 
 
-def scatter_steps(cuts, ins, bufs, sems):
+def scatter_steps(cuts, ins, bufs, sems, made=()):
     local_sem, line_send, line_recv, core_send, core_recv, send, recv = sems
     b, h, core, x, y, across_x, across_y, partner, line = places()
     seen = jnp.where(jnp.logical_or(h == 1, h == 2), 2, 3)
@@ -494,7 +494,16 @@
             )
         )
 
+    def fetch(i, at, src, dst):
+        loads[i, at] = pltpu.make_async_copy(src, dst, local_sem.at[i, at])
+        loads[i, at].start()
+
     def begin(i, some=(0, 1, 2, 3)):
+        if i in made:
+            fetch(i, 0, ins[i][0], bufs[i][1].at[pl.ds(1, 3)])
+            fetch(i, 1, ins[i][1], bufs[i][2])
+            fetch(i, 2, ins[i][2], bufs[i][3])
+            return
         from_partner, total = bufs[i][0], bufs[i][1]
         for t in some:
             go(
@@ -506,11 +515,7 @@
                     (partner, h),
                 )
             )
-            load = pltpu.make_async_copy(
-                ins[i].at[pl.ds((targets[t] * 2 + core) * 4, 4)], total.at[t], local_sem.at[i, t]
-            )
-            load.start()
-            loads[i, t] = load
+            fetch(i, t, ins[i].at[pl.ds((targets[t] * 2 + core) * 4, 4)], total.at[t])
 
     def wait_for(ref, i, d, k):
         remote(ref, ref, send.at[i, d, k], recv.at[i, d, k], (partner, h)).wait_recv()
@@ -523,7 +528,11 @@
     def both_cores(i, t, d, extra=()):
         from_partner, total = bufs[i][0], bufs[i][1]
         place = line[d]
-        value = total[t, place].astype(jnp.float32) + from_partner[t, place].astype(jnp.float32)
+        value = total[t, place].astype(jnp.float32)
+        if i not in made:
+            value = value + from_partner[t, place].astype(jnp.float32)
+        elif not extra:
+            return
         for ref in extra:
             value = value + ref[d].astype(jnp.float32)
         total[t, place] = value.astype(total.dtype)
@@ -547,26 +556,48 @@
             if second is not None:
                 go(remote(part(mine, second), bufs[i][3].at[d], send.at[i, d, 1], recv.at[i, d, 1], (across_y, h)))
 
+    def corner_arrived(i, d, at):
+        if cuts[i][at] is not None and i not in made:
+            wait_for(bufs[i][2 + at].at[d], i, d, at)
+
+    def leave(i, left, sems_):
+        copies = []
+        for t in (1, 2, 3):
+            ready(i, t)
+            for d in order:
+                both_cores(i, t, d)
+            copies.append(pltpu.make_async_copy(bufs[i][1].at[t], left.at[t - 1], sems_.at[i, t]))
+            copies[-1].start()
+        for d in order:
+            for at in range(2):
+                corner_arrived(i, d, at)
+        return copies
+
     def sides(i):
         total = bufs[i][1]
         first, second = cuts[i]
-        ready(i, 1)
-        ready(i, 2)
+        if i in made:
+            for at in range(3):
+                loads[i, at].wait()
+        else:
+            ready(i, 1)
+            ready(i, 2)
         for d in order:
             both_cores(i, 1, d)
             if second is not None:
-                wait_for(bufs[i][3].at[d], i, d, 1)
+                corner_arrived(i, d, 1)
                 add_corner(i, 1, d, bufs[i][3], second)
             go(remote(total.at[1, line[d]], bufs[i][4].at[d], send.at[i, d, 2], recv.at[i, d, 2], (across_x, h)))
             both_cores(i, 2, d)
             if first is not None:
-                wait_for(bufs[i][2].at[d], i, d, 0)
+                corner_arrived(i, d, 0)
                 add_corner(i, 2, d, bufs[i][2], first)
             go(remote(total.at[2, line[d]], bufs[i][5].at[d], send.at[i, d, 3], recv.at[i, d, 3], (across_y, h)))
 
     def own(i):
         total = bufs[i][1]
-        ready(i, 3)
+        if i not in made:
+            ready(i, 3)
         for d in order:
             wait_for(bufs[i][4].at[d], i, d, 2)
             wait_for(bufs[i][5].at[d], i, d, 3)
@@ -591,11 +622,15 @@
     def enter():
         meet(b, h)
 
-    return enter, begin, corner, sides, own, finish, sent
-
-
-def scatter_scratch(chunk, dtype, cuts):
-    shapes = [(4, 4) + chunk, (4, 4) + chunk]
+    return enter, begin, corner, leave, sides, own, finish, sent
+
+
+def weight_cuts(ff, width):
+    return tuple((cut(1, 0, n // 2), cut(1, n // 2, n // 2)) for n in (ff, width))
+
+
+def scatter_scratch(chunk, dtype, cuts, made=False):
+    shapes = [(16, 128) if made else (4, 4) + chunk, (4, 4) + chunk]
     for cut_ in cuts:
         size = [16, 128]
         if cut_ is not None:
@@ -616,18 +651,18 @@
 
 def back_kernel(cuts, *refs):
     (
-        parts_in, up_in, down_in, x_ref, mixed_in, d_mix_ref, g_out_ref, g_vec_ref, g_up_bias_ref,
+        parts_in, up_left, up_first, up_second, down_left, down_first, down_second, x_ref, mixed_in, d_mix_ref, g_out_ref, g_vec_ref, g_up_bias_ref,
         d_x_ref, g_outw_ref, g_query_ref, g_key_ref, g_value_ref, g_up_ref, g_down_ref, g_small_ref,
         land, terms, small, w_ref, d_q, d_k, d_v, w_sem,
-    ), rest = refs[:25], list(refs[25:])
+    ), rest = refs[:29], list(refs[29:])
     q_sems, kv_sems, rest = rest[:3], rest[3:6], rest[6:]
     bufs = [rest[7 * i : 7 * i + 7] for i in range(len(cuts))]
     rows = x_ref.shape[1]
     width = x_ref.shape[2]
     _, shards, depth, _ = terms.shape
-    ins = (up_in, down_in, terms.at[0], terms.at[1], terms.at[2], terms.at[3], small)
-    enter, begin, corner, sides, own, finish, sent = scatter_steps(
-        cuts, ins, bufs, rest[7 * len(cuts) :]
+    ins = ((up_left, up_first, up_second), (down_left, down_first, down_second), terms.at[0], terms.at[1], terms.at[2], terms.at[3], small)
+    enter, begin, corner, _, sides, own, finish, sent = scatter_steps(
+        cuts, ins, bufs, rest[7 * len(cuts) :], (UP, DOWN)
     )
     begin_q, arrive_q, sent_q = exchange(False, parts_in, land, q_sems, pl.ds(rows, rows // 2))
     begin_kv, arrive_kv, sent_kv = exchange(False, parts_in, land, kv_sems, pl.ds(0, rows))
@@ -636,18 +671,22 @@
     def keep_term(at, value):
         terms[at] = value.reshape(shards, depth, width).astype(jnp.bfloat16)
 
+    def keep_term(at, value):
+        terms[at] = value.reshape(shards, depth, width).astype(jnp.bfloat16)
+
+    begin(UP)
+    begin(DOWN)
     enter()
     begin_q()
     begin_kv()
     keep_term(0, g_out_ref[...].astype(jnp.float32))
     small[...] = jnp.zeros(small.shape, jnp.float32)
+    begin(OUT)
+    sides(UP)
+    sides(DOWN)
+    corner(OUT)
+    own(UP)
     arrive_q()
-    begin(UP, (0,))
-    begin(DOWN, (0,))
-    corner(UP)
-    corner(DOWN)
-    begin(UP, (1, 2, 3,))
-    begin(DOWN, (1, 2, 3,))
     arrive_kv()
     spans = []
     for m in range(2):
@@ -682,37 +721,32 @@
     for s in range(shards):
         small[s, :8, :depth] = vectors[:, s * depth : (s + 1) * depth]
         small[s, 8:9, :up_depth] = up_bias[:, s * up_depth : (s + 1) * up_depth]
-    begin(OUT)
     begin(QUERY)
     begin(KEY)
     begin(VALUE)
     begin(SMALL)
-    corner(OUT)
     corner(QUERY)
     corner(KEY)
     corner(VALUE)
     corner(SMALL)
-    sides(UP)
-    sides(DOWN)
+    own(DOWN)
     sides(OUT)
     sides(QUERY)
     sides(KEY)
     sides(VALUE)
     sides(SMALL)
-    own(UP)
     load.wait()
     d_x = d_mix_ref[...]
     for k, half_ref in enumerate((d_q, d_k, d_v)):
         d_x = d_x + dot(half_ref[...], w_ref[:, k * width : (k + 1) * width], ROWS)
     d_x_ref[...] = d_x.astype(jnp.bfloat16).reshape(2, rows, width)
-    own(DOWN)
     g_up_ref[...] = finish(UP)
+    g_down_ref[...] = finish(DOWN)
     own(OUT)
     own(QUERY)
     own(KEY)
     own(VALUE)
     own(SMALL)
-    g_down_ref[...] = finish(DOWN)
     g_outw_ref[...] = finish(OUT)
     g_query_ref[...] = finish(QUERY)
     g_key_ref[...] = finish(KEY)
@@ -723,17 +757,20 @@
     sent_kv()
 
 
-def back_call(parts, g_up, g_down, tokens, mixed, d_mix, g_out, g_vec, g_up_bias, collective):
+def back_call(parts, lefts, tokens, mixed, d_mix, g_out, g_vec, g_up_bias, collective):
     micro, rows, width = tokens.shape
-    devices, depth, ff = g_up.shape
+    devices = parts.shape[0]
+    depth, ff = lefts[0].shape[2:]
     f32, bf16 = jnp.float32, jnp.bfloat16
     one_way, other_way = (cut(1, 0, width), None), (None, cut(1, 0, width))
-    cuts = [(cut(1, 0, ff), None), other_way, one_way, other_way, one_way, other_way, (cut(1, 0, 128), None)]
+    cuts = [*weight_cuts(ff, width), one_way, other_way, one_way, other_way, (cut(1, 0, 128), None)]
     square = (depth, width)
-    chunks = [(g_up.shape[1:], bf16), (g_down.shape[1:], bf16)] + [(square, bf16)] * 4
+    chunks = [(lefts[0].shape[2:], bf16), (lefts[3].shape[2:], bf16)] + [(square, bf16)] * 4
     chunks += [((16, 128), f32)]
     scratch = [
-        one for (chunk, dtype), c in zip(chunks, cuts) for one in scatter_scratch(chunk, dtype, c)
+        one
+        for i, ((chunk, dtype), c) in enumerate(zip(chunks, cuts))
+        for one in scatter_scratch(chunk, dtype, c, i < 2)
     ]
     near = pl.BlockSpec(memory_space=pltpu.VMEM)
     far = pl.BlockSpec(memory_space=pl.ANY)
@@ -741,13 +778,13 @@
     outs += [jax.ShapeDtypeStruct(square, f32)] * 4
     outs += [
         jax.ShapeDtypeStruct((depth, ff), f32),
-        jax.ShapeDtypeStruct(g_down.shape[1:], f32),
+        jax.ShapeDtypeStruct(lefts[3].shape[2:], f32),
         jax.ShapeDtypeStruct((16, 128), f32),
     ]
     return pl.pallas_call(
         partial(back_kernel, cuts),
         out_shape=tuple(outs),
-        in_specs=[far] * 3 + [near, far] + [near] * 4,
+        in_specs=[far] * 7 + [near, far] + [near] * 4,
         out_specs=(near,) * len(outs),
         scratch_shapes=[
             pltpu.VMEM((HEADS * micro,) + parts.shape[1:], bf16),
@@ -764,7 +801,7 @@
             collective_id=collective, has_side_effects=True, vmem_limit_bytes=61 * 2**20
         ),
         name="back",
-    )(parts, g_up, g_down, tokens, mixed, d_mix, g_out, g_vec, g_up_bias)
+    )(parts, *lefts, tokens, mixed, d_mix, g_out, g_vec, g_up_bias)
 
 
 def leave_kernel(*refs):
@@ -851,7 +888,7 @@
     return ref[pl.ds(spot, step), :2].reshape(step * 2 * BLOCK, 2 * HD)
 
 
-GROUP = 8
+GROUP = 16
 STEP = 8
 
 
@@ -1069,9 +1106,9 @@
 
 def dense_kernel(
     c_in, x_ref, cot_ref, wo_in, up_in, down_in, vec_ref, up_bias_ref,
-    out_ref, d_mix_ref, d_land, g_out_ref, g_up_out, g_down_out, g_vec_ref, g_up_bias_ref,
+    out_ref, d_mix_ref, d_land, g_out_ref, up_left, up_first, up_second, down_left, down_first, down_second, g_vec_ref, g_up_bias_ref,
     ctx, first, hat, low, low_t, act, slope, ffn, wo_ref, up_ref, down_ref, g_up_ref, g_down_ref, in_sem, out_sem,
-    c_ref, d_c_ref, *pair_sems,
+    c_ref, d_c_ref, up_other, up_total, down_other, down_total, *sems,
 ):
     rows = x_ref.shape[1]
     width = x_ref.shape[2]
@@ -1086,9 +1123,15 @@
         fetches.append(pltpu.make_async_copy(down_in.at[at], down_ref.at[at], in_sem.at[2 * i + 2]))
     for copy in fetches:
         copy.start()
-    begin_c, arrive_c, sent_c = exchange(False, c_in, c_ref, pair_sems[:3])
-    begin_d, arrive_d, sent_d = exchange(True, d_c_ref, d_land, pair_sems[3:])
-    meet(lax.axis_index("blk"), lax.axis_index("head"))
+    begin_c, arrive_c, sent_c = exchange(False, c_in, c_ref, sems[:3])
+    begin_d, arrive_d, sent_d = exchange(True, d_c_ref, d_land, sems[3:6])
+    enter, begin, corner, leave, _, _, _, sent = scatter_steps(
+        weight_cuts(ff, width),
+        (g_up_ref, g_down_ref),
+        ((up_other, up_total, up_first, up_second), (down_other, down_total, down_first, down_second)),
+        sems[6:],
+    )
+    enter()
     begin_c()
     arrive_c()
     out_bias, attn_gain, attn_shift, down_bias, ffn_gain, ffn_shift = (
@@ -1136,26 +1179,30 @@
     g_vec_ref[3:4, :] = rows_sum(d_ffn.astype(jnp.float32))
     ffn[...] = d_second
 
-    def leave(i):
-        at = pl.ds(pl.multiple_of(i * chunk, chunk), chunk)
-        return (
-            pltpu.make_async_copy(g_up_ref.at[:, at], g_up_out.at[:, at], out_sem.at[0, i]),
-            pltpu.make_async_copy(g_down_ref.at[at, :], g_down_out.at[at, :], out_sem.at[1, i]),
+    shards, depth, _ = g_up_ref.shape
+    down_depth = g_down_ref.shape[1]
+    half = ff // 2
+    for i in range(2):
+        at = pl.ds(i * half, half)
+        g_down_ref[pl.ds(i * (shards // 2), shards // 2)] = (
+            dot(act[:, at], d_ffn, COLS)
+            .reshape(shards // 2, down_depth, width)
+            .astype(jnp.bfloat16)
         )
-
-    def backward(i, carry):
-        at = pl.ds(pl.multiple_of(i * chunk, chunk), chunk)
+    begin(1, (0,))
+    for i in range(2):
+        at = pl.ds(i * half, half)
         d_act = dot(d_ffn, down_ref[at, :], ROWS)
         d_hidden = (d_act * slope[:, at]).astype(jnp.bfloat16)
         g_up_bias_ref[:, at] = rows_sum(d_hidden.astype(jnp.float32))
-        g_down_ref[at, :] = dot(act[:, at], d_ffn, COLS).astype(jnp.bfloat16)
-        g_up_ref[:, at] = dot(low_t[...], d_hidden).astype(jnp.bfloat16)
-        for copy in leave(i):
-            copy.start()
+        g_up_ref[:, :, at] = (
+            dot(low_t[...], d_hidden).reshape(shards, depth, half).astype(jnp.bfloat16)
+        )
         ffn[...] += dot(d_hidden, up_ref[:, at], ROWS)
-        return carry
-
-    lax.fori_loop(0, ff // chunk, backward, 0)
+        if i == 0:
+            corner(1)
+            begin(1, (1, 2, 3))
+    begin(0, (0,))
     d_first = ffn[...]
     g_vec_ref[1:2, :] = rows_sum(d_first * hat[...])
     g_vec_ref[2:3, :] = rows_sum(d_first)
@@ -1164,7 +1211,6 @@
     d_branch = d_mix.astype(jnp.bfloat16)
     g_vec_ref[0:1, :] = rows_sum(d_branch.astype(jnp.float32))
     g_vec_ref[6:8, :] = jnp.zeros((2, width), jnp.float32)
-    g_out_ref[...] = dot(ctx[...], d_branch, COLS).astype(jnp.bfloat16)
     d_ctx = dot(d_branch, wo_ref[...], ROWS).astype(jnp.bfloat16)
     for pair in range(d_c_ref.shape[0]):
         col, top = pair // 2 * HD, pair % 2 * rows
@@ -1173,9 +1219,12 @@
             [halves(d_ctx[top:mid], col), halves(d_ctx[mid : top + rows], col)], axis=1
         )
     begin_d()
-    for i in range(ff // chunk):
-        for copy in leave(i):
-            copy.wait()
+    corner(0)
+    begin(0, (1, 2, 3))
+    g_out_ref[...] = dot(ctx[...], d_branch, COLS).astype(jnp.bfloat16)
+    for copy in leave(1, down_left, out_sem) + leave(0, up_left, out_sem):
+        copy.wait()
+    sent()
     arrive_d()
     sent_c()
     sent_d()
@@ -1185,6 +1234,8 @@
     micro, rows, width = tokens.shape
     ff = up.shape[1]
     both = micro * rows
+    devices = c.shape[0]
+    up_chunk, down_chunk = (width // devices, ff), (ff // devices, width)
     far = pl.BlockSpec(memory_space=pl.ANY)
     f32, bf16 = jnp.float32, jnp.bfloat16
 
@@ -1196,8 +1247,12 @@
         jax.ShapeDtypeStruct((both, width), f32),
         jax.ShapeDtypeStruct(c.shape, bf16),
         jax.ShapeDtypeStruct((width, width), bf16),
-        jax.ShapeDtypeStruct((width, ff), bf16),
-        jax.ShapeDtypeStruct((ff, width), bf16),
+        jax.ShapeDtypeStruct((3, 4) + up_chunk, bf16),
+        jax.ShapeDtypeStruct((4, width // devices, ff // 2), bf16),
+        jax.ShapeDtypeStruct((4, width // devices, ff // 2), bf16),
+        jax.ShapeDtypeStruct((3, 4) + down_chunk, bf16),
+        jax.ShapeDtypeStruct((4, ff // devices, width // 2), bf16),
+        jax.ShapeDtypeStruct((4, ff // devices, width // 2), bf16),
         jax.ShapeDtypeStruct((8, width), f32),
         jax.ShapeDtypeStruct((1, ff), f32),
     )
@@ -1214,7 +1269,7 @@
             full(vec.shape),
             full(up_bias.shape),
         ],
-        out_specs=tuple(far if k in (2, 4, 5) else full(o.shape) for k, o in enumerate(outs)),
+        out_specs=tuple(far if k == 2 or 4 <= k < 10 else full(o.shape) for k, o in enumerate(outs)),
         scratch_shapes=[
             pltpu.VMEM((both, width), bf16),
             pltpu.VMEM((both, width), f32),
@@ -1227,14 +1282,19 @@
             pltpu.VMEM((width, width), bf16),
             pltpu.VMEM((width, ff), bf16),
             pltpu.VMEM((ff, width), bf16),
-            pltpu.VMEM((width, ff), bf16),
-            pltpu.VMEM((ff, width), bf16),
+            pltpu.VMEM((devices,) + up_chunk, bf16),
+            pltpu.VMEM((devices,) + down_chunk, bf16),
             pltpu.SemaphoreType.DMA((1 + 2 * (ff // WEIGHT_CHUNK),)),
-            pltpu.SemaphoreType.DMA((2, ff // WEIGHT_CHUNK)),
+            pltpu.SemaphoreType.DMA((2, 4)),
             pltpu.VMEM((HEADS * micro,) + c.shape[1:], bf16),
             pltpu.VMEM((HEADS * micro,) + c.shape[1:], bf16),
+            pltpu.VMEM((4, 4) + up_chunk, bf16),
+            pltpu.VMEM((4, 4) + up_chunk, bf16),
+            pltpu.VMEM((4, 4) + down_chunk, bf16),
+            pltpu.VMEM((4, 4) + down_chunk, bf16),
         ]
-        + exchange_semaphores() * 2,
+        + exchange_semaphores() * 2
+        + scatter_semaphores(2),
         compiler_params=pltpu.CompilerParams(
             collective_id=collective, has_side_effects=True, vmem_limit_bytes=60 * 2**20
         ),
@@ -1276,14 +1336,13 @@
     )
     land = land.reshape(devices, 3, rows // 2, 2 * HD)
     attended, lse = attend_call(table, land)
-    layer_out, d_mix, d_context, g_out, g_up, g_down, g_vec, g_up_bias = dense_call(
+    layer_out, d_mix, d_context, g_out, *lefts, g_vec, g_up_bias = dense_call(
         attended, inputs, cotangent, mixed, up, down, vec, up_bias_row, 3
     )
     parts = attend_back_call(table, land, d_context, attended, lse)
     results = back_call(
         parts.reshape(devices, 3 * rows // 2, 2 * HD),
-        g_up.reshape(devices, depth, ff),
-        g_down.reshape(devices, -1, width),
+        lefts,
         inputs,
         mixed,
         d_mix,

time: 273 us -> 263 us (0.963)
  Pallas kernels: 269 us -> 259 us
    pallas_call x1, Pallas kernels: 98.5 us -> 82.7 us  [back_call(): pl.pallas_call(partial(back_kernel, cuts), out_shape=tuple(outs), in_spec...]
    pallas_call x1, Pallas kernels: 42.6 us -> 50.5 us  [dense_call(): pl.pallas_call(dense_kernel, out_shape=outs, in_specs=[far, full(tokens.s...]
where the time goes in v4:
time: 263 us; the launch traced here: 262 us
  Pallas kernels  259 us (98%)
    pallas_call x1, Pallas kernels, front_call(): pl.pallas_call(partial(front_kernel, kinds), out_shape=(jax.ShapeDtypeStr...  96.9 us
    pallas_call x1, Pallas kernels, back_call(): pl.pallas_call(partial(back_kernel, cuts), out_shape=tuple(outs), in_spec...  82.7 us
    pallas_call x1, Pallas kernels, dense_call(): pl.pallas_call(dense_kernel, out_shape=outs, in_specs=[far, full(tokens.s...  50.5 us
    pallas_call x1, Pallas kernels, attend_back_call(): pl.pallas_call(attend_back_kernel, out_shape=jax.ShapeDtypeStruct(land.sh...  16.8 us
    pallas_call x1, Pallas kernels, attend_call(): pl.pallas_call(attend_kernel, out_shape=(jax.ShapeDtypeStruct((devices, b...  10.1 us

profile of v4, /device:TPU:0, one launch (start us, length us, event | category | flops | bytes accessed | tf_op | source)
XLA Modules:
  0.0 262.5 jit_solution(6796649461899435235)
XLA Ops:
  0.7 0.0 copy-start
  0.8 0.7 dynamic-slice_bitcast_fusion
  1.5 0.0 copy-done
  1.5 0.1 copy.36
  1.6 0.1 reshape.52
  1.7 0.6 pad_add_fusion.table_ref
  2.3 96.9 %front.1 = (bf16[32,192,128]{2,1,0:T(8,128)(2,1)}, bf16[32,24,3072]{2,1,0:T(8,128)(2,1)}, bf16[32,96,768]{2,1,0:T(8,128)(2,1)}, bf16[768,3072]{1,0:T(8,128)(2,1)}, f32[8,768]{1,0:T(8,128)}, /*index=5*/f32[1,3072]{1,0:T(1,128)}) custom-call(bf16[2,128,768]{2,1,0:T(8,128)(2,1)} %refs_7_.3, bf16[24,768]{1,0:T(8,128)(2,1)} %refs_1_.1, bf16[24,768]{1,0:T(8,128)(2,1)} %refs_2_.1, ...), custom_call_target="tpu_custom_call" | custom-call | tf_op jit(solution)/shard_map/front/pallas_call | solution.py:441
  99.3 10.1 %attend.1 = (bf16[32,64,128]{2,1,0:T(8,128)(2,1)}, f32[64,64,128]{2,1,0:T(8,128)}) custom-call(s32[195]{0:T(256)} %pad_add_fusion.table_ref, bf16[32,3,64,128]{3,2,1,0:T(8,128)(2,1)} %bitcast.12), custom_call_target="tpu_custom_call" | custom-call | tf_op jit(solution)/shard_map/attend/pallas_call | solution.py:956
  109.3 50.5 %dense.1 = (bf16[2,128,768]{2,1,0:T(8,128)(2,1)}, f32[256,768]{1,0:T(8,128)}, bf16[32,64,128]{2,1,0:T(8,128)(2,1)}, bf16[768,768]{1,0:T(8,128)(2,1)}, bf16[3,4,2...) custom-call(bf16[32,64,128]{2,1,0:T(8,128)(2,1)} %get-tuple-element., ...), custom_call_target="tpu_custom_call" | custom-call | tf_op jit(solution)/shard_map/dense/pallas_call | solution.py:1259
  159.8 16.8 %attend_back.1 = bf16[32,3,64,128]{3,2,1,0:T(8,128)(2,1)} custom-call(s32[195]{0:T(256)} %pad_add_fusion.table_ref, bf16[32,3,64,128]{3,2,1,0:T(8,128)(2,1)} %bitcast.13, bf16[32,64,128]{2,1,0:T(8,128)(2,1)} %get-tuple-element.69.d_ref, bf16[32,64,128]{2,1,0:T(8,128)(2,1)} %get-tuple-element.62.c_in.out_ref, f32[64,64,128]{2,1,0:T(8,128)} %get-tuple-element.70.lse_ref), custom_call_target="tpu_custom_call" | custom-call | tf_op jit(solution)/shard_map/attend_back/pallas_call | solution.py:1073
  176.6 0.0 copy-start.1
  176.6 82.7 %back.1 = (bf16[2,128,768]{2,1,0:T(8,128)(2,1)}, f32[24,768]{1,0:T(8,128)}, f32[24,768]{1,0:T(8,128)}, f32[24,768]{1,0:T(8,128)}, f32[24,768]{1,0:T(8,128)}, /*i...) custom-call(bf16[32,192,128]{2,1,0:T(8,128)(2,1)} %bitcast.11, ...), custom_call_target="tpu_custom_call" | custom-call | tf_op jit(solution)/shard_map/back/pallas_call | solution.py:784
  259.3 2.4 leave.1
  261.7 0.0 copy-done.1
  261.7 0.7 copy.38
  (1 shorter events, 0.0 us)
Async XLA Ops:
  0.7 0.8 copy-start
  176.6 85.1 %copy-start.1 = (bf16[2,128,768]{2,1,0:T(8,128)(2,1)S(1)}, bf16[2,128,768]{2,1,0:T(8,128)(2,1)}, u32[]{:S(2)}) copy-start(bf16[2,128,768]{2,1,0:T(8,128)(2,1)} %get-tuple-element.122) | copy-start | bytes 1179652

commit v5 on v4

--- a/solution.py
+++ b/solution.py
@@ -433,8 +433,8 @@
     half = 2 * width
     kinds = [
         (False, True, (cut(1, 0, half), cut(1, half, half + 128))),
-        (False, True, (cut(1, 0, ff), None)),
-        (False, True, (None, cut(1, 0, width))),
+        (False, True, weight_cuts(ff, width)[0]),
+        (False, True, weight_cuts(ff, width)[1]),
     ]
     near = pl.BlockSpec(memory_space=pltpu.VMEM)
     far = pl.BlockSpec(memory_space=pl.ANY)

time: 263 us -> 261 us (level)
  no operation moved by 1% of the time
where the time goes in v5:
time: 261 us
  Pallas kernels  257 us (98%)
    pallas_call x1, Pallas kernels, front_call(): pl.pallas_call(partial(front_kernel, kinds), out_shape=(jax.ShapeDtypeStr...  95.7 us
    pallas_call x1, Pallas kernels, back_call(): pl.pallas_call(partial(back_kernel, cuts), out_shape=tuple(outs), in_spec...  82.7 us
    pallas_call x1, Pallas kernels, dense_call(): pl.pallas_call(dense_kernel, out_shape=outs, in_specs=[far, full(tokens.s...  49.9 us
    pallas_call x1, Pallas kernels, attend_back_call(): pl.pallas_call(attend_back_kernel, out_shape=jax.ShapeDtypeStruct(land.sh...  16.8 us
    pallas_call x1, Pallas kernels, attend_call(): pl.pallas_call(attend_kernel, out_shape=(jax.ShapeDtypeStruct((devices, b...  10 us

profile of v5, /device:TPU:0, one launch (start us, length us, event | category | flops | bytes accessed | tf_op | source)
XLA Modules:
  0.0 260.5 jit_solution(13921425424348841612)
XLA Ops:
  0.7 0.0 copy-start
  0.8 0.7 dynamic-slice_bitcast_fusion
  1.5 0.0 copy-done
  1.5 0.1 copy.36
  1.6 0.1 reshape.52
  1.7 0.6 pad_add_fusion.table_ref
  2.3 95.7 %front.1 = (bf16[32,192,128]{2,1,0:T(8,128)(2,1)}, bf16[32,24,3072]{2,1,0:T(8,128)(2,1)}, bf16[32,96,768]{2,1,0:T(8,128)(2,1)}, bf16[768,3072]{1,0:T(8,128)(2,1)}, f32[8,768]{1,0:T(8,128)}, /*index=5*/f32[1,3072]{1,0:T(1,128)}) custom-call(bf16[2,128,768]{2,1,0:T(8,128)(2,1)} %refs_7_.3, bf16[24,768]{1,0:T(8,128)(2,1)} %refs_1_.1, bf16[24,768]{1,0:T(8,128)(2,1)} %refs_2_.1, ...), custom_call_target="tpu_custom_call" | custom-call | tf_op jit(solution)/shard_map/front/pallas_call | solution.py:441
  98.0 10.0 %attend.1 = (bf16[32,64,128]{2,1,0:T(8,128)(2,1)}, f32[64,64,128]{2,1,0:T(8,128)}) custom-call(s32[195]{0:T(256)} %pad_add_fusion.table_ref, bf16[32,3,64,128]{3,2,1,0:T(8,128)(2,1)} %bitcast.12), custom_call_target="tpu_custom_call" | custom-call | tf_op jit(solution)/shard_map/attend/pallas_call | solution.py:956
  108.1 49.9 %dense.1 = (bf16[2,128,768]{2,1,0:T(8,128)(2,1)}, f32[256,768]{1,0:T(8,128)}, bf16[32,64,128]{2,1,0:T(8,128)(2,1)}, bf16[768,768]{1,0:T(8,128)(2,1)}, bf16[3,4,2...) custom-call(bf16[32,64,128]{2,1,0:T(8,128)(2,1)} %get-tuple-element., ...), custom_call_target="tpu_custom_call" | custom-call | tf_op jit(solution)/shard_map/dense/pallas_call | solution.py:1259
  158.0 16.8 %attend_back.1 = bf16[32,3,64,128]{3,2,1,0:T(8,128)(2,1)} custom-call(s32[195]{0:T(256)} %pad_add_fusion.table_ref, bf16[32,3,64,128]{3,2,1,0:T(8,128)(2,1)} %bitcast.13, bf16[32,64,128]{2,1,0:T(8,128)(2,1)} %get-tuple-element.69.d_ref, bf16[32,64,128]{2,1,0:T(8,128)(2,1)} %get-tuple-element.62.c_in.out_ref, f32[64,64,128]{2,1,0:T(8,128)} %get-tuple-element.70.lse_ref), custom_call_target="tpu_custom_call" | custom-call | tf_op jit(solution)/shard_map/attend_back/pallas_call | solution.py:1073
  174.7 0.0 copy-start.1
  174.7 82.7 %back.1 = (bf16[2,128,768]{2,1,0:T(8,128)(2,1)}, f32[24,768]{1,0:T(8,128)}, f32[24,768]{1,0:T(8,128)}, f32[24,768]{1,0:T(8,128)}, f32[24,768]{1,0:T(8,128)}, /*i...) custom-call(bf16[32,192,128]{2,1,0:T(8,128)(2,1)} %bitcast.11, ...), custom_call_target="tpu_custom_call" | custom-call | tf_op jit(solution)/shard_map/back/pallas_call | solution.py:784
  257.4 2.4 leave.1
  259.8 0.0 copy-done.1
  259.8 0.7 copy.38
  (1 shorter events, 0.0 us)
Async XLA Ops:
  0.7 0.8 copy-start
  174.7 85.1 %copy-start.1 = (bf16[2,128,768]{2,1,0:T(8,128)(2,1)S(1)}, bf16[2,128,768]{2,1,0:T(8,128)(2,1)}, u32[]{:S(2)}) copy-start(bf16[2,128,768]{2,1,0:T(8,128)(2,1)} %get-tuple-element.122) | copy-start | bytes 1179652
